TPU v7x, 32 devices: a whole 2x2x4 slice. The times are simulated.
32 devices in a mesh: tm: 2 (over core), cell: 16 (over z, y, x).
Axes of the slice: x: 2, y: 2, z: 4, core: 2. Of those that a mesh axis runs over, the one named last changes fastest.
Arguments:
- block_rows: int32 [2, 1024], P('tm', 'cell'), may hold values from 0 to 63, as said below
- block_cols: int32 [2, 1024], P('tm', 'cell'), may hold values from 0 to 63, as said below
- block_values: bfloat16 [2, 1024, 128, 128], P('tm', 'cell'), as said below
- growth: float32 [2, 8192], P('tm', 'cell'), may hold values from 0.5 to 4
- first_labels: int32 [8, 8192], P(None, 'cell'), may hold values from 0 to 15, as said below
- last_labels: int32 [8, 8192], P(None, 'cell'), may hold values from 0 to 15
Outputs:
- forward_mass: bfloat16 [2, 128, 8192], P('tm', None, 'cell')
- fate: bfloat16 [2, 128, 8192], P('tm', None, 'cell')
Inputs may be any that keep to these rules, and one draw needn't show every extreme that they name: `block_rows`: the slots n of a coupling with n // 64 = c name row blocks c * 4 to (c + 1) * 4 - 1 only, and each row block is named by exactly 16 slots of each coupling. `block_cols`: A slot's column block differs from its row block by at most 4; a pair of row and column block may stand in several slots, whose blocks then add. `block_values`: every entry is positive. `first_labels`: in every panel each of the 16 types labels exactly 512 cells.
All inputs are finite; a program needn't handle non-finite values.
Results may differ from a plain program's by a relative error of at most 0.006.
Values may be sent and summed in bfloat16 or wider, within the bound.
No kernel may reach another device: no remote copies, remote signals or barrier semaphores. Data moves between devices by JAX's collectives and lax.ppermute only.
A program may use at most 64 MiB of HBM per device.

v0:
```python
import jax
import jax.numpy as jnp
from jax import lax
from jax.sharding import PartitionSpec as P

CELL_TYPES = 16
BAND_REACH = 4


def extended(array, sides, width):
    for axis, dim in sides:
        devices, length = (lax.axis_size(axis), array.shape[dim])
        up = [(i, (i + 1) % devices) for i in range(devices - 1)]
        down = [(j, i) for i, j in up]
        last = lax.slice_in_dim(array, length - width, length, axis=dim)
        initial = lax.slice_in_dim(array, 0, width, axis=dim)
        before = lax.ppermute(last, axis, up)
        after = lax.ppermute(initial, axis, down)
        array = jnp.concatenate([before, array, after], axis=dim)
    return array


def shifted(block, axis, distance):
    devices = range(lax.axis_size(axis))
    route = [(i - distance, i) for i in devices if i - distance in devices]
    return lax.ppermute(block, axis, route)


def seed_stack(labels, width):
    marks = labels[:, None, :] == jnp.arange(CELL_TYPES, dtype=jnp.int32)[None, :, None]
    return marks.astype(jnp.bfloat16).reshape(width * CELL_TYPES, labels.shape[1])


def on_device(block_rows, block_cols, block_values, growth, first_labels, last_labels):
    chain_len = lax.axis_size("tm")
    tm_index = lax.axis_index("tm")
    cell_index = lax.axis_index("cell")
    cell_count = lax.axis_size("cell")
    growth_row = growth[0]
    block_side = block_values.shape[2]
    dev_cells = growth_row.shape[0]
    dev_blocks = dev_cells // block_side
    slot_count = block_rows.shape[1]
    per_row = slot_count // dev_blocks
    window = dev_blocks + 2 * BAND_REACH
    all_cells = dev_cells * cell_count
    panels = first_labels.shape[0]
    local_rows = block_rows[0] - cell_index * dev_blocks
    order = jnp.argsort(local_rows, stable=True)
    blocks = jnp.take(block_values[0], order, axis=0)
    offsets = jnp.take(block_cols[0] - block_rows[0], order, axis=0).reshape(dev_blocks, per_row)

    def forward_step(stack_in):
        height = stack_in.shape[0]
        scaled = (stack_in.astype(jnp.float32) / growth_row[None, :]).astype(jnp.bfloat16)
        by_block = jnp.swapaxes(scaled.reshape(height, dev_blocks, block_side), 0, 1)
        picked = jnp.repeat(by_block, per_row, axis=0)
        carried = jnp.einsum("sqk,skl->sql", picked, blocks, preferred_element_type=jnp.float32)
        grouped = carried.reshape(dev_blocks, per_row, height, block_side)
        spread = jnp.zeros((window, height, block_side), jnp.float32)
        for shift_by in range(-BAND_REACH, BAND_REACH + 1):
            hit = (offsets == shift_by)[:, :, None, None]
            partial_sum = jnp.sum(jnp.where(hit, grouped, 0.0), axis=1)
            low = BAND_REACH + shift_by
            spread = spread + jnp.pad(
                partial_sum, ((low, window - dev_blocks - low), (0, 0), (0, 0))
            )
        spread = jnp.transpose(spread, (1, 0, 2))
        inside = spread[:, BAND_REACH : BAND_REACH + dev_blocks]
        outside = jnp.concatenate(
            [spread[:, :BAND_REACH], spread[:, BAND_REACH + dev_blocks :]], axis=1
        )
        margin = extended(outside.astype(jnp.bfloat16), (("cell", 1),), BAND_REACH).astype(
            outside.dtype
        )
        inside = inside.at[:, :BAND_REACH].add(margin[:, :BAND_REACH])
        inside = inside.at[:, dev_blocks - BAND_REACH :].add(margin[:, 3 * BAND_REACH :])
        totals = lax.psum(jnp.sum(inside, axis=(1, 2)), "cell")
        scaled_mass = inside * (all_cells / totals)[:, None, None]
        return scaled_mass.astype(jnp.bfloat16).reshape(height, dev_cells)

    def backward_step(stack_in):
        height = stack_in.shape[0]
        shaped = stack_in.reshape(height, dev_blocks, block_side)
        widened = extended(shaped, (("cell", 1),), BAND_REACH)
        widened = jnp.swapaxes(widened, 0, 1)
        picked = jnp.zeros((dev_blocks, per_row, height, block_side), jnp.bfloat16)
        for shift_by in range(-BAND_REACH, BAND_REACH + 1):
            low = BAND_REACH + shift_by
            candidate = widened[low : low + dev_blocks][:, None]
            hit = (offsets == shift_by)[:, :, None, None]
            picked = jnp.where(hit, candidate, picked)
        picked = picked.reshape(slot_count, height, block_side)
        pulled = jnp.einsum("skl,sql->sqk", blocks, picked, preferred_element_type=jnp.float32)
        summed = jnp.sum(pulled.reshape(dev_blocks, per_row, height, block_side), axis=1)
        summed = jnp.transpose(summed, (1, 0, 2))
        grouped = summed.reshape(height // CELL_TYPES, CELL_TYPES, dev_blocks, block_side)
        fates = grouped * (CELL_TYPES / jnp.sum(grouped, axis=1, keepdims=True))
        return fates.astype(jnp.bfloat16).reshape(height, dev_cells)

    def forward_section(step_index, received, stored, width):
        fronts = panels // width
        front_index = step_index - tm_index
        active = (front_index >= 0) & (front_index < fronts)
        seeded = seed_stack(first_labels, width)
        stack_in = jnp.where((tm_index == 0) | jnp.logical_not(active), seeded, received)
        computed = forward_step(stack_in)
        result = jnp.where(active, computed, jnp.zeros_like(computed))
        stored = jnp.where(active, result, stored)
        return (shifted(result, "tm", 1), stored)

    def backward_section(step_index, received, stored, width):
        fronts = panels // width
        front_index = step_index - (chain_len - 1 - tm_index)
        active = (front_index >= 0) & (front_index < fronts)
        seeded = seed_stack(last_labels, width)
        stack_in = jnp.where(
            (tm_index == chain_len - 1) | jnp.logical_not(active), seeded, received
        )
        computed = backward_step(stack_in)
        result = jnp.where(active, computed, jnp.zeros_like(computed))
        stored = jnp.where(active, result, stored)
        return (shifted(result, "tm", -1), stored)

    width = panels
    sections = chain_len + panels // width - 1
    empty_stack = jnp.zeros((width * CELL_TYPES, dev_cells), jnp.bfloat16)
    empty_store = jnp.zeros((panels * CELL_TYPES, dev_cells), jnp.bfloat16)

    def forward_turn(step_index, state_pair):
        return forward_section(step_index, state_pair[0], state_pair[1], width)

    def backward_turn(step_index, state_pair):
        return backward_section(step_index, state_pair[0], state_pair[1], width)

    forward_state = lax.fori_loop(0, sections, forward_turn, (empty_stack, empty_store))
    backward_state = lax.fori_loop(0, sections, backward_turn, (empty_stack, empty_store))
    forward_mass = forward_state[1]
    fate = backward_state[1]
    return (forward_mass[None], fate[None])


def solution(mesh):
    placed = (
        P("tm", "cell"),
        P("tm", "cell"),
        P("tm", "cell", None, None),
        P("tm", "cell"),
        P(None, "cell"),
        P(None, "cell"),
    )
    return jax.shard_map(
        on_device,
        mesh=mesh,
        in_specs=placed,
        out_specs=(P("tm", None, "cell"), P("tm", None, "cell")),
        check_vma=False,
    )
```

profile of v0, /device:TPU:0, one launch (start us, length us, event | category | flops | bytes accessed | tf_op | source)
XLA Modules:
  0.0 176.5 jit_solution(17590290924298233088)
XLA Ops:
  1.5 2.0 %sort.17 = (s32[64]{0:T(128)}, s32[64]{0:T(128)S(1)}) sort(s32[64]{0:T(128)S(1)} %get-tuple-element.609, s32[64]{0:T(128)S(1)} %iota.25), dimensions={0}, to_apply=%region_0.0 | sort | flops 384 | bytes 1024 | tf_op jit(solution)/shard_map/jit(argsort)/sort | solution.py:49
  5.0 2.2 %gather_fusion.1 = bf16[64,128,128]{2,1,0:T(8,128)(2,1)} fusion(bf16[64,128,128]{2,1,0:T(8,128)(2,1)S(1)} %bitcast.151, s32[1024]{0:T(1024)S(1)} %pad_clamp_fusion), kind=kCustom, calls=%fused_computation.1 | custom fusion | bytes 4194560 | tf_op jit(solution)/shard_map/jit(_take)/gather | solution.py:50
  7.2 3.2 %broadcast_select_fusion = bf16[64,128,128]{2,1,0:T(8,128)(2,1)} fusion(bf16[64,128,128]{2,1,0:T(8,128)(2,1)} %gather_fusion.1, pred[64]{0:T(512)(128)(4,1)S(1)} %get-tuple-element.579), kind=kLoop, calls=%fused_computation.64 | loop fusion | flops 1048576 | bytes 4194368 | tf_op jit(solution)/shard_map/jit(_take)/select_n | solution.py:50
  10.4 126.2 %while.54 = (s32[]{:T(128)}, bf16[128,512]{0,1:T(8,128)(2,1)S(1)}, bf16[128,512]{0,1:T(8,128)(2,1)S(1)}, s32[]{:T(128)}, s32[4,16]{1,0:T(4,128)}, /*index=5*/pre...) while((s32[]{:T(128)}, bf16[128,512]{0,1:T(8,128)(2,1)S(1)}, ...), condition=%wide.region_13.14_spmd.clone, body=%wide.region_1.13_spmd.clone.sunk | while | flops 289931968 | bytes 27026164 | solution.py:136
  13.8 4.0 %select_reduce_fusion.10 = (f32[4,128,128]{2,1,0:T(8,128)S(1)}, f32[4,128,128]{2,1,0:T(8,128)S(1)}, f32[4,128,128]{2,1,0:T(8,128)S(1)}, f32[4,128,128]{2,1,0:T(8...) fusion(pred[4,16]{1,0:T(4,128)(4,1)S(1)} %get-tuple-element.751, ...), kind=kOutput, calls=%fused_computation.10.clone.1 | convolution fusion | flops 286720000 | bytes 6554176 | tf_op jit(solution)/shard_map/while/body/eval_jaxpr/sqk,skl->sql/dot_general | solution.py:58
  19.3 5.5 %collective-permute-start.1 = (bf16[128,4,128]{2,0,1:T(8,128)(2,1)S(1)}, bf16[128,4,128]{2,0,1:T(8,128)(2,1)S(1)}, u32[]{:S(2)}, u32[]{:S(2)}) collective-permute-start(bf16[128,4,128]{2,0,1:T(8,128)(2,1)S(1)} %get-tuple-element.771), channel_id=1, source_target_pairs={{0,1},{1,2},{2,3},{3,4},{4,5},{5,6},{6,7},{7,8},{8,9},{9,10},{10,1... | collective-permute-start | bytes 393224 | tf_op jit(solution)/shard_map/while/body/eval_jaxpr/ppermute | solution.py:17
  24.7 1.6 collective-permute-done
  26.3 3.9 %collective-permute-done.1 = bf16[128,4,128]{2,0,1:T(8,128)(2,1)S(1)} collective-permute-done((bf16[128,4,128]{2,0,1:T(8,128)(2,1)S(1)}, bf16[128,4,128]{2,0,1:T(8,128)(2,1)S(1)}, u32[]{:S(2)}, u32[]{:S(2)}) %collective-permute-start.1) | collective-permute-done | bytes 131104 | tf_op jit(solution)/shard_map/while/body/eval_jaxpr/ppermute | solution.py:17
  30.9 1.7 fusion.41
  32.5 41.2 %psum.16 = f32[128]{0:T(128)S(1)} all-reduce(f32[128]{0:T(128)} %get-tuple-element.774), channel_id=1, replica_groups=mesh['tm'=2,'cell'=16] {'cell'}, use_global_device_ids=true, to_apply=%region_12.12 | all-reduce | flops 128 | bytes 1024 | tf_op jit(solution)/shard_map/while/body/eval_jaxpr/psum | solution.py:78
  79.6 4.0 %select_reduce_fusion.10 = (f32[4,128,128]{2,1,0:T(8,128)S(1)}, f32[4,128,128]{2,1,0:T(8,128)S(1)}, f32[4,128,128]{2,1,0:T(8,128)S(1)}, f32[4,128,128]{2,1,0:T(8...) fusion(pred[4,16]{1,0:T(4,128)(4,1)S(1)} %get-tuple-element.751, ...), kind=kOutput, calls=%fused_computation.10.clone.1 | convolution fusion | flops 286720000 | bytes 6554176 | tf_op jit(solution)/shard_map/while/body/eval_jaxpr/sqk,skl->sql/dot_general | solution.py:58
  85.1 4.6 %collective-permute-start.1 = (bf16[128,4,128]{2,0,1:T(8,128)(2,1)S(1)}, bf16[128,4,128]{2,0,1:T(8,128)(2,1)S(1)}, u32[]{:S(2)}, u32[]{:S(2)}) collective-permute-start(bf16[128,4,128]{2,0,1:T(8,128)(2,1)S(1)} %get-tuple-element.771), channel_id=1, source_target_pairs={{0,1},{1,2},{2,3},{3,4},{4,5},{5,6},{6,7},{7,8},{8,9},{9,10},{10,1... | collective-permute-start | bytes 393224 | tf_op jit(solution)/shard_map/while/body/eval_jaxpr/ppermute | solution.py:17
  89.6 2.3 %collective-permute-done = bf16[128,4,128]{2,0,1:T(8,128)(2,1)S(1)} collective-permute-done((bf16[128,4,128]{2,0,1:T(8,128)(2,1)S(1)}, bf16[128,4,128]{2,0,1:T(8,128)(2,1)S(1)}, u32[]{:S(2)}, u32[]{:S(2)}) %collective-permute-start) | collective-permute-done | bytes 131104 | tf_op jit(solution)/shard_map/while/body/eval_jaxpr/ppermute | solution.py:18
  93.3 1.7 fusion.41
  95.0 39.1 %psum.16 = f32[128]{0:T(128)S(1)} all-reduce(f32[128]{0:T(128)} %get-tuple-element.774), channel_id=1, replica_groups=mesh['tm'=2,'cell'=16] {'cell'}, use_global_device_ids=true, to_apply=%region_12.12 | all-reduce | flops 128 | bytes 1024 | tf_op jit(solution)/shard_map/while/body/eval_jaxpr/psum | solution.py:78
  137.4 38.3 %while.55 = (s32[]{:T(128)}, bf16[128,512]{0,1:T(8,128)(2,1)S(1)}, bf16[128,512]{0,1:T(8,128)(2,1)S(1)}, s32[]{:T(128)}, s32[4,16]{1,0:T(4,128)}, /*index=5*/pre...) while((s32[]{:T(128)}, bf16[128,512]{0,1:T(8,128)(2,1)S(1)}, ...), condition=%wide.region_17.18_spmd.clone, body=%wide.region_14.17_spmd.clone.sunk | while | flops 280625728 | bytes 27120428 | solution.py:137
  139.8 4.6 %collective-permute-start.4 = (bf16[128,4,128]{2,1,0:T(4,128)(2,1)S(1)}, bf16[128,4,128]{2,1,0:T(4,128)(2,1)S(1)}, u32[]{:S(2)}, u32[]{:S(2)}) collective-permute-start(bf16[128,4,128]{2,1,0:T(4,128)(2,1)S(1)} %reshape.489), channel_id=1, source_target_pairs={{0,1},{1,2},{2,3},{3,4},{4,5},{5,6},{6,7},{7,8},{8,9},{9,10},{10,1... | collective-permute-start | bytes 393224 | tf_op jit(solution)/shard_map/while/body/eval_jaxpr/ppermute | solution.py:17
  148.4 2.0 %fusion.47 = bf16[64,128,128]{2,1,0:T(8,128)(2,1)S(1)} fusion(pred[64]{0:T(512)(128)(4,1)S(1)} %eq.471, pred[64]{0:T(512)(128)(4,1)S(1)} %eq.472, pred[64]{0:T(512)(128)(4,1)S(1)} %eq.473, pred[64]{0:T(512)(128)(4,1)S(1)} %eq.474, pred[64]{0:T(512)(128)(4,1)S(1)} %eq.475, pred[64]{0:T(512)(128)(4,1)S(1)} %eq.476, pred[64]{0:T(512)(128)(4,1)S(1)} %eq.477, ...), kind=kLoop, calls=%fused_computation.43.clone.1 | loop fusion | flops 9437184 | bytes 3277376 | tf_op jit(solution)/shard_map/while/body/eval_jaxpr/jit(_where)/select_n | solution.py:92
  150.4 1.5 bitcast_reduce_fusion.4
  153.7 1.9 %collective-permute-done.5 = bf16[128,512]{0,1:T(8,128)(2,1)S(1)} collective-permute-done((bf16[128,512]{0,1:T(8,128)(2,1)S(1)}, bf16[128,512]{0,1:T(8,128)(2,1)S(1)}, u32[]{:S(2)}, u32[]{:S(2)}) %collective-permute-start.5) | collective-permute-done | bytes 131104 | tf_op jit(solution)/shard_map/while/body/eval_jaxpr/ppermute | solution.py:26
  158.0 5.0 %collective-permute-start.4 = (bf16[128,4,128]{2,1,0:T(4,128)(2,1)S(1)}, bf16[128,4,128]{2,1,0:T(4,128)(2,1)S(1)}, u32[]{:S(2)}, u32[]{:S(2)}) collective-permute-start(bf16[128,4,128]{2,1,0:T(4,128)(2,1)S(1)} %reshape.489), channel_id=1, source_target_pairs={{0,1},{1,2},{2,3},{3,4},{4,5},{5,6},{6,7},{7,8},{8,9},{9,10},{10,1... | collective-permute-start | bytes 393224 | tf_op jit(solution)/shard_map/while/body/eval_jaxpr/ppermute | solution.py:17
  164.9 2.6 %collective-permute-done.4 = bf16[128,4,128]{2,1,0:T(4,128)(2,1)S(1)} collective-permute-done((bf16[128,4,128]{2,1,0:T(4,128)(2,1)S(1)}, bf16[128,4,128]{2,1,0:T(4,128)(2,1)S(1)}, u32[]{:S(2)}, u32[]{:S(2)}) %collective-permute-start.4) | collective-permute-done | bytes 131104 | tf_op jit(solution)/shard_map/while/body/eval_jaxpr/ppermute | solution.py:17
  168.5 2.0 %fusion.47 = bf16[64,128,128]{2,1,0:T(8,128)(2,1)S(1)} fusion(pred[64]{0:T(512)(128)(4,1)S(1)} %eq.471, pred[64]{0:T(512)(128)(4,1)S(1)} %eq.472, pred[64]{0:T(512)(128)(4,1)S(1)} %eq.473, pred[64]{0:T(512)(128)(4,1)S(1)} %eq.474, pred[64]{0:T(512)(128)(4,1)S(1)} %eq.475, pred[64]{0:T(512)(128)(4,1)S(1)} %eq.476, pred[64]{0:T(512)(128)(4,1)S(1)} %eq.477, ...), kind=kLoop, calls=%fused_computation.43.clone.1 | loop fusion | flops 9437184 | bytes 3277376 | tf_op jit(solution)/shard_map/while/body/eval_jaxpr/jit(_where)/select_n | solution.py:92
  173.8 1.9 %collective-permute-done.5 = bf16[128,512]{0,1:T(8,128)(2,1)S(1)} collective-permute-done((bf16[128,512]{0,1:T(8,128)(2,1)S(1)}, bf16[128,512]{0,1:T(8,128)(2,1)S(1)}, u32[]{:S(2)}, u32[]{:S(2)}) %collective-permute-start.5) | collective-permute-done | bytes 131104 | tf_op jit(solution)/shard_map/while/body/eval_jaxpr/ppermute | solution.py:26
  (144 shorter events, 36.7 us)
Async XLA Ops:
  0.6 4.4 %copy-start = (bf16[1,64,128,128]{3,2,1,0:T(8,128)(2,1)S(1)}, bf16[1,64,128,128]{3,2,1,0:T(8,128)(2,1)}, u32[]{:S(2)}) copy-start(bf16[1,64,128,128]{3,2,1,0:T(8,128)(2,1)} %param.20) | copy-start | bytes 6291460
  7.2 3.2 %copy-start.5 = (s32[8,512]{1,0:T(8,128)S(1)}, s32[8,512]{1,0:T(8,128)}, u32[]{:S(2)}) copy-start(s32[8,512]{1,0:T(8,128)} %param.22) | copy-start | bytes 49156
  12.2 1.6 copy-start.1
  18.0 8.3 %collective-permute-start = (bf16[128,4,128]{2,0,1:T(8,128)(2,1)S(1)}, bf16[128,4,128]{2,0,1:T(8,128)(2,1)S(1)}, u32[]{:S(2)}, u32[]{:S(2)}) collective-permute-start(bf16[128,4,128]{2,0,1:T(8,128)(2,1)S(1)} %get-tuple-element.770), channel_id=1, source_target_pairs={{1,0},{2,1},{3,2},{4,3},{5,4},{6,5},{7,6},{8,7},{9,8},{10,9},{11,1... | collective-permute-start | bytes 393224 | tf_op jit(solution)/shard_map/while/body/eval_jaxpr/ppermute | solution.py:18
  19.3 11.0 %collective-permute-start.1 = (bf16[128,4,128]{2,0,1:T(8,128)(2,1)S(1)}, bf16[128,4,128]{2,0,1:T(8,128)(2,1)S(1)}, u32[]{:S(2)}, u32[]{:S(2)}) collective-permute-start(bf16[128,4,128]{2,0,1:T(8,128)(2,1)S(1)} %get-tuple-element.771), channel_id=1, source_target_pairs={{0,1},{1,2},{2,3},{3,4},{4,5},{5,6},{6,7},{7,8},{8,9},{9,10},{10,1... | collective-permute-start | bytes 393224 | tf_op jit(solution)/shard_map/while/body/eval_jaxpr/ppermute | solution.py:17
  26.3 3.9 %copy-start.3 = (bf16[128,4,128]{2,0,1:T(8,128)(2,1)}, bf16[128,4,128]{2,0,1:T(8,128)(2,1)S(1)}, u32[]{:S(2)}) copy-start(bf16[128,4,128]{2,0,1:T(8,128)(2,1)S(1)} %collective-permute-done) | copy-start | bytes 393220 | tf_op jit(solution)/shard_map/while
  30.2 0.7 copy-start.4
  74.0 2.3 %collective-permute-start.2 = (bf16[128,512]{0,1:T(8,128)(2,1)S(1)}, bf16[128,512]{0,1:T(8,128)(2,1)S(1)}, u32[]{:S(2)}, u32[]{:S(2)}) collective-permute-start(bf16[128,512]{0,1:T(8,128)(2,1)S(1)} %bitcast.156), channel_id=1, source_target_pairs={{0,16},{1,17},{2,18},{3,19},{4,20},{5,21},{6,22},{7,23},{8,24},{9,... | collective-permute-start | bytes 393224 | tf_op jit(solution)/shard_map/while/body/eval_jaxpr/ppermute | solution.py:26
  78.0 1.6 copy-start.1
  83.8 8.2 %collective-permute-start = (bf16[128,4,128]{2,0,1:T(8,128)(2,1)S(1)}, bf16[128,4,128]{2,0,1:T(8,128)(2,1)S(1)}, u32[]{:S(2)}, u32[]{:S(2)}) collective-permute-start(bf16[128,4,128]{2,0,1:T(8,128)(2,1)S(1)} %get-tuple-element.770), channel_id=1, source_target_pairs={{1,0},{2,1},{3,2},{4,3},{5,4},{6,5},{7,6},{8,7},{9,8},{10,9},{11,1... | collective-permute-start | bytes 393224 | tf_op jit(solution)/shard_map/while/body/eval_jaxpr/ppermute | solution.py:18
  85.1 7.5 %collective-permute-start.1 = (bf16[128,4,128]{2,0,1:T(8,128)(2,1)S(1)}, bf16[128,4,128]{2,0,1:T(8,128)(2,1)S(1)}, u32[]{:S(2)}, u32[]{:S(2)}) collective-permute-start(bf16[128,4,128]{2,0,1:T(8,128)(2,1)S(1)} %get-tuple-element.771), channel_id=1, source_target_pairs={{0,1},{1,2},{2,3},{3,4},{4,5},{5,6},{6,7},{7,8},{8,9},{9,10},{10,1... | collective-permute-start | bytes 393224 | tf_op jit(solution)/shard_map/while/body/eval_jaxpr/ppermute | solution.py:17
  92.0 0.7 copy-start.3
  92.6 0.7 copy-start.4
  134.4 2.3 %collective-permute-start.2 = (bf16[128,512]{0,1:T(8,128)(2,1)S(1)}, bf16[128,512]{0,1:T(8,128)(2,1)S(1)}, u32[]{:S(2)}, u32[]{:S(2)}) collective-permute-start(bf16[128,512]{0,1:T(8,128)(2,1)S(1)} %bitcast.156), channel_id=1, source_target_pairs={{0,16},{1,17},{2,18},{3,19},{4,20},{5,21},{6,22},{7,23},{8,24},{9,... | collective-permute-start | bytes 393224 | tf_op jit(solution)/shard_map/while/body/eval_jaxpr/ppermute | solution.py:26
  138.5 8.2 %collective-permute-start.3 = (bf16[128,4,128]{2,1,0:T(4,128)(2,1)S(1)}, bf16[128,4,128]{2,1,0:T(4,128)(2,1)S(1)}, u32[]{:S(2)}, u32[]{:S(2)}) collective-permute-start(bf16[128,4,128]{2,1,0:T(4,128)(2,1)S(1)} %reshape.489), channel_id=1, source_target_pairs={{1,0},{2,1},{3,2},{4,3},{5,4},{6,5},{7,6},{8,7},{9,8},{10,9},{11,1... | collective-permute-start | bytes 393224 | tf_op jit(solution)/shard_map/while/body/eval_jaxpr/ppermute | solution.py:18
  139.8 7.5 %collective-permute-start.4 = (bf16[128,4,128]{2,1,0:T(4,128)(2,1)S(1)}, bf16[128,4,128]{2,1,0:T(4,128)(2,1)S(1)}, u32[]{:S(2)}, u32[]{:S(2)}) collective-permute-start(bf16[128,4,128]{2,1,0:T(4,128)(2,1)S(1)} %reshape.489), channel_id=1, source_target_pairs={{0,1},{1,2},{2,3},{3,4},{4,5},{5,6},{6,7},{7,8},{8,9},{9,10},{10,1... | collective-permute-start | bytes 393224 | tf_op jit(solution)/shard_map/while/body/eval_jaxpr/ppermute | solution.py:17
  148.3 2.1 %copy-start.2 = (bf16[64,128,128]{2,1,0:T(8,128)(2,1)S(1)}, bf16[64,128,128]{2,1,0:T(8,128)(2,1)}, u32[]{:S(2)}) copy-start(bf16[64,128,128]{2,1,0:T(8,128)(2,1)} %get-tuple-element.863) | copy-start | bytes 6291460 | tf_op jit(solution)/shard_map/while
  152.4 3.2 %collective-permute-start.5 = (bf16[128,512]{0,1:T(8,128)(2,1)S(1)}, bf16[128,512]{0,1:T(8,128)(2,1)S(1)}, u32[]{:S(2)}, u32[]{:S(2)}) collective-permute-start(bf16[128,512]{0,1:T(8,128)(2,1)S(1)} %get-tuple-element.801), channel_id=1, source_target_pairs={{16,0},{17,1},{18,2},{19,3},{20,4},{21,5},{22,6},{23,7},{24,8},{25... | collective-permute-start | bytes 393224 | tf_op jit(solution)/shard_map/while/body/eval_jaxpr/ppermute | solution.py:26
  156.7 8.2 %collective-permute-start.3 = (bf16[128,4,128]{2,1,0:T(4,128)(2,1)S(1)}, bf16[128,4,128]{2,1,0:T(4,128)(2,1)S(1)}, u32[]{:S(2)}, u32[]{:S(2)}) collective-permute-start(bf16[128,4,128]{2,1,0:T(4,128)(2,1)S(1)} %reshape.489), channel_id=1, source_target_pairs={{1,0},{2,1},{3,2},{4,3},{5,4},{6,5},{7,6},{8,7},{9,8},{10,9},{11,1... | collective-permute-start | bytes 393224 | tf_op jit(solution)/shard_map/while/body/eval_jaxpr/ppermute | solution.py:18
  158.0 9.5 %collective-permute-start.4 = (bf16[128,4,128]{2,1,0:T(4,128)(2,1)S(1)}, bf16[128,4,128]{2,1,0:T(4,128)(2,1)S(1)}, u32[]{:S(2)}, u32[]{:S(2)}) collective-permute-start(bf16[128,4,128]{2,1,0:T(4,128)(2,1)S(1)} %reshape.489), channel_id=1, source_target_pairs={{0,1},{1,2},{2,3},{3,4},{4,5},{5,6},{6,7},{7,8},{8,9},{9,10},{10,1... | collective-permute-start | bytes 393224 | tf_op jit(solution)/shard_map/while/body/eval_jaxpr/ppermute | solution.py:17
  168.4 2.1 %copy-start.2 = (bf16[64,128,128]{2,1,0:T(8,128)(2,1)S(1)}, bf16[64,128,128]{2,1,0:T(8,128)(2,1)}, u32[]{:S(2)}) copy-start(bf16[64,128,128]{2,1,0:T(8,128)(2,1)} %get-tuple-element.863) | copy-start | bytes 6291460 | tf_op jit(solution)/shard_map/while
  172.5 3.2 %collective-permute-start.5 = (bf16[128,512]{0,1:T(8,128)(2,1)S(1)}, bf16[128,512]{0,1:T(8,128)(2,1)S(1)}, u32[]{:S(2)}, u32[]{:S(2)}) collective-permute-start(bf16[128,512]{0,1:T(8,128)(2,1)S(1)} %get-tuple-element.801), channel_id=1, source_target_pairs={{16,0},{17,1},{18,2},{19,3},{20,4},{21,5},{22,6},{23,7},{24,8},{25... | collective-permute-start | bytes 393224 | tf_op jit(solution)/shard_map/while/body/eval_jaxpr/ppermute | solution.py:26
where the time goes:
time: 178 us; the launch traced here: 177 us
  blocking collectives  80.4 us (45%)
  starting transfers between devices  30 us (17%)
  other arithmetic  20.7 us (12%)
  waiting for transfers between devices  18.6 us (10%)
  local copies, waits for them, and re-layouts  14.5 us (8%)
  matrix products  11 us (6%)
    psum x2, blocking collectives, forward_step(): totals = lax.psum(jnp.sum(inside, axis=(1, 2)), 'cell')  80.4 us
    ppermute x4, starting transfers between devices, extended(): before = lax.ppermute(last, axis, up)  19.6 us
    dot_general x2, matrix products, forward_step(): jnp.einsum('sqk,skl->sql', picked, blocks, preferred_element_type=jnp.flo...  7.96 us
    ppermute x4, waiting for transfers between devices, extended(): before = lax.ppermute(last, axis, up)  7.71 us
    ppermute x4, waiting for transfers between devices, shifted(): return lax.ppermute(block, axis, route)  5.71 us
    ppermute x4, starting transfers between devices, shifted(): return lax.ppermute(block, axis, route)  5.18 us
    ppermute x4, starting transfers between devices, extended(): after = lax.ppermute(initial, axis, down)  5.17 us
    ppermute x4, waiting for transfers between devices, extended(): after = lax.ppermute(initial, axis, down)  5.16 us
  transfers between devices with their start and end apart: 12, of which 12 were waited for; matrix products, arithmetic and copies ran while one was open for 2% of the time, Pallas kernels for 0%

commit v1 on v0

v1 whole, which is shorter than its diff:
```python
import functools
import jax
import jax.numpy as jnp
from jax import lax
from jax.experimental import pallas as pl
from jax.experimental.pallas import tpu as pltpu
from jax.sharding import PartitionSpec as P

CELL_TYPES = 16
BAND_REACH = 4
LABEL_ROWS = 16
CHUNKS = 8


def rows_of(block, side):
    return pl.ds(pl.multiple_of(block * side, side), side)


def as_column(row, side):
    return jnp.transpose(jnp.broadcast_to(row, (side, side)))


def as_row(column, side):
    return jnp.transpose(jnp.broadcast_to(column, (side, side)))[0:8]


def one_hot(labels):
    types = lax.broadcasted_iota(jnp.int32, (CELL_TYPES, labels.shape[1]), 0)
    return jnp.concatenate([labels[p : p + 1] == types for p in range(labels.shape[0])], axis=0)


def load_blocks(blocks_hbm, blk, sems):
    part = blk.shape[0] // CHUNKS
    return [
        pltpu.make_async_copy(blocks_hbm.at[0, pl.ds(i * part, part)], blk.at[pl.ds(i * part, part)], sems.at[i])
        for i in range(CHUNKS)
    ]


def push_forward(rows_ref, cols_ref, src, blk, acc, first_row, first_col, copies):
    side = blk.shape[1]
    acc[...] = jnp.zeros_like(acc)
    part = blk.shape[0] // CHUNKS
    for n in range(blk.shape[0]):
        if copies is not None and n % part == 0:
            copies[n // part].wait()
        row = rows_of(rows_ref[0, n] - first_row, side)
        col = rows_of(cols_ref[0, n] - first_col, side)
        acc[col, :] += jnp.dot(src[row, :], blk[n], preferred_element_type=jnp.float32)


def pull_backward(rows_ref, cols_ref, src, blk, acc, first_row, first_col, copies):
    side = blk.shape[1]
    acc[...] = jnp.zeros_like(acc)
    part = blk.shape[0] // CHUNKS
    for n in range(blk.shape[0]):
        if copies is not None and n % part == 0:
            copies[n // part].wait()
        row = rows_of(rows_ref[0, n] - first_row, side)
        col = rows_of(cols_ref[0, n] - first_col, side)
        acc[row, :] += lax.dot_general(
            src[col, :], blk[n], (((1,), (1,)), ((), ())), preferred_element_type=jnp.float32
        )


def fates_of(pulled):
    height, cells = pulled.shape
    grouped = pulled.reshape(height // CELL_TYPES, CELL_TYPES, cells)
    scale = CELL_TYPES / jnp.sum(grouped, axis=1, keepdims=True)
    return (grouped * scale).reshape(height, cells).astype(jnp.bfloat16)


def first_kernel(own, rows_ref, cols_ref, growth_ref, first_ref, last_ref, blocks_hbm,
                 left_ref, mid_ref, right_ref, keep_ref, part_ref, half_ref, blk, src, acc, sems):
    side = blk.shape[1]
    first_row = lax.axis_index("cell") * own
    copies = load_blocks(blocks_hbm, blk, sems)
    for copy in copies:
        copy.start()

    @pl.when(lax.axis_index("tm") == 0)
    def _():
        for b in range(own):
            cells = pl.ds(b * side, side)
            inverse = 1.0 / growth_ref[0:1, cells]
            hot = one_hot(first_ref[:, cells])
            src[pl.ds(b * side, side), :] = jnp.where(hot, inverse, 0.0).astype(jnp.bfloat16)
        push_forward(rows_ref, cols_ref, src, blk, acc, first_row, first_row - BAND_REACH, copies)
        reach = BAND_REACH * side
        inner = own * side
        left_ref[0:reach, :] = acc[0:reach, :].astype(jnp.bfloat16)
        mid_ref[...] = acc[reach : reach + inner, :].astype(jnp.bfloat16)
        right_ref[0:reach, :] = acc[reach + inner :, :].astype(jnp.bfloat16)
        keep_ref[...] = acc[reach : reach + inner, :]
        for b in range(own):
            labels = last_ref[:, b * side : (b + 1) * side].astype(jnp.float32).astype(jnp.bfloat16)
            tall = jnp.concatenate([labels, labels], axis=0)
            left_ref[pl.ds(reach + b * LABEL_ROWS, LABEL_ROWS), :] = tall
            right_ref[pl.ds(reach + b * LABEL_ROWS, LABEL_ROWS), :] = tall
        total = acc[0:side, :]
        for w in range(1, own + 2 * BAND_REACH):
            total += acc[w * side : (w + 1) * side, :]
        sums = jnp.sum(jnp.transpose(total), axis=0, keepdims=True)
        part_ref[0:8, :] = jnp.broadcast_to(sums, (8, side))
        part_ref[8:16, :] = jnp.zeros((8, side), jnp.float32)
        half_ref[...] = jnp.zeros_like(half_ref)

    @pl.when(lax.axis_index("tm") != 0)
    def _():
        for copy in copies:
            copy.wait()
        largest = blk[0].astype(jnp.float32)
        for n in range(1, blk.shape[0]):
            largest = jnp.maximum(largest, blk[n].astype(jnp.float32))
        top = jnp.max(jnp.max(largest, axis=0, keepdims=True), axis=1, keepdims=True)
        half = jnp.round(0.5 * jnp.log2(jnp.maximum(top, 2.0**-126)))
        half_ref[...] = jnp.broadcast_to(half, half_ref.shape)


def second_kernel(own, rows_ref, cols_ref, growth_ref, last_ref, left_ref, mid_ref, right_ref, part_in, half_ref,
                  blocks_hbm, to_left, to_mid, to_right, keep_ref, part_ref, blk, src, acc, fated, pulled, sems):
    side = blk.shape[1]
    here = lax.axis_index("cell")
    first_row = here * own
    reach, inner = BAND_REACH * side, own * side

    @pl.when(lax.axis_index("tm") == 0)
    def _():
        part_ref[...] = part_in[...]

    @pl.when(lax.axis_index("tm") != 0)
    def _():
        copies = load_blocks(blocks_hbm, blk, sems)
        for copy in copies:
            copy.start()
        has_left, has_right = here > 0, here < lax.axis_size("cell") - 1
        sides = []
        mass = []
        for b in range(own):
            at = pl.ds(b * side, side)
            aside = jnp.where(has_left, left_ref[at, :].astype(jnp.float32), 0.0)
            aside += jnp.where(has_right, right_ref[at, :].astype(jnp.float32), 0.0)
            to_mid[pl.ds(inner + b * side, side), :] = aside.astype(jnp.bfloat16)
            mass.append(aside + mid_ref[at, :].astype(jnp.float32))
        top = functools.reduce(jnp.maximum, mass)
        top = jnp.max(top, axis=1, keepdims=True)
        power = jnp.round(jnp.log2(jnp.clip(top, 2.0**-126, 2.0**126)))
        half = half_ref[0:1, 0:1]
        for b in range(own):
            at = pl.ds(b * side, side)
            scaled = (mass[b] * jnp.exp2(-power) * jnp.exp2(-half)).astype(jnp.bfloat16)
            grown = scaled.astype(jnp.float32) / growth_ref[0:1, at]
            src[at, :] = grown.astype(jnp.bfloat16)
        push_forward(rows_ref, cols_ref, src, blk, acc, first_row, first_row - BAND_REACH, copies)
        power_row = as_row(power + half, side)
        to_left[pl.ds(inner, reach), :] = acc[0:reach, :].astype(jnp.bfloat16)
        to_right[pl.ds(inner, reach), :] = acc[reach + inner :, :].astype(jnp.bfloat16)
        keep_ref[...] = acc[reach : reach + inner, :]
        tall = jnp.concatenate([power_row, power_row], axis=0).astype(jnp.bfloat16)
        to_left[pl.ds(inner + reach, 16), :] = tall
        to_right[pl.ds(inner + reach, 16), :] = tall
        total = acc[0:side, :]
        for w in range(1, own + 2 * BAND_REACH):
            total += acc[w * side : (w + 1) * side, :]
        sums = jnp.sum(jnp.transpose(total), axis=0, keepdims=True)
        part_ref[0:8, :] = jnp.broadcast_to(sums, (8, side))
        part_ref[8:16, :] = power_row

        panels = last_ref.shape[0]
        for w in range(own + 2 * BAND_REACH):
            if w < BAND_REACH:
                rows = pl.ds(reach + w * LABEL_ROWS, LABEL_ROWS)
                labels = left_ref[rows, :][0:panels].astype(jnp.float32).astype(jnp.int32)
            elif w < BAND_REACH + own:
                labels = last_ref[:, pl.ds((w - BAND_REACH) * side, side)]
            else:
                rows = pl.ds(reach + (w - BAND_REACH - own) * LABEL_ROWS, LABEL_ROWS)
                labels = right_ref[rows, :][0:panels].astype(jnp.float32).astype(jnp.int32)
            fated[pl.ds(w * side, side), :] = jnp.where(one_hot(labels), 1.0, 0.0).astype(jnp.bfloat16)
        pull_backward(rows_ref, cols_ref, fated, blk, pulled, first_row, first_row - BAND_REACH, None)
        for b in range(own):
            at = pl.ds(b * side, side)
            fates = fates_of(pulled[at, :])
            to_left[at, :] = fates
            to_mid[at, :] = fates
            to_right[at, :] = fates


def third_kernel(own, rows_ref, cols_ref, left_ref, mid_ref, right_ref, mine_ref, blocks_hbm,
                 fate_ref, blk, fated, pulled, sems):
    side = blk.shape[1]
    first_row = lax.axis_index("cell") * own
    reach, inner = BAND_REACH * side, own * side

    @pl.when(lax.axis_index("tm") == 0)
    def _():
        copies = load_blocks(blocks_hbm, blk, sems)
        for copy in copies:
            copy.start()
        fated[0:reach, :] = left_ref[0:reach, :]
        fated[reach : reach + inner, :] = mid_ref[0:inner, :]
        fated[reach + inner :, :] = right_ref[0:reach, :]
        pull_backward(rows_ref, cols_ref, fated, blk, pulled, first_row, first_row - BAND_REACH, copies)
        for b in range(own):
            at = pl.ds(b * side, side)
            fate_ref[0, :, at] = fates_of(pulled[at, :])

    @pl.when(lax.axis_index("tm") != 0)
    def _():
        for b in range(own):
            at = pl.ds(b * side, side)
            fate_ref[0, :, at] = mine_ref[at, :]


def combined(parts):
    top = functools.reduce(jnp.maximum, [part[8:16] for part in parts])
    total = sum(part[0:8] * jnp.exp2(part[8:16] - top) for part in parts)
    return total, top


def last_kernel(own, all_cells, count, *refs):
    part_refs = refs[:count]
    own_part, keep_first, halo_first, keep_second, left_ref, right_ref, mass_ref = refs[count:]
    side = keep_first.shape[1]
    reach, inner = BAND_REACH * side, own * side
    here = lax.axis_index("cell")
    total, top = combined([part[...] for part in part_refs])
    scale = all_cells / as_column(total[0:1], side)

    @pl.when(lax.axis_index("tm") == 0)
    def _():
        for b in range(own):
            at = pl.ds(b * side, side)
            mass = keep_first[at, :] + halo_first[pl.ds(inner + b * side, side), :].astype(jnp.float32)
            mass_ref[0, :, at] = (mass * scale).astype(jnp.bfloat16)

    @pl.when(lax.axis_index("tm") != 0)
    def _():
        has_left, has_right = here > 0, here < lax.axis_size("cell") - 1
        power = pl.ds(inner + reach, 16)
        own_scale = as_column(jnp.exp2(own_part[8:9] - top[0:1]), side)
        left_scale = as_column(jnp.exp2(left_ref[power, :][0:1].astype(jnp.float32) - top[0:1]), side)
        right_scale = as_column(jnp.exp2(right_ref[power, :][0:1].astype(jnp.float32) - top[0:1]), side)
        for b in range(own):
            at = pl.ds(b * side, side)
            aside = pl.ds(inner + b * side, side)
            mass = keep_second[at, :] * own_scale
            mass += jnp.where(has_left, left_ref[aside, :].astype(jnp.float32) * left_scale, 0.0)
            mass += jnp.where(has_right, right_ref[aside, :].astype(jnp.float32) * right_scale, 0.0)
            mass_ref[0, :, at] = (mass * scale).astype(jnp.bfloat16)


def across(array, distance):
    count = lax.axis_size("cell")
    route = []
    for c in range(count):
        there, back = c + distance, c - distance
        route.append((c, count + there if 0 <= there < count else c))
        route.append((count + c, back if 0 <= back < count else count + c))
    return lax.ppermute(array, ("tm", "cell"), route)


def flipped(array, bits):
    return lax.ppermute(array, "cell", [(c, c ^ bits) for c in range(lax.axis_size("cell"))])


def on_device(block_rows, block_cols, block_values, growth, first_labels, last_labels):
    cell_count = lax.axis_size("cell")
    side = block_values.shape[2]
    slots = block_values.shape[1]
    cells = growth.shape[1]
    own = cells // side
    panels = first_labels.shape[0]
    height = panels * CELL_TYPES
    window = own + 2 * BAND_REACH
    reach, inner = BAND_REACH * side, own * side

    smem = pl.BlockSpec(memory_space=pltpu.SMEM)
    vmem = pl.BlockSpec(memory_space=pltpu.VMEM)
    hbm = pl.BlockSpec(memory_space=pl.ANY)
    bf16 = lambda *shape: jax.ShapeDtypeStruct(shape, jnp.bfloat16)
    f32 = lambda *shape: jax.ShapeDtypeStruct(shape, jnp.float32)
    params = pltpu.CompilerParams(vmem_limit_bytes=40 * 1024 * 1024)
    blocks_scratch = pltpu.VMEM((slots, side, side), jnp.bfloat16)
    sems = pltpu.SemaphoreType.DMA((CHUNKS,))

    left, mid, right, keep_first, part, half = pl.pallas_call(
        functools.partial(first_kernel, own),
        out_shape=(
            bf16(reach + own * LABEL_ROWS, side), bf16(inner, side), bf16(reach + own * LABEL_ROWS, side),
            f32(inner, side), f32(16, side), f32(8, side),
        ),
        in_specs=[smem, smem, vmem, vmem, vmem, hbm],
        out_specs=[vmem] * 6,
        scratch_shapes=[
            blocks_scratch, pltpu.VMEM((inner, side), jnp.bfloat16), pltpu.VMEM((window * side, side), jnp.float32), sems,
        ],
        compiler_params=params,
        name="push_first",
    )(block_rows, block_cols, growth, first_labels, last_labels, block_values)

    from_left = across(right, 1)
    from_right = across(left, -1)
    from_mid = across(mid, 0)

    to_left, to_mid, to_right, keep_second, part = pl.pallas_call(
        functools.partial(second_kernel, own),
        out_shape=(
            bf16(inner + reach + 16, side), bf16(2 * inner, side), bf16(inner + reach + 16, side),
            f32(inner, side), f32(16, side),
        ),
        in_specs=[smem, smem] + [vmem] * 7 + [hbm],
        out_specs=[vmem] * 5,
        scratch_shapes=[
            blocks_scratch, pltpu.VMEM((inner, side), jnp.bfloat16), pltpu.VMEM((window * side, side), jnp.float32),
            pltpu.VMEM((window * side, side), jnp.bfloat16), pltpu.VMEM((inner, side), jnp.float32), sems,
        ],
        compiler_params=params,
        name="push_second_pull_first",
    )(block_rows, block_cols, growth, last_labels, from_left, from_mid, from_right, part, half, block_values)

    back_left = across(to_right, -1)
    back_right = across(to_left, 1)
    back_mid = across(to_mid, 0)

    parts = [part]
    bit = 1
    while bit < cell_count:
        if bit > 1:
            total, top = combined(parts)
            parts = [jnp.concatenate([total, top], axis=0)]
        masks = [bit] if 2 * bit >= cell_count else [bit, 2 * bit, 3 * bit]
        parts = [parts[0]] + [flipped(parts[0], mask) for mask in masks]
        bit *= 4

    swap_left = across(back_left, 0)
    swap_right = across(back_right, 0)

    fate = pl.pallas_call(
        functools.partial(third_kernel, own),
        out_shape=bf16(1, height, cells),
        in_specs=[smem, smem] + [vmem] * 4 + [hbm],
        out_specs=vmem,
        scratch_shapes=[
            blocks_scratch, pltpu.VMEM((window * side, side), jnp.bfloat16), pltpu.VMEM((inner, side), jnp.float32), sems,
        ],
        compiler_params=params,
        name="pull_second",
    )(block_rows, block_cols, back_left, back_mid, back_right, to_mid, block_values)

    forward_mass = pl.pallas_call(
        functools.partial(last_kernel, own, float(cells * cell_count), len(parts)),
        out_shape=bf16(1, height, cells),
        in_specs=[vmem] * (len(parts) + 6),
        out_specs=vmem,
        compiler_params=params,
        name="normalise",
    )(*parts, part, keep_first, back_mid, keep_second, swap_left, swap_right)
    return forward_mass, fate


def solution(mesh):
    placed = (
        P("tm", "cell"),
        P("tm", "cell"),
        P("tm", "cell", None, None),
        P("tm", "cell"),
        P(None, "cell"),
        P(None, "cell"),
    )
    return jax.shard_map(
        on_device,
        mesh=mesh,
        in_specs=placed,
        out_specs=(P("tm", None, "cell"), P("tm", None, "cell")),
        check_vma=False,
    )
```

time: 178 us -> 52.9 us (0.30)
  blocking collectives: 80.4 us -> 0 us
  other arithmetic: 20.7 us -> 0.02 us
  matrix products: 11 us -> 0 us
  local copies, waits for them, and re-layouts: 14.5 us -> 5.02 us
  waiting for transfers between devices: 18.6 us -> 9.26 us
  Pallas kernels: 0 us -> 8.37 us
    psum x2 -> x0, blocking collectives: 80.4 us -> none  [forward_step(): totals = lax.psum(jnp.sum(inside, axis=(1, 2)), 'cell')]
    dot_general x4 -> x0, matrix products: 11 us -> none  [the longest x2 7.96 us: forward_step(): jnp.einsum('sqk,skl->sql', picked, blocks, preferred_element_type=jnp.flo...]
    ppermute x12 -> x14, waiting for transfers between devices: 18.6 us -> 9.26 us  [the longest x6 8.25 us: flipped(): lax.ppermute(array, 'cell', [(c, c ^ bits) for c in range(lax.axis_size('...]
    select_n x13 -> x0, other arithmetic: 9.18 us -> none  [the longest x2 3.94 us: backward_step(): picked = jnp.where(hit, candidate, picked)]
    pallas_call x0 -> x4, Pallas kernels: none -> 8.37 us  [the longest x1 4.04 us: on_device(): pl.pallas_call(functools.partial(third_kernel, own), out_shape=bf16(1, he...]
    while x24 -> x0, local copies, waits for them, and re-layouts: 5.49 us -> none
    unnamed x4 -> x16, local copies, waits for them, and re-layouts: 0.01 us -> 5.02 us
    reduce_sum x4 -> x0, other arithmetic: 3.41 us -> none  [the longest x2 3.32 us: forward_step(): totals = lax.psum(jnp.sum(inside, axis=(1, 2)), 'cell')]
  transfers between devices with their start and end apart: 12 -> 14, of which waited for: 12 -> 3; matrix products, arithmetic and copies ran while one was open for 2% -> 0% of each run, Pallas kernels for 0% -> 8%
where the time goes in v1:
time: 52.9 us; the launch traced here: 52.5 us
  starting transfers between devices  29 us (55%)
  waiting for transfers between devices  9.26 us (18%)
  Pallas kernels  8.37 us (16%)
  local copies, waits for them, and re-layouts  5.02 us (9%)
  between operations  0.75 us (1%)
    ppermute x8, starting transfers between devices, across(): return lax.ppermute(array, ('tm', 'cell'), route)  19.9 us
    ppermute x6, starting transfers between devices, flipped(): lax.ppermute(array, 'cell', [(c, c ^ bits) for c in range(lax.axis_size('...  9.14 us
    ppermute x6, waiting for transfers between devices, flipped(): lax.ppermute(array, 'cell', [(c, c ^ bits) for c in range(lax.axis_size('...  8.25 us
    unnamed x16, local copies, waits for them, and re-layouts  5.02 us
    pallas_call x1, Pallas kernels, on_device(): pl.pallas_call(functools.partial(third_kernel, own), out_shape=bf16(1, he...  4.04 us
    pallas_call x1, Pallas kernels, on_device(): pl.pallas_call(functools.partial(first_kernel, own), out_shape=(bf16(reac...  2.9 us
  transfers between devices with their start and end apart: 14, of which 3 were waited for; matrix products, arithmetic and copies ran while one was open for 0% of the time, Pallas kernels for 8%

profile of v1, /device:TPU:0, one launch (start us, length us, event | category | flops | bytes accessed | tf_op | source)
XLA Modules:
  0.0 52.5 jit_solution(10980934573894659490)
XLA Ops:
  0.6 1.6 %copy-done = bf16[1,64,128,128]{3,2,1,0:T(8,128)(2,1)S(1)} copy-done((bf16[1,64,128,128]{3,2,1,0:T(8,128)(2,1)S(1)}, bf16[1,64,128,128]{3,2,1,0:T(8,128)(2,1)}, u32[]{:S(2)}) %copy-start) | copy-done | bytes 2097176
  2.2 0.7 %copy-done.2 = s32[8,512]{1,0:T(8,128)S(1)} copy-done((s32[8,512]{1,0:T(8,128)S(1)}, s32[8,512]{1,0:T(8,128)}, u32[]{:S(2)}) %copy-start.2) | copy-done | bytes 16408
  2.9 0.7 %copy-done.4 = s32[8,512]{1,0:T(8,128)S(1)} copy-done((s32[8,512]{1,0:T(8,128)S(1)}, s32[8,512]{1,0:T(8,128)}, u32[]{:S(2)}) %copy-start.4) | copy-done | bytes 16408
  3.7 0.7 %copy-done.5 = f32[1,512]{1,0:T(1,128)S(1)} copy-done((f32[1,512]{1,0:T(1,128)S(1)}, f32[1,512]{1,0:T(1,128)}, u32[]{:S(2)}) %copy-start.5) | copy-done | bytes 2072
  4.3 0.7 %copy-done.6 = s32[1,64]{1,0:T(1,128)S(1)} copy-done((s32[1,64]{1,0:T(1,128)S(1)}, s32[1,64]{1,0:T(1,128)}, u32[]{:S(2)}) %copy-start.6) | copy-done | bytes 280
  5.0 0.7 %copy-done.7 = s32[1,64]{1,0:T(1,128)S(1)} copy-done((s32[1,64]{1,0:T(1,128)S(1)}, s32[1,64]{1,0:T(1,128)}, u32[]{:S(2)}) %copy-start.7) | copy-done | bytes 280
  5.7 2.9 %push_first.1 = (bf16[576,128]{1,0:T(8,128)(2,1)S(1)}, bf16[512,128]{1,0:T(8,128)(2,1)S(1)}, bf16[576,128]{1,0:T(8,128)(2,1)S(1)}, f32[512,128]{1,0:T(8,128)S(1)...) custom-call(s32[1,64]{1,0:T(1,128)S(1)} %copy-done.6, s32[1,64]{1,0:T(1,128)S(1)} %copy-done.7, f32[1,512]{1,0:T(1,128)S(1)} %copy-done.5, ...), custom_call_target="tpu_custom_call" | custom-call | tf_op jit(solution)/shard_map/push_first/pallas_call | solution.py:287
  8.6 2.5 %collective-permute-start = (bf16[576,128]{1,0:T(8,128)(2,1)S(1)}, bf16[576,128]{1,0:T(8,128)(2,1)S(1)}, u32[]{:S(2)}, u32[]{:S(2)}) collective-permute-start(bf16[576,128]{1,0:T(8,128)(2,1)S(1)} %get-tuple-element.13), channel_id=1, source_target_pairs={{0,17},{16,16},{1,18},{17,0},{2,19},{18,1},{3,20},{19,2},{4,21},{2... | collective-permute-start | bytes 442376 | tf_op jit(solution)/shard_map/ppermute | solution.py:260
  11.1 0.7 %collective-permute-start.2 = (bf16[576,128]{1,0:T(8,128)(2,1)S(1)}, bf16[576,128]{1,0:T(8,128)(2,1)S(1)}, u32[]{:S(2)}, u32[]{:S(2)}) collective-permute-start(bf16[576,128]{1,0:T(8,128)(2,1)S(1)} %get-tuple-element.15), channel_id=1, source_target_pairs={{0,0},{16,1},{1,16},{17,2},{2,17},{18,3},{3,18},{19,4},{4,19},{20,... | collective-permute-start | bytes 442376 | tf_op jit(solution)/shard_map/ppermute | solution.py:260
  11.8 3.7 %collective-permute-start.1 = (bf16[512,128]{1,0:T(8,128)(2,1)S(1)}, bf16[512,128]{1,0:T(8,128)(2,1)S(1)}, u32[]{:S(2)}, u32[]{:S(2)}) collective-permute-start(bf16[512,128]{1,0:T(8,128)(2,1)S(1)} %get-tuple-element.14), channel_id=1, source_target_pairs={{0,16},{16,0},{1,17},{17,1},{2,18},{18,2},{3,19},{19,3},{4,20},{20... | collective-permute-start | bytes 393224 | tf_op jit(solution)/shard_map/ppermute | solution.py:260
  15.5 1.0 %collective-permute-done.1.mid_ref = bf16[512,128]{1,0:T(8,128)(2,1)S(1)} collective-permute-done((bf16[512,128]{1,0:T(8,128)(2,1)S(1)}, bf16[512,128]{1,0:T(8,128)(2,1)S(1)}, u32[]{:S(2)}, u32[]{:S(2)}) %collective-permute-start.1) | collective-permute-done | bytes 131104 | tf_op jit(solution)/shard_map/ppermute | solution.py:260
  16.5 0.6 %push_second_pull_first.1 = (bf16[1040,128]{1,0:T(8,128)(2,1)S(1)}, bf16[1024,128]{1,0:T(8,128)(2,1)S(1)}, bf16[1040,128]{1,0:T(8,128)(2,1)S(1)}, f32[512,128]{1,0:T(8,128)S(1)}, f32[16,128]{1,0:T(8,128)S(1)}) custom-call(s32[1,64]{1,0:T(1,128)S(1)} %copy-done.6, s32[1,64]{1,0:T(1,128)S(1)} %copy-done.7, f32[1,512]{1,0:T(1,128)S(1)} %copy-done.5, ...), custom_call_target="tpu_custom_call" | custom-call | tf_op jit(solution)/shard_map/push_second_pull_first/pallas_call | solution.py:306
  17.2 0.7 %collective-permute-start.10 = (bf16[1040,128]{1,0:T(8,128)(2,1)S(1)}, bf16[1040,128]{1,0:T(8,128)(2,1)S(1)}, u32[]{:S(2)}, u32[]{:S(2)}) collective-permute-start(bf16[1040,128]{1,0:T(8,128)(2,1)S(1)} %get-tuple-element.22), channel_id=1, source_target_pairs={{0,0},{16,1},{1,16},{17,2},{2,17},{18,3},{3,18},{19,4},{4,19},{20,... | collective-permute-start | bytes 798728 | tf_op jit(solution)/shard_map/ppermute | solution.py:260
  17.9 11.7 %collective-permute-start.12 = (bf16[1040,128]{1,0:T(8,128)(2,1)S(1)}, bf16[1040,128]{1,0:T(8,128)(2,1)S(1)}, u32[]{:S(2)}, u32[]{:S(2)}) collective-permute-start(bf16[1040,128]{1,0:T(8,128)(2,1)S(1)} %get-tuple-element.23), channel_id=1, source_target_pairs={{0,17},{16,16},{1,18},{17,0},{2,19},{18,1},{3,20},{19,2},{4,21},{2... | collective-permute-start | bytes 798728 | tf_op jit(solution)/shard_map/ppermute | solution.py:260
  29.6 1.4 %collective-permute-start.3 = (f32[16,128]{1,0:T(8,128)S(1)}, f32[16,128]{1,0:T(8,128)S(1)}, u32[]{:S(2)}, u32[]{:S(2)}) collective-permute-start(f32[16,128]{1,0:T(8,128)S(1)} %get-tuple-element.18.refs_4_), channel_id=1, source_target_pairs={{0,1},{1,0},{2,3},{3,2},{4,5},{5,4},{6,7},{7,6},{8,9},{9,8},{10,11... | collective-permute-start | bytes 24584 | tf_op jit(solution)/shard_map/ppermute | solution.py:264
  30.9 2.5 %collective-permute-start.4 = (f32[16,128]{1,0:T(8,128)S(1)}, f32[16,128]{1,0:T(8,128)S(1)}, u32[]{:S(2)}, u32[]{:S(2)}) collective-permute-start(f32[16,128]{1,0:T(8,128)S(1)} %get-tuple-element.18.refs_4_), channel_id=1, source_target_pairs={{0,2},{1,3},{2,0},{3,1},{4,6},{5,7},{6,4},{7,5},{8,10},{9,11},{10,... | collective-permute-start | bytes 24584 | tf_op jit(solution)/shard_map/ppermute | solution.py:264
  33.4 7.1 %collective-permute-done.3 = f32[16,128]{1,0:T(8,128)S(1)} collective-permute-done((f32[16,128]{1,0:T(8,128)S(1)}, f32[16,128]{1,0:T(8,128)S(1)}, u32[]{:S(2)}, u32[]{:S(2)}) %collective-permute-start.3) | collective-permute-done | bytes 8224 | tf_op jit(solution)/shard_map/ppermute | solution.py:264
  40.5 0.5 collective-permute-start.11
  41.2 2.4 %collective-permute-start.6 = (f32[16,128]{1,0:T(8,128)S(1)}, f32[16,128]{1,0:T(8,128)S(1)}, u32[]{:S(2)}, u32[]{:S(2)}) collective-permute-start(f32[16,128]{1,0:T(8,128)S(1)} %pad_maximum_fusion.refs_0_), channel_id=1, source_target_pairs={{0,4},{1,5},{2,6},{3,7},{4,0},{5,1},{6,2},{7,3},{8,12},{9,13},{10,... | collective-permute-start | bytes 24584 | tf_op jit(solution)/shard_map/ppermute | solution.py:264
  43.6 2.6 %collective-permute-start.7 = (f32[16,128]{1,0:T(8,128)S(1)}, f32[16,128]{1,0:T(8,128)S(1)}, u32[]{:S(2)}, u32[]{:S(2)}) collective-permute-start(f32[16,128]{1,0:T(8,128)S(1)} %pad_maximum_fusion.refs_0_), channel_id=1, source_target_pairs={{0,8},{1,9},{2,10},{3,11},{4,12},{5,13},{6,14},{7,15},{8,0},{9,1},... | collective-permute-start | bytes 24584 | tf_op jit(solution)/shard_map/ppermute | solution.py:264
  46.2 0.3 collective-permute-start.8
  46.5 4.0 %pull_second.1 = bf16[1,128,512]{2,1,0:T(8,128)(2,1)} custom-call(s32[1,64]{1,0:T(1,128)S(1)} %copy-done.6, s32[1,64]{1,0:T(1,128)S(1)} %copy-done.7, bf16[1040,128]{1,0:T(8,128)(2,1)S(1)} %collective-permute-done.10.left_ref, bf16[1024,128]{1,0:T(8,128)(2,1)S(1)} %collective-permute-done.9.refs_6_.mid_ref, ...), custom_call_target="tpu_custom_call" | custom-call | tf_op jit(solution)/shard_map/pull_second/pallas_call | solution.py:339
  50.5 1.1 %collective-permute-done.8.refs_3_ = f32[16,128]{1,0:T(8,128)S(1)} collective-permute-done((f32[16,128]{1,0:T(8,128)S(1)}, f32[16,128]{1,0:T(8,128)S(1)}, u32[]{:S(2)}, u32[]{:S(2)}) %collective-permute-start.8) | collective-permute-done | bytes 8224 | tf_op jit(solution)/shard_map/ppermute | solution.py:264
  51.6 0.8 %normalise.1 = bf16[1,128,512]{2,1,0:T(8,128)(2,1)} custom-call(f32[16,128]{1,0:T(8,128)S(1)} %pad_maximum_fusion.refs_0_, f32[16,128]{1,0:T(8,128)S(1)} %collective-permute-done.6.refs_1_, f32[16,128]{1,0:T(8,128)S(1)} %collective-permute-done.7.refs_2_, f32[16,128]{1,0:T(8,128)S(1)} %collective-permute-done.8.refs_3_, ...), custom_call_target="tpu_custom_call" | custom-call | tf_op jit(solution)/shard_map/normalise/pallas_call | solution.py:351
  (26 shorter events, 0.1 us)
Async XLA Ops:
  0.6 1.6 %copy-start = (bf16[1,64,128,128]{3,2,1,0:T(8,128)(2,1)S(1)}, bf16[1,64,128,128]{3,2,1,0:T(8,128)(2,1)}, u32[]{:S(2)}) copy-start(bf16[1,64,128,128]{3,2,1,0:T(8,128)(2,1)} %blocks_hbm.5) | copy-start | bytes 6291460
  2.2 0.7 %copy-start.2 = (s32[8,512]{1,0:T(8,128)S(1)}, s32[8,512]{1,0:T(8,128)}, u32[]{:S(2)}) copy-start(s32[8,512]{1,0:T(8,128)} %last_ref.3) | copy-start | bytes 49156
  2.9 0.7 %copy-start.4 = (s32[8,512]{1,0:T(8,128)S(1)}, s32[8,512]{1,0:T(8,128)}, u32[]{:S(2)}) copy-start(s32[8,512]{1,0:T(8,128)} %first_ref.1) | copy-start | bytes 49156
  3.7 0.7 %copy-start.5 = (f32[1,512]{1,0:T(1,128)S(1)}, f32[1,512]{1,0:T(1,128)}, u32[]{:S(2)}) copy-start(f32[1,512]{1,0:T(1,128)} %growth_ref.3) | copy-start | bytes 6148
  4.3 0.7 %copy-start.6 = (s32[1,64]{1,0:T(1,128)S(1)}, s32[1,64]{1,0:T(1,128)}, u32[]{:S(2)}) copy-start(s32[1,64]{1,0:T(1,128)} %rows_ref.5) | copy-start | bytes 772
  5.0 0.7 %copy-start.7 = (s32[1,64]{1,0:T(1,128)S(1)}, s32[1,64]{1,0:T(1,128)}, u32[]{:S(2)}) copy-start(s32[1,64]{1,0:T(1,128)} %cols_ref.5) | copy-start | bytes 772
  5.7 10.9 %copy-start.1 = (bf16[1,64,128,128]{3,2,1,0:T(8,128)(2,1)S(1)}, bf16[1,64,128,128]{3,2,1,0:T(8,128)(2,1)}, u32[]{:S(2)}) copy-start(bf16[1,64,128,128]{3,2,1,0:T(8,128)(2,1)} %blocks_hbm.5) | copy-start | bytes 6291460
  5.7 10.9 %copy-start.3 = (s32[8,512]{1,0:T(8,128)S(1)}, s32[8,512]{1,0:T(8,128)}, u32[]{:S(2)}) copy-start(s32[8,512]{1,0:T(8,128)} %last_ref.3) | copy-start | bytes 49156
  8.6 7.9 %collective-permute-start = (bf16[576,128]{1,0:T(8,128)(2,1)S(1)}, bf16[576,128]{1,0:T(8,128)(2,1)S(1)}, u32[]{:S(2)}, u32[]{:S(2)}) collective-permute-start(bf16[576,128]{1,0:T(8,128)(2,1)S(1)} %get-tuple-element.13), channel_id=1, source_target_pairs={{0,17},{16,16},{1,18},{17,0},{2,19},{18,1},{3,20},{19,2},{4,21},{2... | collective-permute-start | bytes 442376 | tf_op jit(solution)/shard_map/ppermute | solution.py:260
  11.1 5.4 %collective-permute-start.2 = (bf16[576,128]{1,0:T(8,128)(2,1)S(1)}, bf16[576,128]{1,0:T(8,128)(2,1)S(1)}, u32[]{:S(2)}, u32[]{:S(2)}) collective-permute-start(bf16[576,128]{1,0:T(8,128)(2,1)S(1)} %get-tuple-element.15), channel_id=1, source_target_pairs={{0,0},{16,1},{1,16},{17,2},{2,17},{18,3},{3,18},{19,4},{4,19},{20,... | collective-permute-start | bytes 442376 | tf_op jit(solution)/shard_map/ppermute | solution.py:260
  11.8 4.7 %collective-permute-start.1 = (bf16[512,128]{1,0:T(8,128)(2,1)S(1)}, bf16[512,128]{1,0:T(8,128)(2,1)S(1)}, u32[]{:S(2)}, u32[]{:S(2)}) collective-permute-start(bf16[512,128]{1,0:T(8,128)(2,1)S(1)} %get-tuple-element.14), channel_id=1, source_target_pairs={{0,16},{16,0},{1,17},{17,1},{2,18},{18,2},{3,19},{19,3},{4,20},{20... | collective-permute-start | bytes 393224 | tf_op jit(solution)/shard_map/ppermute | solution.py:260
  17.2 23.4 %collective-permute-start.10 = (bf16[1040,128]{1,0:T(8,128)(2,1)S(1)}, bf16[1040,128]{1,0:T(8,128)(2,1)S(1)}, u32[]{:S(2)}, u32[]{:S(2)}) collective-permute-start(bf16[1040,128]{1,0:T(8,128)(2,1)S(1)} %get-tuple-element.22), channel_id=1, source_target_pairs={{0,0},{16,1},{1,16},{17,2},{2,17},{18,3},{3,18},{19,4},{4,19},{20,... | collective-permute-start | bytes 798728 | tf_op jit(solution)/shard_map/ppermute | solution.py:260
  17.9 23.2 %collective-permute-start.12 = (bf16[1040,128]{1,0:T(8,128)(2,1)S(1)}, bf16[1040,128]{1,0:T(8,128)(2,1)S(1)}, u32[]{:S(2)}, u32[]{:S(2)}) collective-permute-start(bf16[1040,128]{1,0:T(8,128)(2,1)S(1)} %get-tuple-element.23), channel_id=1, source_target_pairs={{0,17},{16,16},{1,18},{17,0},{2,19},{18,1},{3,20},{19,2},{4,21},{2... | collective-permute-start | bytes 798728 | tf_op jit(solution)/shard_map/ppermute | solution.py:260
  29.6 11.0 %collective-permute-start.3 = (f32[16,128]{1,0:T(8,128)S(1)}, f32[16,128]{1,0:T(8,128)S(1)}, u32[]{:S(2)}, u32[]{:S(2)}) collective-permute-start(f32[16,128]{1,0:T(8,128)S(1)} %get-tuple-element.18.refs_4_), channel_id=1, source_target_pairs={{0,1},{1,0},{2,3},{3,2},{4,5},{5,4},{6,7},{7,6},{8,9},{9,8},{10,11... | collective-permute-start | bytes 24584 | tf_op jit(solution)/shard_map/ppermute | solution.py:264
  30.9 10.2 %collective-permute-start.4 = (f32[16,128]{1,0:T(8,128)S(1)}, f32[16,128]{1,0:T(8,128)S(1)}, u32[]{:S(2)}, u32[]{:S(2)}) collective-permute-start(f32[16,128]{1,0:T(8,128)S(1)} %get-tuple-element.18.refs_4_), channel_id=1, source_target_pairs={{0,2},{1,3},{2,0},{3,1},{4,6},{5,7},{6,4},{7,5},{8,10},{9,11},{10,... | collective-permute-start | bytes 24584 | tf_op jit(solution)/shard_map/ppermute | solution.py:264
  33.4 7.7 %collective-permute-start.5 = (f32[16,128]{1,0:T(8,128)S(1)}, f32[16,128]{1,0:T(8,128)S(1)}, u32[]{:S(2)}, u32[]{:S(2)}) collective-permute-start(f32[16,128]{1,0:T(8,128)S(1)} %get-tuple-element.18.refs_4_), channel_id=1, source_target_pairs={{0,3},{1,2},{2,1},{3,0},{4,7},{5,6},{6,5},{7,4},{8,11},{9,10},{10,... | collective-permute-start | bytes 24584 | tf_op jit(solution)/shard_map/ppermute | solution.py:264
  40.5 5.6 %collective-permute-start.9 = (bf16[1024,128]{1,0:T(8,128)(2,1)S(1)}, bf16[1024,128]{1,0:T(8,128)(2,1)S(1)}, u32[]{:S(2)}, u32[]{:S(2)}) collective-permute-start(bf16[1024,128]{1,0:T(8,128)(2,1)S(1)} %get-tuple-element.20.mine_ref), channel_id=1, source_target_pairs={{0,16},{16,0},{1,17},{17,1},{2,18},{18,2},{3,19},{19,3},{4,20},{20... | collective-permute-start | bytes 786440 | tf_op jit(solution)/shard_map/ppermute | solution.py:260
  40.5 11.1 %collective-permute-start.11 = (bf16[1040,128]{1,0:T(8,128)(2,1)S(1)}, bf16[1040,128]{1,0:T(8,128)(2,1)S(1)}, u32[]{:S(2)}, u32[]{:S(2)}) collective-permute-start(bf16[1040,128]{1,0:T(8,128)(2,1)S(1)} %collective-permute-done.10.left_ref), channel_id=1, source_target_pairs={{0,16},{16,0},{1,17},{17,1},{2,18},{18,2},{3,19},{19,3},{4,20},{20... | collective-permute-start | bytes 798728 | tf_op jit(solution)/shard_map/ppermute | solution.py:260
  41.1 10.6 %collective-permute-start.13 = (bf16[1040,128]{1,0:T(8,128)(2,1)S(1)}, bf16[1040,128]{1,0:T(8,128)(2,1)S(1)}, u32[]{:S(2)}, u32[]{:S(2)}) collective-permute-start(bf16[1040,128]{1,0:T(8,128)(2,1)S(1)} %collective-permute-done.12.right_ref), channel_id=1, source_target_pairs={{0,16},{16,0},{1,17},{17,1},{2,18},{18,2},{3,19},{19,3},{4,20},{20... | collective-permute-start | bytes 798728 | tf_op jit(solution)/shard_map/ppermute | solution.py:260
  41.2 9.3 %collective-permute-start.6 = (f32[16,128]{1,0:T(8,128)S(1)}, f32[16,128]{1,0:T(8,128)S(1)}, u32[]{:S(2)}, u32[]{:S(2)}) collective-permute-start(f32[16,128]{1,0:T(8,128)S(1)} %pad_maximum_fusion.refs_0_), channel_id=1, source_target_pairs={{0,4},{1,5},{2,6},{3,7},{4,0},{5,1},{6,2},{7,3},{8,12},{9,13},{10,... | collective-permute-start | bytes 24584 | tf_op jit(solution)/shard_map/ppermute | solution.py:264
  43.6 6.9 %collective-permute-start.7 = (f32[16,128]{1,0:T(8,128)S(1)}, f32[16,128]{1,0:T(8,128)S(1)}, u32[]{:S(2)}, u32[]{:S(2)}) collective-permute-start(f32[16,128]{1,0:T(8,128)S(1)} %pad_maximum_fusion.refs_0_), channel_id=1, source_target_pairs={{0,8},{1,9},{2,10},{3,11},{4,12},{5,13},{6,14},{7,15},{8,0},{9,1},... | collective-permute-start | bytes 24584 | tf_op jit(solution)/shard_map/ppermute | solution.py:264
  46.2 5.4 %collective-permute-start.8 = (f32[16,128]{1,0:T(8,128)S(1)}, f32[16,128]{1,0:T(8,128)S(1)}, u32[]{:S(2)}, u32[]{:S(2)}) collective-permute-start(f32[16,128]{1,0:T(8,128)S(1)} %pad_maximum_fusion.refs_0_), channel_id=1, source_target_pairs={{0,12},{1,13},{2,14},{3,15},{4,8},{5,9},{6,10},{7,11},{8,4},{9,5},... | collective-permute-start | bytes 24584 | tf_op jit(solution)/shard_map/ppermute | solution.py:264

commit v2 on v1

v2 whole, which is shorter than its diff:
```python
import functools
import jax
import jax.numpy as jnp
from jax import lax
from jax.experimental import pallas as pl
from jax.experimental.pallas import tpu as pltpu
from jax.sharding import PartitionSpec as P

CELL_TYPES = 16
BAND_REACH = 4
LABEL_ROWS = 16
CHUNKS = 8
XA = ((0,), (0,), (0,1))
XB = ((1,), (1,), (0,1))
XC = (0,1)


def rows_of(block, side):
    return pl.ds(pl.multiple_of(block * side, side), side)


def as_column(row, side):
    return jnp.transpose(jnp.broadcast_to(row, (side, side)))


def as_row(column, side):
    return jnp.transpose(jnp.broadcast_to(column, (side, side)))[0:8]


def one_hot(labels):
    types = lax.broadcasted_iota(jnp.int32, (CELL_TYPES, labels.shape[1]), 0)
    return jnp.concatenate([labels[p : p + 1] == types for p in range(labels.shape[0])], axis=0)


def pull_backward(table, src, blk, out, own):
    side = blk.shape[-1]
    per_row = blk.shape[0] // own
    for row in range(own):
        total = None
        for first in range(row * per_row, (row + 1) * per_row, 2):
            slots = [table[0, first], table[0, first + 1]]
            spots = [rows_of(table[1, first], side), rows_of(table[1, first + 1], side)]
            wide = jnp.concatenate([src[spot, :] for spot in spots], axis=1)
            pair = jnp.concatenate([blk[slot] for slot in slots], axis=1)
            pulled = lax.dot_general(wide, pair, (((1,), (1,)), ((), ())), preferred_element_type=jnp.float32)
            total = pulled if total is None else total + pulled
        out[row * side : (row + 1) * side, :] = total


def fates_of(pulled):
    height, cells = pulled.shape
    grouped = pulled.reshape(height // CELL_TYPES, CELL_TYPES, cells)
    scale = CELL_TYPES / jnp.sum(grouped, axis=1, keepdims=True)
    return (grouped * scale).reshape(height, cells).astype(jnp.bfloat16)


def first_kernel(own, rows_hbm, cols_hbm, growth_hbm, first_hbm, last_hbm, blocks_hbm,
                 left_ref, mid_ref, right_ref, keep_ref, part_ref, half_ref, table_hbm, growth, labels, blk,
                 rows, cols, src, acc, count, table, small_sems, sems):
    side = blk.shape[1]
    slots = blk.shape[0]
    first_row = lax.axis_index("cell") * own
    first_col = first_row - BAND_REACH
    on_first = lax.axis_index("tm") == 0
    chunk = slots // CHUNKS
    small = [
        pltpu.make_async_copy(rows_hbm, rows, small_sems.at[0]),
        pltpu.make_async_copy(cols_hbm, cols, small_sems.at[1]),
        pltpu.make_async_copy(growth_hbm, growth, small_sems.at[2]),
        pltpu.make_async_copy(first_hbm, labels.at[0], small_sems.at[3]),
        pltpu.make_async_copy(last_hbm, labels.at[1], small_sems.at[4]),
    ]
    copies = [
        pltpu.make_async_copy(blocks_hbm.at[0, pl.ds(i * chunk, chunk)], blk.at[pl.ds(i * chunk, chunk)], sems.at[i])
        for i in range(CHUNKS)
    ]
    for copy in small + copies:
        copy.start()
    small[0].wait()
    small[1].wait()
    for row in range(own):
        count[row] = row * (slots // own)
    for n in range(slots):
        row = rows[0, n] - first_row
        place = count[row]
        count[row] = place + 1
        table[0, place] = n
        table[1, place] = cols[0, n] - first_col
    table_copy = pltpu.make_async_copy(table, table_hbm, small_sems.at[5])
    table_copy.start()
    for copy in small[2:]:
        copy.wait()

    @pl.when(on_first)
    def _():
        for b in range(own):
            cells = pl.ds(b * side, side)
            inverse = 1.0 / growth[0:1, cells]
            hot = one_hot(labels[0, :, cells])
            src[pl.ds(b * side, side), :] = jnp.where(hot, inverse, 0.0).astype(jnp.bfloat16)
        acc[...] = jnp.zeros_like(acc)
        for n in range(slots):
            if n % chunk == 0:
                copies[n // chunk].wait()
            row = rows_of(rows[0, n] - first_row, side)
            col = rows_of(cols[0, n] - first_col, side)
            acc[col, :] += jnp.dot(src[row, :], blk[n], preferred_element_type=jnp.float32)
        reach = BAND_REACH * side
        inner = own * side
        left_ref[0:reach, :] = acc[0:reach, :].astype(jnp.bfloat16)
        mid_ref[...] = acc[reach : reach + inner, :].astype(jnp.bfloat16)
        right_ref[0:reach, :] = acc[reach + inner :, :].astype(jnp.bfloat16)
        keep_ref[...] = acc[reach : reach + inner, :]
        for b in range(own):
            known = labels[1, :, pl.ds(b * side, side)].astype(jnp.float32).astype(jnp.bfloat16)
            tall = jnp.concatenate([known, known], axis=0)
            left_ref[pl.ds(reach + b * LABEL_ROWS, LABEL_ROWS), :] = tall
            right_ref[pl.ds(reach + b * LABEL_ROWS, LABEL_ROWS), :] = tall
        total = acc[0:side, :]
        for w in range(1, own + 2 * BAND_REACH):
            total += acc[w * side : (w + 1) * side, :]
        sums = jnp.sum(jnp.transpose(total), axis=0, keepdims=True)
        part_ref[0:8, :] = jnp.broadcast_to(sums, (8, side))
        part_ref[8:16, :] = jnp.zeros((8, side), jnp.float32)

    @pl.when(jnp.logical_not(on_first))
    def _():
        for copy in copies:
            copy.wait()
        largest = blk[0].astype(jnp.float32)
        for n in range(1, slots):
            largest = jnp.maximum(largest, blk[n].astype(jnp.float32))
        top = jnp.max(jnp.max(largest, axis=0, keepdims=True), axis=1, keepdims=True)
        half = jnp.round(0.5 * jnp.log2(jnp.maximum(top, 2.0**-126)))
        half_ref[...] = jnp.broadcast_to(half, half_ref.shape)

    table_copy.wait()


def second_kernel(own, table_hbm, growth_ref, labels_ref, left_ref, mid_ref, right_ref, part_in, half_ref, blk,
                  to_left, to_mid, to_right, keep_ref, part_ref, table, src, acc, fated, pulled, sem):
    side = blk.shape[1]
    slots = blk.shape[0]
    here = lax.axis_index("cell")
    reach, inner = BAND_REACH * side, own * side

    @pl.when(lax.axis_index("tm") == 0)
    def _():
        part_ref[...] = part_in[...]

    @pl.when(lax.axis_index("tm") != 0)
    def _():
        table_copy = pltpu.make_async_copy(table_hbm, table, sem)
        table_copy.start()
        has_left, has_right = here > 0, here < lax.axis_size("cell") - 1
        mass = []
        for b in range(own):
            at = pl.ds(b * side, side)
            aside = jnp.where(has_left, left_ref[at, :].astype(jnp.float32), 0.0)
            aside += jnp.where(has_right, right_ref[at, :].astype(jnp.float32), 0.0)
            to_mid[pl.ds(inner + b * side, side), :] = aside.astype(jnp.bfloat16)
            mass.append(aside + mid_ref[at, :].astype(jnp.float32))
        top = functools.reduce(jnp.maximum, mass)
        top = jnp.max(top, axis=1, keepdims=True)
        power = jnp.round(jnp.log2(jnp.clip(top, 2.0**-126, 2.0**126)))
        half = half_ref[0:1, 0:1]
        for b in range(own):
            at = pl.ds(b * side, side)
            scaled = (mass[b] * jnp.exp2(-power) * jnp.exp2(-half)).astype(jnp.bfloat16)
            grown = scaled.astype(jnp.float32) / growth_ref[0:1, at]
            src[at, :] = grown.astype(jnp.bfloat16)
        acc[...] = jnp.zeros_like(acc)
        table_copy.wait()
        for n in range(slots):
            row = n // (slots // own) * side
            col = rows_of(table[1, n], side)
            acc[col, :] += jnp.dot(src[row : row + side, :], blk[table[0, n]], preferred_element_type=jnp.float32)
        power_row = as_row(power + half, side)
        to_left[pl.ds(inner, reach), :] = acc[0:reach, :].astype(jnp.bfloat16)
        to_right[pl.ds(inner, reach), :] = acc[reach + inner :, :].astype(jnp.bfloat16)
        keep_ref[...] = acc[reach : reach + inner, :]
        tall = jnp.concatenate([power_row, power_row], axis=0).astype(jnp.bfloat16)
        to_left[pl.ds(inner + reach, 16), :] = tall
        to_right[pl.ds(inner + reach, 16), :] = tall
        total = acc[0:side, :]
        for w in range(1, own + 2 * BAND_REACH):
            total += acc[w * side : (w + 1) * side, :]
        sums = jnp.sum(jnp.transpose(total), axis=0, keepdims=True)
        part_ref[0:8, :] = jnp.broadcast_to(sums, (8, side))
        part_ref[8:16, :] = power_row

        panels = labels_ref.shape[1]
        for w in range(own + 2 * BAND_REACH):
            if w < BAND_REACH:
                rows = pl.ds(reach + w * LABEL_ROWS, LABEL_ROWS)
                labels = left_ref[rows, :][0:panels].astype(jnp.float32).astype(jnp.int32)
            elif w < BAND_REACH + own:
                labels = labels_ref[1, :, pl.ds((w - BAND_REACH) * side, side)]
            else:
                rows = pl.ds(reach + (w - BAND_REACH - own) * LABEL_ROWS, LABEL_ROWS)
                labels = right_ref[rows, :][0:panels].astype(jnp.float32).astype(jnp.int32)
            fated[pl.ds(w * side, side), :] = jnp.where(one_hot(labels), 1.0, 0.0).astype(jnp.bfloat16)
        pull_backward(table, fated, blk, pulled, own)
        for b in range(own):
            at = pl.ds(b * side, side)
            fates = fates_of(pulled[at, :])
            to_left[at, :] = fates
            to_mid[at, :] = fates
            to_right[at, :] = fates


def third_kernel(own, table_hbm, left_ref, mid_ref, right_ref, mine_ref, blk, fate_ref, table, fated, pulled, sem):
    side = blk.shape[1]
    reach, inner = BAND_REACH * side, own * side

    @pl.when(lax.axis_index("tm") == 0)
    def _():
        table_copy = pltpu.make_async_copy(table_hbm, table, sem)
        table_copy.start()
        fated[0:reach, :] = left_ref[0:reach, :]
        fated[reach : reach + inner, :] = mid_ref[0:inner, :]
        fated[reach + inner :, :] = right_ref[0:reach, :]
        table_copy.wait()
        pull_backward(table, fated, blk, pulled, own)
        for b in range(own):
            at = pl.ds(b * side, side)
            fate_ref[0, :, at] = fates_of(pulled[at, :])

    @pl.when(lax.axis_index("tm") != 0)
    def _():
        for b in range(own):
            at = pl.ds(b * side, side)
            fate_ref[0, :, at] = mine_ref[at, :]


def combined(parts):
    top = functools.reduce(jnp.maximum, [part[8:16] for part in parts])
    total = sum(part[0:8] * jnp.exp2(part[8:16] - top) for part in parts)
    return total, top


def last_kernel(own, all_cells, count, *refs):
    part_refs = refs[:count]
    own_part, keep_first, halo_first, keep_second, left_ref, right_ref, mass_ref = refs[count:]
    side = keep_first.shape[1]
    reach, inner = BAND_REACH * side, own * side
    here = lax.axis_index("cell")
    total, top = combined([part[...] for part in part_refs])
    scale = all_cells / as_column(total[0:1], side)

    @pl.when(lax.axis_index("tm") == 0)
    def _():
        for b in range(own):
            at = pl.ds(b * side, side)
            mass = keep_first[at, :] + halo_first[pl.ds(inner + b * side, side), :].astype(jnp.float32)
            mass_ref[0, :, at] = (mass * scale).astype(jnp.bfloat16)

    @pl.when(lax.axis_index("tm") != 0)
    def _():
        has_left, has_right = here > 0, here < lax.axis_size("cell") - 1
        power = pl.ds(inner + reach, 16)
        own_scale = as_column(jnp.exp2(own_part[8:9] - top[0:1]), side)
        left_scale = as_column(jnp.exp2(left_ref[power, :][0:1].astype(jnp.float32) - top[0:1]), side)
        right_scale = as_column(jnp.exp2(right_ref[power, :][0:1].astype(jnp.float32) - top[0:1]), side)
        for b in range(own):
            at = pl.ds(b * side, side)
            aside = pl.ds(inner + b * side, side)
            mass = keep_second[at, :] * own_scale
            mass += jnp.where(has_left, left_ref[aside, :].astype(jnp.float32) * left_scale, 0.0)
            mass += jnp.where(has_right, right_ref[aside, :].astype(jnp.float32) * right_scale, 0.0)
            mass_ref[0, :, at] = (mass * scale).astype(jnp.bfloat16)


def across(array, distance, ways=(0, 1)):
    count = lax.axis_size("cell")
    route = []
    for c in range(count):
        there, back = c + distance, c - distance
        if 0 in ways and (0 <= there < count or len(ways) == 2):
            route.append((c, count + there if 0 <= there < count else c))
        if 1 in ways and (0 <= back < count or len(ways) == 2):
            route.append((count + c, back if 0 <= back < count else count + c))
    return lax.ppermute(array, ("tm", "cell"), route)


def flipped(array, bits):
    return lax.ppermute(array, "cell", [(c, c ^ bits) for c in range(lax.axis_size("cell"))])


def on_device(block_rows, block_cols, block_values, growth, first_labels, last_labels):
    cell_count = lax.axis_size("cell")
    side = block_values.shape[2]
    slots = block_values.shape[1]
    cells = growth.shape[1]
    own = cells // side
    panels = first_labels.shape[0]
    height = panels * CELL_TYPES
    window = own + 2 * BAND_REACH
    reach, inner = BAND_REACH * side, own * side

    smem = pl.BlockSpec(memory_space=pltpu.SMEM)
    vmem = pl.BlockSpec(memory_space=pltpu.VMEM)
    hbm = pl.BlockSpec(memory_space=pltpu.HBM)
    bf16 = lambda *shape: jax.ShapeDtypeStruct(shape, jnp.bfloat16)
    f32 = lambda *shape: jax.ShapeDtypeStruct(shape, jnp.float32)
    params = pltpu.CompilerParams(vmem_limit_bytes=16 * 1024 * 1024)
    table_scratch = pltpu.SMEM((2, slots), jnp.int32)
    sem = pltpu.SemaphoreType.DMA

    left, mid, right, keep_first, part, half, table, grown, labels, blocks = pl.pallas_call(
        functools.partial(first_kernel, own),
        out_shape=(
            bf16(reach + own * LABEL_ROWS, side), bf16(inner, side), bf16(reach + own * LABEL_ROWS, side),
            f32(inner, side), f32(16, side), f32(8, side), jax.ShapeDtypeStruct((2, slots), jnp.int32),
            f32(1, cells), jax.ShapeDtypeStruct((2, panels, cells), jnp.int32), bf16(slots, side, side),
        ),
        in_specs=[hbm] * 6,
        out_specs=[vmem] * 6 + [hbm] + [vmem] * 3,
        scratch_shapes=[
            pltpu.SMEM((1, slots), jnp.int32), pltpu.SMEM((1, slots), jnp.int32),
            pltpu.VMEM((inner, side), jnp.bfloat16), pltpu.VMEM((window * side, side), jnp.float32),
            pltpu.SMEM((own,), jnp.int32), table_scratch, sem((6,)), sem((CHUNKS,)),
        ],
        compiler_params=params,
        name="push_first",
    )(*[pltpu.with_memory_space_constraint(array, pltpu.HBM) for array in (
        block_rows, block_cols, growth, first_labels, last_labels, block_values
    )])

    from_left = across(right, 1, XA[0])
    from_right = across(left, -1, XA[1])
    from_mid = across(mid, 0, XA[2])

    to_left, to_mid, to_right, keep_second, part = pl.pallas_call(
        functools.partial(second_kernel, own),
        out_shape=(
            bf16(inner + reach + 16, side), bf16(2 * inner, side), bf16(inner + reach + 16, side),
            f32(inner, side), f32(16, side),
        ),
        in_specs=[hbm] + [vmem] * 8,
        out_specs=[vmem] * 5,
        scratch_shapes=[
            table_scratch, pltpu.VMEM((inner, side), jnp.bfloat16), pltpu.VMEM((window * side, side), jnp.float32),
            pltpu.VMEM((window * side, side), jnp.bfloat16), pltpu.VMEM((inner, side), jnp.float32), sem,
        ],
        compiler_params=params,
        name="push_second_pull_first",
    )(table, grown, labels, from_left, from_mid, from_right, part, half, blocks)

    back_left = across(to_right, -1, XB[0])
    back_right = across(to_left, 1, XB[1])
    back_mid = across(to_mid, 0, XB[2])

    parts = [part]
    bit = 1
    while bit < cell_count:
        if bit > 1:
            total, top = combined(parts)
            parts = [jnp.concatenate([total, top], axis=0)]
        masks = [bit] if 2 * bit >= cell_count else [bit, 2 * bit, 3 * bit]
        parts = [parts[0]] + [flipped(parts[0], mask) for mask in masks]
        bit *= 4

    swap_left = across(back_left, 0, XC)
    swap_right = across(back_right, 0, XC)

    fate = pl.pallas_call(
        functools.partial(third_kernel, own),
        out_shape=bf16(1, height, cells),
        in_specs=[hbm] + [vmem] * 5,
        out_specs=vmem,
        scratch_shapes=[
            table_scratch, pltpu.VMEM((window * side, side), jnp.bfloat16), pltpu.VMEM((inner, side), jnp.float32), sem,
        ],
        compiler_params=params,
        name="pull_second",
    )(table, back_left, back_mid, back_right, to_mid, blocks)

    forward_mass = pl.pallas_call(
        functools.partial(last_kernel, own, float(cells * cell_count), len(parts)),
        out_shape=bf16(1, height, cells),
        in_specs=[vmem] * (len(parts) + 6),
        out_specs=vmem,
        compiler_params=params,
        name="normalise",
    )(*parts, part, keep_first, back_mid, keep_second, swap_left, swap_right)
    return forward_mass, fate


def solution(mesh):
    placed = (
        P("tm", "cell"),
        P("tm", "cell"),
        P("tm", "cell", None, None),
        P("tm", "cell"),
        P(None, "cell"),
        P(None, "cell"),
    )
    return jax.shard_map(
        on_device,
        mesh=mesh,
        in_specs=placed,
        out_specs=(P("tm", None, "cell"), P("tm", None, "cell")),
        check_vma=False,
    )
```

time: 52.9 us -> 35.9 us (0.68)
  starting transfers between devices: 29 us -> 23.4 us
  local copies, waits for them, and re-layouts: 5.02 us -> 0 us
  waiting for transfers between devices: 9.26 us -> 5.2 us
  Pallas kernels: 8.37 us -> 6.41 us
    ppermute x8, starting transfers between devices: 19.9 us -> 13.6 us  [across(): return lax.ppermute(array, ('tm', 'cell'), route)]
    unnamed x16 -> x0, local copies, waits for them, and re-layouts: 5.02 us -> none
    ppermute x6, waiting for transfers between devices: 8.25 us -> 3.29 us  [flipped(): lax.ppermute(array, 'cell', [(c, c ^ bits) for c in range(lax.axis_size('...]
    pallas_call x1, Pallas kernels: 4.04 us -> 1.98 us  [on_device(): pl.pallas_call(functools.partial(third_kernel, own), out_shape=bf16(1, he...]
    ppermute x8, waiting for transfers between devices: 1 us -> 1.91 us  [across(): return lax.ppermute(array, ('tm', 'cell'), route)]
    pallas_call x1, Pallas kernels: 2.9 us -> 3.62 us  [on_device(): pl.pallas_call(functools.partial(first_kernel, own), out_shape=(bf16(reac...]
    ppermute x6, starting transfers between devices: 9.14 us -> 9.76 us  [flipped(): lax.ppermute(array, 'cell', [(c, c ^ bits) for c in range(lax.axis_size('...]
    pallas_call x1, Pallas kernels: 0.64 us -> 0.01 us  [on_device(): pl.pallas_call(functools.partial(second_kernel, own), out_shape=(bf16(inn...]
  transfers between devices with their start and end apart: 14 -> 14, of which waited for: 3 -> 4; matrix products, arithmetic and copies ran while one was open for 0% -> 0% of each run, Pallas kernels for 8% -> 6%
where the time goes in v2:
time: 35.9 us; the launch traced here: 35.7 us
  starting transfers between devices  23.4 us (65%)
  Pallas kernels  6.41 us (18%)
  waiting for transfers between devices  5.2 us (14%)
  between operations  0.73 us (2%)
    ppermute x8, starting transfers between devices, across(): return lax.ppermute(array, ('tm', 'cell'), route)  13.6 us
    ppermute x6, starting transfers between devices, flipped(): lax.ppermute(array, 'cell', [(c, c ^ bits) for c in range(lax.axis_size('...  9.76 us
    pallas_call x1, Pallas kernels, on_device(): pl.pallas_call(functools.partial(first_kernel, own), out_shape=(bf16(reac...  3.62 us
    ppermute x6, waiting for transfers between devices, flipped(): lax.ppermute(array, 'cell', [(c, c ^ bits) for c in range(lax.axis_size('...  3.29 us
    pallas_call x1, Pallas kernels, on_device(): pl.pallas_call(functools.partial(third_kernel, own), out_shape=bf16(1, he...  1.98 us
    ppermute x8, waiting for transfers between devices, across(): return lax.ppermute(array, ('tm', 'cell'), route)  1.91 us
    pallas_call x1, Pallas kernels, on_device(): pl.pallas_call(functools.partial(last_kernel, own, float(cells * cell_cou...  0.81 us
  transfers between devices with their start and end apart: 14, of which 4 were waited for; matrix products, arithmetic and copies ran while one was open for 0% of the time, Pallas kernels for 6%

profile of v2, /device:TPU:0, one launch (start us, length us, event | category | flops | bytes accessed | tf_op | source)
XLA Modules:
  0.0 35.7 jit_solution(12664276485775835803)
XLA Ops:
  0.6 3.6 %push_first.1 = (bf16[576,128]{1,0:T(8,128)(2,1)S(1)}, bf16[512,128]{1,0:T(8,128)(2,1)S(1)}, bf16[576,128]{1,0:T(8,128)(2,1)S(1)}, f32[512,128]{1,0:T(8,128)S(1)...) custom-call(s32[1,64]{1,0:T(1,128)} %rows_hbm.1, ...), custom_call_target="tpu_custom_call" | custom-call | tf_op jit(solution)/shard_map/push_first/pallas_call | solution.py:310
  4.3 2.7 %collective-permute-start = (bf16[576,128]{1,0:T(8,128)(2,1)S(1)}, bf16[576,128]{1,0:T(8,128)(2,1)S(1)}, u32[]{:S(2)}, u32[]{:S(2)}) collective-permute-start(bf16[576,128]{1,0:T(8,128)(2,1)S(1)} %get-tuple-element.20), channel_id=1, source_target_pairs={{0,17},{1,18},{2,19},{3,20},{4,21},{5,22},{6,23},{7,24},{8,25},{9,... | collective-permute-start | bytes 442376 | tf_op jit(solution)/shard_map/ppermute | solution.py:283
  7.0 0.7 %collective-permute-start.2 = (bf16[576,128]{1,0:T(8,128)(2,1)S(1)}, bf16[576,128]{1,0:T(8,128)(2,1)S(1)}, u32[]{:S(2)}, u32[]{:S(2)}) collective-permute-start(bf16[576,128]{1,0:T(8,128)(2,1)S(1)} %get-tuple-element.22), channel_id=1, source_target_pairs={{1,16},{2,17},{3,18},{4,19},{5,20},{6,21},{7,22},{8,23},{9,24},{10... | collective-permute-start | bytes 442376 | tf_op jit(solution)/shard_map/ppermute | solution.py:283
  7.7 0.1 collective-permute-start.1
  7.7 1.3 %collective-permute-done.1.mid_ref = bf16[512,128]{1,0:T(8,128)(2,1)S(1)} collective-permute-done((bf16[512,128]{1,0:T(8,128)(2,1)S(1)}, bf16[512,128]{1,0:T(8,128)(2,1)S(1)}, u32[]{:S(2)}, u32[]{:S(2)}) %collective-permute-start.1) | collective-permute-done | bytes 131104 | tf_op jit(solution)/shard_map/ppermute | solution.py:283
  9.1 0.6 %collective-permute-done.left_ref = bf16[576,128]{1,0:T(8,128)(2,1)S(1)} collective-permute-done((bf16[576,128]{1,0:T(8,128)(2,1)S(1)}, bf16[576,128]{1,0:T(8,128)(2,1)S(1)}, u32[]{:S(2)}, u32[]{:S(2)}) %collective-permute-start) | collective-permute-done | bytes 147488 | tf_op jit(solution)/shard_map/ppermute | solution.py:283
  9.6 0.0 collective-permute-done.2.right_ref
  9.7 0.7 %collective-permute-start.10 = (bf16[1040,128]{1,0:T(8,128)(2,1)S(1)}, bf16[1040,128]{1,0:T(8,128)(2,1)S(1)}, u32[]{:S(2)}, u32[]{:S(2)}) collective-permute-start(bf16[1040,128]{1,0:T(8,128)(2,1)S(1)} %get-tuple-element.30), channel_id=1, source_target_pairs={{16,1},{17,2},{18,3},{19,4},{20,5},{21,6},{22,7},{23,8},{24,9},{25... | collective-permute-start | bytes 798728 | tf_op jit(solution)/shard_map/ppermute | solution.py:283
  10.3 1.3 %collective-permute-start.12 = (bf16[1040,128]{1,0:T(8,128)(2,1)S(1)}, bf16[1040,128]{1,0:T(8,128)(2,1)S(1)}, u32[]{:S(2)}, u32[]{:S(2)}) collective-permute-start(bf16[1040,128]{1,0:T(8,128)(2,1)S(1)} %get-tuple-element.31), channel_id=1, source_target_pairs={{17,0},{18,1},{19,2},{20,3},{21,4},{22,5},{23,6},{24,7},{25,8},{26... | collective-permute-start | bytes 798728 | tf_op jit(solution)/shard_map/ppermute | solution.py:283
  11.6 3.8 %collective-permute-start.3 = (f32[16,128]{1,0:T(8,128)S(1)}, f32[16,128]{1,0:T(8,128)S(1)}, u32[]{:S(2)}, u32[]{:S(2)}) collective-permute-start(f32[16,128]{1,0:T(8,128)S(1)} %get-tuple-element.26.refs_4_), channel_id=1, source_target_pairs={{0,1},{1,0},{2,3},{3,2},{4,5},{5,4},{6,7},{7,6},{8,9},{9,8},{10,11... | collective-permute-start | bytes 24584 | tf_op jit(solution)/shard_map/ppermute | solution.py:287
  15.4 1.3 %collective-permute-start.4 = (f32[16,128]{1,0:T(8,128)S(1)}, f32[16,128]{1,0:T(8,128)S(1)}, u32[]{:S(2)}, u32[]{:S(2)}) collective-permute-start(f32[16,128]{1,0:T(8,128)S(1)} %get-tuple-element.26.refs_4_), channel_id=1, source_target_pairs={{0,2},{1,3},{2,0},{3,1},{4,6},{5,7},{6,4},{7,5},{8,10},{9,11},{10,... | collective-permute-start | bytes 24584 | tf_op jit(solution)/shard_map/ppermute | solution.py:287
  16.7 0.3 collective-permute-start.5
  16.9 0.1 collective-permute-done.3
  17.0 7.7 %collective-permute-start.9 = (bf16[1024,128]{1,0:T(8,128)(2,1)S(1)}, bf16[1024,128]{1,0:T(8,128)(2,1)S(1)}, u32[]{:S(2)}, u32[]{:S(2)}) collective-permute-start(bf16[1024,128]{1,0:T(8,128)(2,1)S(1)} %get-tuple-element.28.mine_ref), channel_id=1, source_target_pairs={{0,16},{16,0},{1,17},{17,1},{2,18},{18,2},{3,19},{19,3},{4,20},{20... | collective-permute-start | bytes 786440 | tf_op jit(solution)/shard_map/ppermute | solution.py:283
  24.7 0.0 collective-permute-done.10.left_ref
  24.7 0.0 collective-permute-start.11
  24.7 0.5 %collective-permute-start.13 = (bf16[1040,128]{1,0:T(8,128)(2,1)S(1)}, bf16[1040,128]{1,0:T(8,128)(2,1)S(1)}, u32[]{:S(2)}, u32[]{:S(2)}) collective-permute-start(bf16[1040,128]{1,0:T(8,128)(2,1)S(1)} %collective-permute-done.12.right_ref), channel_id=1, source_target_pairs={{0,16},{16,0},{1,17},{17,1},{2,18},{18,2},{3,19},{19,3},{4,20},{20... | collective-permute-start | bytes 798728 | tf_op jit(solution)/shard_map/ppermute | solution.py:283
  25.2 0.0 collective-permute-done.4
  25.3 1.6 %collective-permute-start.6 = (f32[16,128]{1,0:T(8,128)S(1)}, f32[16,128]{1,0:T(8,128)S(1)}, u32[]{:S(2)}, u32[]{:S(2)}) collective-permute-start(f32[16,128]{1,0:T(8,128)S(1)} %pad_maximum_fusion.refs_0_), channel_id=1, source_target_pairs={{0,4},{1,5},{2,6},{3,7},{4,0},{5,1},{6,2},{7,3},{8,12},{9,13},{10,... | collective-permute-start | bytes 24584 | tf_op jit(solution)/shard_map/ppermute | solution.py:287
  26.9 2.6 %collective-permute-start.7 = (f32[16,128]{1,0:T(8,128)S(1)}, f32[16,128]{1,0:T(8,128)S(1)}, u32[]{:S(2)}, u32[]{:S(2)}) collective-permute-start(f32[16,128]{1,0:T(8,128)S(1)} %pad_maximum_fusion.refs_0_), channel_id=1, source_target_pairs={{0,8},{1,9},{2,10},{3,11},{4,12},{5,13},{6,14},{7,15},{8,0},{9,1},... | collective-permute-start | bytes 24584 | tf_op jit(solution)/shard_map/ppermute | solution.py:287
  29.5 0.3 collective-permute-start.8
  29.7 2.0 %pull_second.1 = bf16[1,128,512]{2,1,0:T(8,128)(2,1)} custom-call(s32[2,64]{1,0:T(2,128)S(1)} %get-tuple-element.17.table_hbm, bf16[1040,128]{1,0:T(8,128)(2,1)S(1)} %collective-permute-done.10.left_ref, bf16[1024,128]{1,0:T(8,128)(2,1)S(1)} %collective-permute-done.9.refs_6_.mid_ref, bf16[1040,128]{1,0:T(8,128)(2,1)S(1)} %collective-permute-done.12.right_ref, ...), custom_call_target="tpu_custom_call" | custom-call | tf_op jit(solution)/shard_map/pull_second/pallas_call | solution.py:367
  31.7 3.2 %collective-permute-done.8.refs_3_ = f32[16,128]{1,0:T(8,128)S(1)} collective-permute-done((f32[16,128]{1,0:T(8,128)S(1)}, f32[16,128]{1,0:T(8,128)S(1)}, u32[]{:S(2)}, u32[]{:S(2)}) %collective-permute-start.8) | collective-permute-done | bytes 8224 | tf_op jit(solution)/shard_map/ppermute | solution.py:287
  34.9 0.8 %normalise.1 = bf16[1,128,512]{2,1,0:T(8,128)(2,1)} custom-call(f32[16,128]{1,0:T(8,128)S(1)} %pad_maximum_fusion.refs_0_, f32[16,128]{1,0:T(8,128)S(1)} %collective-permute-done.6.refs_1_, f32[16,128]{1,0:T(8,128)S(1)} %collective-permute-done.7.refs_2_, f32[16,128]{1,0:T(8,128)S(1)} %collective-permute-done.8.refs_3_, ...), custom_call_target="tpu_custom_call" | custom-call | tf_op jit(solution)/shard_map/normalise/pallas_call | solution.py:379
  (10 shorter events, 0.0 us)
Async XLA Ops:
  4.3 5.4 %collective-permute-start = (bf16[576,128]{1,0:T(8,128)(2,1)S(1)}, bf16[576,128]{1,0:T(8,128)(2,1)S(1)}, u32[]{:S(2)}, u32[]{:S(2)}) collective-permute-start(bf16[576,128]{1,0:T(8,128)(2,1)S(1)} %get-tuple-element.20), channel_id=1, source_target_pairs={{0,17},{1,18},{2,19},{3,20},{4,21},{5,22},{6,23},{7,24},{8,25},{9,... | collective-permute-start | bytes 442376 | tf_op jit(solution)/shard_map/ppermute | solution.py:283
  7.0 2.7 %collective-permute-start.2 = (bf16[576,128]{1,0:T(8,128)(2,1)S(1)}, bf16[576,128]{1,0:T(8,128)(2,1)S(1)}, u32[]{:S(2)}, u32[]{:S(2)}) collective-permute-start(bf16[576,128]{1,0:T(8,128)(2,1)S(1)} %get-tuple-element.22), channel_id=1, source_target_pairs={{1,16},{2,17},{3,18},{4,19},{5,20},{6,21},{7,22},{8,23},{9,24},{10... | collective-permute-start | bytes 442376 | tf_op jit(solution)/shard_map/ppermute | solution.py:283
  7.7 1.4 %collective-permute-start.1 = (bf16[512,128]{1,0:T(8,128)(2,1)S(1)}, bf16[512,128]{1,0:T(8,128)(2,1)S(1)}, u32[]{:S(2)}, u32[]{:S(2)}) collective-permute-start(bf16[512,128]{1,0:T(8,128)(2,1)S(1)} %get-tuple-element.21), channel_id=1, source_target_pairs={{0,16},{16,0},{1,17},{17,1},{2,18},{18,2},{3,19},{19,3},{4,20},{20... | collective-permute-start | bytes 393224 | tf_op jit(solution)/shard_map/ppermute | solution.py:283
  9.7 15.1 %collective-permute-start.10 = (bf16[1040,128]{1,0:T(8,128)(2,1)S(1)}, bf16[1040,128]{1,0:T(8,128)(2,1)S(1)}, u32[]{:S(2)}, u32[]{:S(2)}) collective-permute-start(bf16[1040,128]{1,0:T(8,128)(2,1)S(1)} %get-tuple-element.30), channel_id=1, source_target_pairs={{16,1},{17,2},{18,3},{19,4},{20,5},{21,6},{22,7},{23,8},{24,9},{25... | collective-permute-start | bytes 798728 | tf_op jit(solution)/shard_map/ppermute | solution.py:283
  10.3 14.4 %collective-permute-start.12 = (bf16[1040,128]{1,0:T(8,128)(2,1)S(1)}, bf16[1040,128]{1,0:T(8,128)(2,1)S(1)}, u32[]{:S(2)}, u32[]{:S(2)}) collective-permute-start(bf16[1040,128]{1,0:T(8,128)(2,1)S(1)} %get-tuple-element.31), channel_id=1, source_target_pairs={{17,0},{18,1},{19,2},{20,3},{21,4},{22,5},{23,6},{24,7},{25,8},{26... | collective-permute-start | bytes 798728 | tf_op jit(solution)/shard_map/ppermute | solution.py:283
  11.6 5.4 %collective-permute-start.3 = (f32[16,128]{1,0:T(8,128)S(1)}, f32[16,128]{1,0:T(8,128)S(1)}, u32[]{:S(2)}, u32[]{:S(2)}) collective-permute-start(f32[16,128]{1,0:T(8,128)S(1)} %get-tuple-element.26.refs_4_), channel_id=1, source_target_pairs={{0,1},{1,0},{2,3},{3,2},{4,5},{5,4},{6,7},{7,6},{8,9},{9,8},{10,11... | collective-permute-start | bytes 24584 | tf_op jit(solution)/shard_map/ppermute | solution.py:287
  15.4 9.8 %collective-permute-start.4 = (f32[16,128]{1,0:T(8,128)S(1)}, f32[16,128]{1,0:T(8,128)S(1)}, u32[]{:S(2)}, u32[]{:S(2)}) collective-permute-start(f32[16,128]{1,0:T(8,128)S(1)} %get-tuple-element.26.refs_4_), channel_id=1, source_target_pairs={{0,2},{1,3},{2,0},{3,1},{4,6},{5,7},{6,4},{7,5},{8,10},{9,11},{10,... | collective-permute-start | bytes 24584 | tf_op jit(solution)/shard_map/ppermute | solution.py:287
  16.7 8.6 %collective-permute-start.5 = (f32[16,128]{1,0:T(8,128)S(1)}, f32[16,128]{1,0:T(8,128)S(1)}, u32[]{:S(2)}, u32[]{:S(2)}) collective-permute-start(f32[16,128]{1,0:T(8,128)S(1)} %get-tuple-element.26.refs_4_), channel_id=1, source_target_pairs={{0,3},{1,2},{2,1},{3,0},{4,7},{5,6},{6,5},{7,4},{8,11},{9,10},{10,... | collective-permute-start | bytes 24584 | tf_op jit(solution)/shard_map/ppermute | solution.py:287
  17.0 12.4 %collective-permute-start.9 = (bf16[1024,128]{1,0:T(8,128)(2,1)S(1)}, bf16[1024,128]{1,0:T(8,128)(2,1)S(1)}, u32[]{:S(2)}, u32[]{:S(2)}) collective-permute-start(bf16[1024,128]{1,0:T(8,128)(2,1)S(1)} %get-tuple-element.28.mine_ref), channel_id=1, source_target_pairs={{0,16},{16,0},{1,17},{17,1},{2,18},{18,2},{3,19},{19,3},{4,20},{20... | collective-permute-start | bytes 786440 | tf_op jit(solution)/shard_map/ppermute | solution.py:283
  24.7 10.2 %collective-permute-start.11 = (bf16[1040,128]{1,0:T(8,128)(2,1)S(1)}, bf16[1040,128]{1,0:T(8,128)(2,1)S(1)}, u32[]{:S(2)}, u32[]{:S(2)}) collective-permute-start(bf16[1040,128]{1,0:T(8,128)(2,1)S(1)} %collective-permute-done.10.left_ref), channel_id=1, source_target_pairs={{0,16},{16,0},{1,17},{17,1},{2,18},{18,2},{3,19},{19,3},{4,20},{20... | collective-permute-start | bytes 798728 | tf_op jit(solution)/shard_map/ppermute | solution.py:283
  24.7 10.2 %collective-permute-start.13 = (bf16[1040,128]{1,0:T(8,128)(2,1)S(1)}, bf16[1040,128]{1,0:T(8,128)(2,1)S(1)}, u32[]{:S(2)}, u32[]{:S(2)}) collective-permute-start(bf16[1040,128]{1,0:T(8,128)(2,1)S(1)} %collective-permute-done.12.right_ref), channel_id=1, source_target_pairs={{0,16},{16,0},{1,17},{17,1},{2,18},{18,2},{3,19},{19,3},{4,20},{20... | collective-permute-start | bytes 798728 | tf_op jit(solution)/shard_map/ppermute | solution.py:283
  25.3 6.4 %collective-permute-start.6 = (f32[16,128]{1,0:T(8,128)S(1)}, f32[16,128]{1,0:T(8,128)S(1)}, u32[]{:S(2)}, u32[]{:S(2)}) collective-permute-start(f32[16,128]{1,0:T(8,128)S(1)} %pad_maximum_fusion.refs_0_), channel_id=1, source_target_pairs={{0,4},{1,5},{2,6},{3,7},{4,0},{5,1},{6,2},{7,3},{8,12},{9,13},{10,... | collective-permute-start | bytes 24584 | tf_op jit(solution)/shard_map/ppermute | solution.py:287
  26.9 4.8 %collective-permute-start.7 = (f32[16,128]{1,0:T(8,128)S(1)}, f32[16,128]{1,0:T(8,128)S(1)}, u32[]{:S(2)}, u32[]{:S(2)}) collective-permute-start(f32[16,128]{1,0:T(8,128)S(1)} %pad_maximum_fusion.refs_0_), channel_id=1, source_target_pairs={{0,8},{1,9},{2,10},{3,11},{4,12},{5,13},{6,14},{7,15},{8,0},{9,1},... | collective-permute-start | bytes 24584 | tf_op jit(solution)/shard_map/ppermute | solution.py:287
  29.5 5.4 %collective-permute-start.8 = (f32[16,128]{1,0:T(8,128)S(1)}, f32[16,128]{1,0:T(8,128)S(1)}, u32[]{:S(2)}, u32[]{:S(2)}) collective-permute-start(f32[16,128]{1,0:T(8,128)S(1)} %pad_maximum_fusion.refs_0_), channel_id=1, source_target_pairs={{0,12},{1,13},{2,14},{3,15},{4,8},{5,9},{6,10},{7,11},{8,4},{9,5},... | collective-permute-start | bytes 24584 | tf_op jit(solution)/shard_map/ppermute | solution.py:287

commit v3 on v2

--- a/solution.py
+++ b/solution.py
@@ -9,10 +9,10 @@
 CELL_TYPES = 16
 BAND_REACH = 4
 LABEL_ROWS = 16
-CHUNKS = 8
-XA = ((0,), (0,), (0,1))
-XB = ((1,), (1,), (0,1))
-XC = (0,1)
+CHUNKS = 2
+XA = ("inc", "chain", "full")
+XB = ("inc", "chain", "full")
+XC = "full"
 
 
 def rows_of(block, side):
@@ -54,21 +54,13 @@
     return (grouped * scale).reshape(height, cells).astype(jnp.bfloat16)
 
 
-def first_kernel(own, rows_hbm, cols_hbm, growth_hbm, first_hbm, last_hbm, blocks_hbm,
-                 left_ref, mid_ref, right_ref, keep_ref, part_ref, half_ref, table_hbm, growth, labels, blk,
-                 rows, cols, src, acc, count, table, small_sems, sems):
-    side = blk.shape[1]
-    slots = blk.shape[0]
-    first_row = lax.axis_index("cell") * own
-    first_col = first_row - BAND_REACH
-    on_first = lax.axis_index("tm") == 0
-    chunk = slots // CHUNKS
+def load(own, rows_hbm, cols_hbm, growth_hbm, last_hbm, blocks_hbm, growth, known, blk, rows, cols, small_sems, sems):
+    chunk = blk.shape[0] // CHUNKS
     small = [
         pltpu.make_async_copy(rows_hbm, rows, small_sems.at[0]),
         pltpu.make_async_copy(cols_hbm, cols, small_sems.at[1]),
         pltpu.make_async_copy(growth_hbm, growth, small_sems.at[2]),
-        pltpu.make_async_copy(first_hbm, labels.at[0], small_sems.at[3]),
-        pltpu.make_async_copy(last_hbm, labels.at[1], small_sems.at[4]),
+        pltpu.make_async_copy(last_hbm, known, small_sems.at[3]),
     ]
     copies = [
         pltpu.make_async_copy(blocks_hbm.at[0, pl.ds(i * chunk, chunk)], blk.at[pl.ds(i * chunk, chunk)], sems.at[i])
@@ -76,8 +68,11 @@
     ]
     for copy in small + copies:
         copy.start()
-    small[0].wait()
-    small[1].wait()
+    return small, copies
+
+
+def sort_slots(own, rows, cols, count, table, first_row):
+    slots = table.shape[1]
     for row in range(own):
         count[row] = row * (slots // own)
     for n in range(slots):
@@ -85,35 +80,51 @@
         place = count[row]
         count[row] = place + 1
         table[0, place] = n
-        table[1, place] = cols[0, n] - first_col
-    table_copy = pltpu.make_async_copy(table, table_hbm, small_sems.at[5])
-    table_copy.start()
-    for copy in small[2:]:
-        copy.wait()
-
-    @pl.when(on_first)
-    def _():
+        table[1, place] = cols[0, n] - first_row + BAND_REACH
+
+
+def first_kernel(own, rows_hbm, cols_hbm, growth_hbm, first_hbm, last_hbm, blocks_hbm,
+                 left_ref, mid_ref, right_ref, keep_ref, part_ref, table_ref, growth, known, blk,
+                 rows, cols, labels, src, acc, count, table, small_sems, sems):
+    side = blk.shape[1]
+    slots = blk.shape[0]
+    first_row = lax.axis_index("cell") * own
+    reach, inner = BAND_REACH * side, own * side
+
+    @pl.when(lax.axis_index("tm") == 0)
+    def _():
+        labels_copy = pltpu.make_async_copy(first_hbm, labels, small_sems.at[5])
+        labels_copy.start()
+        small, copies = load(
+            own, rows_hbm, cols_hbm, growth_hbm, last_hbm, blocks_hbm, growth, known, blk, rows, cols, small_sems, sems
+        )
+        small[0].wait()
+        small[1].wait()
+        sort_slots(own, rows, cols, count, table, first_row)
+        table_copy = pltpu.make_async_copy(table, table_ref, small_sems.at[4])
+        table_copy.start()
+        small[2].wait()
+        small[3].wait()
+        labels_copy.wait()
         for b in range(own):
             cells = pl.ds(b * side, side)
             inverse = 1.0 / growth[0:1, cells]
-            hot = one_hot(labels[0, :, cells])
+            hot = one_hot(labels[:, cells])
             src[pl.ds(b * side, side), :] = jnp.where(hot, inverse, 0.0).astype(jnp.bfloat16)
         acc[...] = jnp.zeros_like(acc)
         for n in range(slots):
-            if n % chunk == 0:
-                copies[n // chunk].wait()
+            if n % (slots // CHUNKS) == 0:
+                copies[n // (slots // CHUNKS)].wait()
             row = rows_of(rows[0, n] - first_row, side)
-            col = rows_of(cols[0, n] - first_col, side)
+            col = rows_of(cols[0, n] - first_row + BAND_REACH, side)
             acc[col, :] += jnp.dot(src[row, :], blk[n], preferred_element_type=jnp.float32)
-        reach = BAND_REACH * side
-        inner = own * side
         left_ref[0:reach, :] = acc[0:reach, :].astype(jnp.bfloat16)
         mid_ref[...] = acc[reach : reach + inner, :].astype(jnp.bfloat16)
         right_ref[0:reach, :] = acc[reach + inner :, :].astype(jnp.bfloat16)
         keep_ref[...] = acc[reach : reach + inner, :]
         for b in range(own):
-            known = labels[1, :, pl.ds(b * side, side)].astype(jnp.float32).astype(jnp.bfloat16)
-            tall = jnp.concatenate([known, known], axis=0)
+            exact = known[:, pl.ds(b * side, side)].astype(jnp.float32).astype(jnp.bfloat16)
+            tall = jnp.concatenate([exact, exact], axis=0)
             left_ref[pl.ds(reach + b * LABEL_ROWS, LABEL_ROWS), :] = tall
             right_ref[pl.ds(reach + b * LABEL_ROWS, LABEL_ROWS), :] = tall
         total = acc[0:side, :]
@@ -122,22 +133,40 @@
         sums = jnp.sum(jnp.transpose(total), axis=0, keepdims=True)
         part_ref[0:8, :] = jnp.broadcast_to(sums, (8, side))
         part_ref[8:16, :] = jnp.zeros((8, side), jnp.float32)
-
-    @pl.when(jnp.logical_not(on_first))
-    def _():
+        table_copy.wait()
+
+
+def prepare_kernel(own, rows_hbm, cols_hbm, growth_hbm, last_hbm, blocks_hbm, table_in, growth_in, known_in, blk_in,
+                   table_ref, growth, known, blk, half_ref, rows, cols, count, table, small_sems, sems):
+    side = blk.shape[1]
+    slots = blk.shape[0]
+    first_row = lax.axis_index("cell") * own
+
+    @pl.when(lax.axis_index("tm") != 0)
+    def _():
+        small, copies = load(
+            own, rows_hbm, cols_hbm, growth_hbm, last_hbm, blocks_hbm, growth, known, blk, rows, cols, small_sems, sems
+        )
+        small[0].wait()
+        small[1].wait()
+        sort_slots(own, rows, cols, count, table, first_row)
+        table_copy = pltpu.make_async_copy(table, table_ref, small_sems.at[4])
+        table_copy.start()
+        small[2].wait()
+        small[3].wait()
         for copy in copies:
             copy.wait()
-        largest = blk[0].astype(jnp.float32)
+        largest = blk[0]
         for n in range(1, slots):
-            largest = jnp.maximum(largest, blk[n].astype(jnp.float32))
+            largest = jnp.maximum(largest, blk[n])
+        largest = largest.astype(jnp.float32)
         top = jnp.max(jnp.max(largest, axis=0, keepdims=True), axis=1, keepdims=True)
-        half = jnp.round(0.5 * jnp.log2(jnp.maximum(top, 2.0**-126)))
-        half_ref[...] = jnp.broadcast_to(half, half_ref.shape)
-
-    table_copy.wait()
-
-
-def second_kernel(own, table_hbm, growth_ref, labels_ref, left_ref, mid_ref, right_ref, part_in, half_ref, blk,
+        power = jnp.round(jnp.log2(jnp.clip(top, 2.0**-126, 2.0**126)))
+        half_ref[...] = jnp.broadcast_to(jnp.round(0.5 * power), half_ref.shape)
+        table_copy.wait()
+
+
+def second_kernel(own, table_ref, growth_ref, known_ref, left_ref, mid_ref, right_ref, part_in, half_ref, blk,
                   to_left, to_mid, to_right, keep_ref, part_ref, table, src, acc, fated, pulled, sem):
     side = blk.shape[1]
     slots = blk.shape[0]
@@ -150,7 +179,7 @@
 
     @pl.when(lax.axis_index("tm") != 0)
     def _():
-        table_copy = pltpu.make_async_copy(table_hbm, table, sem)
+        table_copy = pltpu.make_async_copy(table_ref, table, sem)
         table_copy.start()
         has_left, has_right = here > 0, here < lax.axis_size("cell") - 1
         mass = []
@@ -189,13 +218,13 @@
         part_ref[0:8, :] = jnp.broadcast_to(sums, (8, side))
         part_ref[8:16, :] = power_row
 
-        panels = labels_ref.shape[1]
+        panels = known_ref.shape[0]
         for w in range(own + 2 * BAND_REACH):
             if w < BAND_REACH:
                 rows = pl.ds(reach + w * LABEL_ROWS, LABEL_ROWS)
                 labels = left_ref[rows, :][0:panels].astype(jnp.float32).astype(jnp.int32)
             elif w < BAND_REACH + own:
-                labels = labels_ref[1, :, pl.ds((w - BAND_REACH) * side, side)]
+                labels = known_ref[:, pl.ds((w - BAND_REACH) * side, side)]
             else:
                 rows = pl.ds(reach + (w - BAND_REACH - own) * LABEL_ROWS, LABEL_ROWS)
                 labels = right_ref[rows, :][0:panels].astype(jnp.float32).astype(jnp.int32)
@@ -209,13 +238,13 @@
             to_right[at, :] = fates
 
 
-def third_kernel(own, table_hbm, left_ref, mid_ref, right_ref, mine_ref, blk, fate_ref, table, fated, pulled, sem):
+def third_kernel(own, table_ref, left_ref, mid_ref, right_ref, mine_ref, blk, fate_ref, table, fated, pulled, sem):
     side = blk.shape[1]
     reach, inner = BAND_REACH * side, own * side
 
     @pl.when(lax.axis_index("tm") == 0)
     def _():
-        table_copy = pltpu.make_async_copy(table_hbm, table, sem)
+        table_copy = pltpu.make_async_copy(table_ref, table, sem)
         table_copy.start()
         fated[0:reach, :] = left_ref[0:reach, :]
         fated[reach : reach + inner, :] = mid_ref[0:inner, :]
@@ -239,13 +268,18 @@
     return total, top
 
 
-def last_kernel(own, all_cells, count, *refs):
-    part_refs = refs[:count]
-    own_part, keep_first, halo_first, keep_second, left_ref, right_ref, mass_ref = refs[count:]
+def combine_kernel(count, *refs):
+    total, top = combined([part[...] for part in refs[:count]])
+    out = refs[count + 2]
+    out[0:8, :] = total
+    out[8:16, :] = top
+
+
+def last_kernel(own, all_cells, whole, own_part, keep_first, halo_first, keep_second, left_ref, right_ref, mass_ref):
     side = keep_first.shape[1]
     reach, inner = BAND_REACH * side, own * side
     here = lax.axis_index("cell")
-    total, top = combined([part[...] for part in part_refs])
+    total, top = whole[0:8, :], whole[8:16, :]
     scale = all_cells / as_column(total[0:1], side)
 
     @pl.when(lax.axis_index("tm") == 0)
@@ -271,16 +305,20 @@
             mass_ref[0, :, at] = (mass * scale).astype(jnp.bfloat16)
 
 
-def across(array, distance, ways=(0, 1)):
+def across(array, distance, sender, mode):
     count = lax.axis_size("cell")
-    route = []
-    for c in range(count):
-        there, back = c + distance, c - distance
-        if 0 in ways and (0 <= there < count or len(ways) == 2):
-            route.append((c, count + there if 0 <= there < count else c))
-        if 1 in ways and (0 <= back < count or len(ways) == 2):
-            route.append((count + c, back if 0 <= back < count else count + c))
-    return lax.ppermute(array, ("tm", "cell"), route)
+    at = lambda core, c: core * count + c
+    other = 1 - sender
+    route = {at(sender, c): at(other, c + distance) for c in range(count) if 0 <= c + distance < count}
+    if mode == "full":
+        for c in range(count):
+            route[at(other, c)] = at(sender, c - distance) if 0 <= c - distance < count else at(other, c)
+            route.setdefault(at(sender, c), at(sender, c))
+    if mode == "chain":
+        for c in range(count):
+            route[at(other, c)] = at(sender, c)
+            route.setdefault(at(sender, c), at(other, (c + distance) % count))
+    return lax.ppermute(array, ("tm", "cell"), list(route.items()))
 
 
 def flipped(array, bits):
@@ -298,38 +336,51 @@
     window = own + 2 * BAND_REACH
     reach, inner = BAND_REACH * side, own * side
 
-    smem = pl.BlockSpec(memory_space=pltpu.SMEM)
     vmem = pl.BlockSpec(memory_space=pltpu.VMEM)
     hbm = pl.BlockSpec(memory_space=pltpu.HBM)
+    anywhere = pl.BlockSpec(memory_space=pl.ANY)
     bf16 = lambda *shape: jax.ShapeDtypeStruct(shape, jnp.bfloat16)
     f32 = lambda *shape: jax.ShapeDtypeStruct(shape, jnp.float32)
+    i32 = lambda *shape: jax.ShapeDtypeStruct(shape, jnp.int32)
     params = pltpu.CompilerParams(vmem_limit_bytes=16 * 1024 * 1024)
-    table_scratch = pltpu.SMEM((2, slots), jnp.int32)
     sem = pltpu.SemaphoreType.DMA
-
-    left, mid, right, keep_first, part, half, table, grown, labels, blocks = pl.pallas_call(
+    slot_scratch = [pltpu.SMEM((1, slots), jnp.int32), pltpu.SMEM((1, slots), jnp.int32)]
+    sort_scratch = [pltpu.SMEM((own,), jnp.int32), pltpu.SMEM((2, slots), jnp.int32)]
+    loaded = (i32(2, slots), f32(1, cells), i32(panels, cells), bf16(slots, side, side))
+    inputs = [pltpu.with_memory_space_constraint(array, pltpu.HBM) for array in (
+        block_rows, block_cols, growth, first_labels, last_labels, block_values
+    )]
+
+    left, mid, right, keep_first, part, *loads = pl.pallas_call(
         functools.partial(first_kernel, own),
         out_shape=(
-            bf16(reach + own * LABEL_ROWS, side), bf16(inner, side), bf16(reach + own * LABEL_ROWS, side),
-            f32(inner, side), f32(16, side), f32(8, side), jax.ShapeDtypeStruct((2, slots), jnp.int32),
-            f32(1, cells), jax.ShapeDtypeStruct((2, panels, cells), jnp.int32), bf16(slots, side, side),
+            bf16(reach + own * LABEL_ROWS, side), bf16(inner, side), bf16(reach + own * LABEL_ROWS, side), f32(inner, side),
+            f32(16, side), *loaded,
         ),
         in_specs=[hbm] * 6,
-        out_specs=[vmem] * 6 + [hbm] + [vmem] * 3,
-        scratch_shapes=[
-            pltpu.SMEM((1, slots), jnp.int32), pltpu.SMEM((1, slots), jnp.int32),
-            pltpu.VMEM((inner, side), jnp.bfloat16), pltpu.VMEM((window * side, side), jnp.float32),
-            pltpu.SMEM((own,), jnp.int32), table_scratch, sem((6,)), sem((CHUNKS,)),
-        ],
+        out_specs=[vmem] * 9,
+        scratch_shapes=slot_scratch + [
+            pltpu.VMEM((panels, cells), jnp.int32), pltpu.VMEM((inner, side), jnp.bfloat16),
+            pltpu.VMEM((window * side, side), jnp.float32),
+        ] + sort_scratch + [sem((6,)), sem((CHUNKS,))],
         compiler_params=params,
         name="push_first",
-    )(*[pltpu.with_memory_space_constraint(array, pltpu.HBM) for array in (
-        block_rows, block_cols, growth, first_labels, last_labels, block_values
-    )])
-
-    from_left = across(right, 1, XA[0])
-    from_right = across(left, -1, XA[1])
-    from_mid = across(mid, 0, XA[2])
+    )(*inputs)
+
+    from_left = across(right, 1, 0, XA[0])
+    from_right = across(left, -1, 0, XA[1])
+    from_mid = across(mid, 0, 0, XA[2])
+
+    table, rates, known, blocks, half = pl.pallas_call(
+        functools.partial(prepare_kernel, own),
+        out_shape=loaded + (f32(8, side),),
+        in_specs=[hbm] * 5 + [vmem] * 4,
+        out_specs=[vmem] * 5,
+        scratch_shapes=slot_scratch + sort_scratch + [sem((6,)), sem((CHUNKS,))],
+        input_output_aliases={5 + i: i for i in range(4)},
+        compiler_params=params,
+        name="prepare",
+    )(*inputs[:3], *inputs[4:], *loads)
 
     to_left, to_mid, to_right, keep_second, part = pl.pallas_call(
         functools.partial(second_kernel, own),
@@ -337,53 +388,60 @@
             bf16(inner + reach + 16, side), bf16(2 * inner, side), bf16(inner + reach + 16, side),
             f32(inner, side), f32(16, side),
         ),
-        in_specs=[hbm] + [vmem] * 8,
+        in_specs=[vmem] * 9,
         out_specs=[vmem] * 5,
         scratch_shapes=[
-            table_scratch, pltpu.VMEM((inner, side), jnp.bfloat16), pltpu.VMEM((window * side, side), jnp.float32),
+            pltpu.SMEM((2, slots), jnp.int32), pltpu.VMEM((inner, side), jnp.bfloat16), pltpu.VMEM((window * side, side), jnp.float32),
             pltpu.VMEM((window * side, side), jnp.bfloat16), pltpu.VMEM((inner, side), jnp.float32), sem,
         ],
         compiler_params=params,
         name="push_second_pull_first",
-    )(table, grown, labels, from_left, from_mid, from_right, part, half, blocks)
-
-    back_left = across(to_right, -1, XB[0])
-    back_right = across(to_left, 1, XB[1])
-    back_mid = across(to_mid, 0, XB[2])
-
-    parts = [part]
+    )(table, rates, known, from_left, from_mid, from_right, part, half, blocks)
+
+    back_left = across(to_right, 1, 1, XB[0])
+    back_right = across(to_left, -1, 1, XB[1])
+    back_mid = across(to_mid, 0, 1, XB[2])
+
+    whole = part
     bit = 1
     while bit < cell_count:
         if bit > 1:
-            total, top = combined(parts)
-            parts = [jnp.concatenate([total, top], axis=0)]
-        masks = [bit] if 2 * bit >= cell_count else [bit, 2 * bit, 3 * bit]
-        parts = [parts[0]] + [flipped(parts[0], mask) for mask in masks]
+            whole = jnp.concatenate(combined(parts), axis=0)
+        parts = [whole] + [flipped(whole, k * bit) for k in range(1, 4) if k * bit < cell_count]
         bit *= 4
-
-    swap_left = across(back_left, 0, XC)
-    swap_right = across(back_right, 0, XC)
+    whole, back_left, back_right = pl.pallas_call(
+        functools.partial(combine_kernel, len(parts)),
+        out_shape=(f32(16, side), bf16(inner + reach + 16, side), bf16(inner + reach + 16, side)),
+        in_specs=[vmem] * len(parts) + [anywhere] * 2,
+        out_specs=[vmem] + [anywhere] * 2,
+        input_output_aliases={len(parts): 1, len(parts) + 1: 2},
+        compiler_params=params,
+        name="combine",
+    )(*parts, back_left, back_right)
+
+    swap_left = across(back_left, 0, 0, XC)
+    swap_right = across(back_right, 0, 0, XC)
 
     fate = pl.pallas_call(
         functools.partial(third_kernel, own),
         out_shape=bf16(1, height, cells),
-        in_specs=[hbm] + [vmem] * 5,
+        in_specs=[vmem] * 6,
         out_specs=vmem,
         scratch_shapes=[
-            table_scratch, pltpu.VMEM((window * side, side), jnp.bfloat16), pltpu.VMEM((inner, side), jnp.float32), sem,
+            pltpu.SMEM((2, slots), jnp.int32), pltpu.VMEM((window * side, side), jnp.bfloat16), pltpu.VMEM((inner, side), jnp.float32), sem,
         ],
         compiler_params=params,
         name="pull_second",
     )(table, back_left, back_mid, back_right, to_mid, blocks)
 
     forward_mass = pl.pallas_call(
-        functools.partial(last_kernel, own, float(cells * cell_count), len(parts)),
+        functools.partial(last_kernel, own, float(cells * cell_count)),
         out_shape=bf16(1, height, cells),
-        in_specs=[vmem] * (len(parts) + 6),
+        in_specs=[vmem] * 7,
         out_specs=vmem,
         compiler_params=params,
         name="normalise",
-    )(*parts, part, keep_first, back_mid, keep_second, swap_left, swap_right)
+    )(whole, part, keep_first, back_mid, keep_second, swap_left, swap_right)
     return forward_mass, fate
 
 

time: 35.9 us -> 31.7 us (0.88)
  starting transfers between devices: 23.4 us -> 17.4 us
  waiting for transfers between devices: 5.2 us -> 8.08 us
  Pallas kernels: 6.41 us -> 5.38 us
    ppermute x8, starting transfers between devices: 13.6 us -> 9.36 us  [across(): return lax.ppermute(array, ('tm', 'cell'), list(route.items()))]
    ppermute x8, waiting for transfers between devices: 1.91 us -> 4.31 us  [across(): return lax.ppermute(array, ('tm', 'cell'), list(route.items()))]
    ppermute x6, starting transfers between devices: 9.76 us -> 8 us  [flipped(): lax.ppermute(array, 'cell', [(c, c ^ bits) for c in range(lax.axis_size('...]
    pallas_call x1, Pallas kernels: 3.62 us -> 2.51 us  [on_device(): pl.pallas_call(functools.partial(first_kernel, own), out_shape=(bf16(reac...]
    ppermute x6, waiting for transfers between devices: 3.29 us -> 3.77 us  [flipped(): lax.ppermute(array, 'cell', [(c, c ^ bits) for c in range(lax.axis_size('...]
  transfers between devices with their start and end apart: 14 -> 14, of which waited for: 4 -> 5; matrix products, arithmetic and copies ran while one was open for 0% -> 0% of each run, Pallas kernels for 6% -> 6%
where the time goes in v3:
time: 31.7 us; the launch traced here: 31.6 us
  starting transfers between devices  17.4 us (55%)
  waiting for transfers between devices  8.08 us (25%)
  Pallas kernels  5.38 us (17%)
  between operations  0.74 us (2%)
    ppermute x8, starting transfers between devices, across(): return lax.ppermute(array, ('tm', 'cell'), list(route.items()))  9.36 us
    ppermute x6, starting transfers between devices, flipped(): lax.ppermute(array, 'cell', [(c, c ^ bits) for c in range(lax.axis_size('...  8 us
    ppermute x8, waiting for transfers between devices, across(): return lax.ppermute(array, ('tm', 'cell'), list(route.items()))  4.31 us
    ppermute x6, waiting for transfers between devices, flipped(): lax.ppermute(array, 'cell', [(c, c ^ bits) for c in range(lax.axis_size('...  3.77 us
    pallas_call x1, Pallas kernels, on_device(): pl.pallas_call(functools.partial(first_kernel, own), out_shape=(bf16(reac...  2.51 us
    pallas_call x1, Pallas kernels, on_device(): pl.pallas_call(functools.partial(third_kernel, own), out_shape=bf16(1, he...  1.98 us
    pallas_call x1, Pallas kernels, on_device(): pl.pallas_call(functools.partial(last_kernel, own, float(cells * cell_cou...  0.79 us
  transfers between devices with their start and end apart: 14, of which 5 were waited for; matrix products, arithmetic and copies ran while one was open for 0% of the time, Pallas kernels for 6%

profile of v3, /device:TPU:0, one launch (start us, length us, event | category | flops | bytes accessed | tf_op | source)
XLA Modules:
  0.0 31.6 jit_solution(3094115842267289530)
XLA Ops:
  0.6 2.5 %push_first.1 = (bf16[576,128]{1,0:T(8,128)(2,1)S(1)}, bf16[512,128]{1,0:T(8,128)(2,1)S(1)}, bf16[576,128]{1,0:T(8,128)(2,1)S(1)}, f32[512,128]{1,0:T(8,128)S(1)...) custom-call(s32[1,64]{1,0:T(1,128)} %rows_hbm.3, ...), custom_call_target="tpu_custom_call" | custom-call | tf_op jit(solution)/shard_map/push_first/pallas_call | solution.py:354
  3.1 1.9 %collective-permute-start = (bf16[576,128]{1,0:T(8,128)(2,1)S(1)}, bf16[576,128]{1,0:T(8,128)(2,1)S(1)}, u32[]{:S(2)}, u32[]{:S(2)}) collective-permute-start(bf16[576,128]{1,0:T(8,128)(2,1)S(1)} %get-tuple-element.31), channel_id=1, source_target_pairs={{0,17},{1,18},{2,19},{3,20},{4,21},{5,22},{6,23},{7,24},{8,25},{9,... | collective-permute-start | bytes 442376 | tf_op jit(solution)/shard_map/ppermute | solution.py:321
  5.0 3.4 %collective-permute-start.2 = (bf16[576,128]{1,0:T(8,128)(2,1)S(1)}, bf16[576,128]{1,0:T(8,128)(2,1)S(1)}, u32[]{:S(2)}, u32[]{:S(2)}) collective-permute-start(bf16[576,128]{1,0:T(8,128)(2,1)S(1)} %get-tuple-element.33), channel_id=1, source_target_pairs={{1,16},{2,17},{3,18},{4,19},{5,20},{6,21},{7,22},{8,23},{9,24},{10... | collective-permute-start | bytes 442376 | tf_op jit(solution)/shard_map/ppermute | solution.py:321
  8.5 0.0 collective-permute-start.1
  8.5 0.1 prepare.1
  8.5 1.3 %collective-permute-done.1.mid_ref = bf16[512,128]{1,0:T(8,128)(2,1)S(1)} collective-permute-done((bf16[512,128]{1,0:T(8,128)(2,1)S(1)}, bf16[512,128]{1,0:T(8,128)(2,1)S(1)}, u32[]{:S(2)}, u32[]{:S(2)}) %collective-permute-start.1) | collective-permute-done | bytes 131104 | tf_op jit(solution)/shard_map/ppermute | solution.py:321
  9.8 0.0 collective-permute-done.left_ref
  9.8 1.3 %collective-permute-done.2.right_ref = bf16[576,128]{1,0:T(8,128)(2,1)S(1)} collective-permute-done((bf16[576,128]{1,0:T(8,128)(2,1)S(1)}, bf16[576,128]{1,0:T(8,128)(2,1)S(1)}, u32[]{:S(2)}, u32[]{:S(2)}) %collective-permute-start.2) | collective-permute-done | bytes 147488 | tf_op jit(solution)/shard_map/ppermute | solution.py:321
  11.1 0.1 collective-permute-start.5
  11.2 1.9 %collective-permute-start.4 = (f32[16,128]{1,0:T(8,128)S(1)}, f32[16,128]{1,0:T(8,128)S(1)}, u32[]{:S(2)}, u32[]{:S(2)}) collective-permute-start(f32[16,128]{1,0:T(8,128)S(1)} %get-tuple-element.37.own_part), channel_id=1, source_target_pairs={{0,2},{1,3},{2,0},{3,1},{4,6},{5,7},{6,4},{7,5},{8,10},{9,11},{10,... | collective-permute-start | bytes 24584 | tf_op jit(solution)/shard_map/ppermute | solution.py:325
  13.2 1.5 %collective-permute-start.3 = (f32[16,128]{1,0:T(8,128)S(1)}, f32[16,128]{1,0:T(8,128)S(1)}, u32[]{:S(2)}, u32[]{:S(2)}) collective-permute-start(f32[16,128]{1,0:T(8,128)S(1)} %get-tuple-element.37.own_part), channel_id=1, source_target_pairs={{0,1},{1,0},{2,3},{3,2},{4,5},{5,4},{6,7},{7,6},{8,9},{9,8},{10,11... | collective-permute-start | bytes 24584 | tf_op jit(solution)/shard_map/ppermute | solution.py:325
  14.7 0.7 %collective-permute-start.9 = (bf16[1040,128]{1,0:T(8,128)(2,1)S(1)}, bf16[1040,128]{1,0:T(8,128)(2,1)S(1)}, u32[]{:S(2)}, u32[]{:S(2)}) collective-permute-start(bf16[1040,128]{1,0:T(8,128)(2,1)S(1)} %get-tuple-element.38), channel_id=1, source_target_pairs={{16,1},{17,2},{18,3},{19,4},{20,5},{21,6},{22,7},{23,8},{24,9},{25... | collective-permute-start | bytes 798728 | tf_op jit(solution)/shard_map/ppermute | solution.py:321
  15.4 2.7 %collective-permute-start.10 = (bf16[1040,128]{1,0:T(8,128)(2,1)S(1)}, bf16[1040,128]{1,0:T(8,128)(2,1)S(1)}, u32[]{:S(2)}, u32[]{:S(2)}) collective-permute-start(bf16[1040,128]{1,0:T(8,128)(2,1)S(1)} %get-tuple-element.39), channel_id=1, source_target_pairs={{17,0},{18,1},{19,2},{20,3},{21,4},{22,5},{23,6},{24,7},{25,8},{26... | collective-permute-start | bytes 798728 | tf_op jit(solution)/shard_map/ppermute | solution.py:321
  18.2 3.7 %collective-permute-start.8 = (f32[16,128]{1,0:T(8,128)S(1)}, f32[16,128]{1,0:T(8,128)S(1)}, u32[]{:S(2)}, u32[]{:S(2)}) collective-permute-start(f32[16,128]{1,0:T(8,128)S(1)} %pad_maximum_fusion.refs_0_), channel_id=1, source_target_pairs={{0,12},{1,13},{2,14},{3,15},{4,8},{5,9},{6,10},{7,11},{8,4},{9,5},... | collective-permute-start | bytes 24584 | tf_op jit(solution)/shard_map/ppermute | solution.py:325
  21.8 0.8 %collective-permute-start.6 = (f32[16,128]{1,0:T(8,128)S(1)}, f32[16,128]{1,0:T(8,128)S(1)}, u32[]{:S(2)}, u32[]{:S(2)}) collective-permute-start(f32[16,128]{1,0:T(8,128)S(1)} %pad_maximum_fusion.refs_0_), channel_id=1, source_target_pairs={{0,4},{1,5},{2,6},{3,7},{4,0},{5,1},{6,2},{7,3},{8,12},{9,13},{10,... | collective-permute-start | bytes 24584 | tf_op jit(solution)/shard_map/ppermute | solution.py:325
  22.6 1.1 %collective-permute-done.8.refs_3_ = f32[16,128]{1,0:T(8,128)S(1)} collective-permute-done((f32[16,128]{1,0:T(8,128)S(1)}, f32[16,128]{1,0:T(8,128)S(1)}, u32[]{:S(2)}, u32[]{:S(2)}) %collective-permute-start.8) | collective-permute-done | bytes 8224 | tf_op jit(solution)/shard_map/ppermute | solution.py:325
  23.8 2.6 %collective-permute-done.7.refs_2_ = f32[16,128]{1,0:T(8,128)S(1)} collective-permute-done((f32[16,128]{1,0:T(8,128)S(1)}, f32[16,128]{1,0:T(8,128)S(1)}, u32[]{:S(2)}, u32[]{:S(2)}) %collective-permute-start.7) | collective-permute-done | bytes 8224 | tf_op jit(solution)/shard_map/ppermute | solution.py:325
  26.4 0.0 collective-permute-done.6.refs_1_
  26.4 0.1 collective-permute-start.12
  26.5 0.5 %collective-permute-start.13 = (bf16[1040,128]{1,0:T(8,128)(2,1)S(1)}, bf16[1040,128]{1,0:T(8,128)(2,1)S(1)}, u32[]{:S(2)}, u32[]{:S(2)}) collective-permute-start(bf16[1040,128]{1,0:T(8,128)(2,1)S(1)} %get-tuple-element.45.right_ref), channel_id=1, source_target_pairs={{0,16},{1,17},{2,18},{3,19},{4,20},{5,21},{6,22},{7,23},{8,24},{9,... | collective-permute-start | bytes 798728 | tf_op jit(solution)/shard_map/ppermute | solution.py:321
  27.0 0.1 collective-permute-start.11
  27.1 1.7 %collective-permute-done.11.halo_first.mid_ref = bf16[1024,128]{1,0:T(8,128)(2,1)S(1)} collective-permute-done((bf16[1024,128]{1,0:T(8,128)(2,1)S(1)}, bf16[1024,128]{1,0:T(8,128)(2,1)S(1)}, u32[]{:S(2)}, u32[]{:S(2)}) %collective-permute-start.11) | collective-permute-done | bytes 262176 | tf_op jit(solution)/shard_map/ppermute | solution.py:321
  28.8 2.0 %pull_second.1 = bf16[1,128,512]{2,1,0:T(8,128)(2,1)} custom-call(s32[2,64]{1,0:T(2,128)S(1)} %get-tuple-element.28.table_ref, bf16[1040,128]{1,0:T(8,128)(2,1)S(1)} %get-tuple-element.44.left_ref, bf16[1024,128]{1,0:T(8,128)(2,1)S(1)} %collective-permute-done.11.halo_first.mid_ref, bf16[1040,128]{1,0:T(8,128)(2,1)S(1)} %get-tuple-element.45.right_ref, ...), custom_call_target="tpu_custom_call" | custom-call | tf_op jit(solution)/shard_map/pull_second/pallas_call | solution.py:425
  30.8 0.8 %normalise.1 = bf16[1,128,512]{2,1,0:T(8,128)(2,1)} custom-call(f32[16,128]{1,0:T(8,128)S(1)} %get-tuple-element.40.whole, f32[16,128]{1,0:T(8,128)S(1)} %get-tuple-element.37.own_part, f32[512,128]{1,0:T(8,128)S(1)} %get-tuple-element.41.keep_first, bf16[1024,128]{1,0:T(8,128)(2,1)S(1)} %collective-permute-done.11.halo_first.mid_ref, ...), custom_call_target="tpu_custom_call" | custom-call | tf_op jit(solution)/shard_map/normalise/pallas_call | solution.py:437
  (12 shorter events, 0.1 us)
Async XLA Ops:
  3.1 6.7 %collective-permute-start = (bf16[576,128]{1,0:T(8,128)(2,1)S(1)}, bf16[576,128]{1,0:T(8,128)(2,1)S(1)}, u32[]{:S(2)}, u32[]{:S(2)}) collective-permute-start(bf16[576,128]{1,0:T(8,128)(2,1)S(1)} %get-tuple-element.31), channel_id=1, source_target_pairs={{0,17},{1,18},{2,19},{3,20},{4,21},{5,22},{6,23},{7,24},{8,25},{9,... | collective-permute-start | bytes 442376 | tf_op jit(solution)/shard_map/ppermute | solution.py:321
  5.0 6.1 %collective-permute-start.2 = (bf16[576,128]{1,0:T(8,128)(2,1)S(1)}, bf16[576,128]{1,0:T(8,128)(2,1)S(1)}, u32[]{:S(2)}, u32[]{:S(2)}) collective-permute-start(bf16[576,128]{1,0:T(8,128)(2,1)S(1)} %get-tuple-element.33), channel_id=1, source_target_pairs={{1,16},{2,17},{3,18},{4,19},{5,20},{6,21},{7,22},{8,23},{9,24},{10... | collective-permute-start | bytes 442376 | tf_op jit(solution)/shard_map/ppermute | solution.py:321
  8.5 1.3 %collective-permute-start.1 = (bf16[512,128]{1,0:T(8,128)(2,1)S(1)}, bf16[512,128]{1,0:T(8,128)(2,1)S(1)}, u32[]{:S(2)}, u32[]{:S(2)}) collective-permute-start(bf16[512,128]{1,0:T(8,128)(2,1)S(1)} %get-tuple-element.32), channel_id=1, source_target_pairs={{0,16},{1,17},{2,18},{3,19},{4,20},{5,21},{6,22},{7,23},{8,24},{9,... | collective-permute-start | bytes 393224 | tf_op jit(solution)/shard_map/ppermute | solution.py:321
  11.1 7.0 %collective-permute-start.5 = (f32[16,128]{1,0:T(8,128)S(1)}, f32[16,128]{1,0:T(8,128)S(1)}, u32[]{:S(2)}, u32[]{:S(2)}) collective-permute-start(f32[16,128]{1,0:T(8,128)S(1)} %get-tuple-element.37.own_part), channel_id=1, source_target_pairs={{0,3},{1,2},{2,1},{3,0},{4,7},{5,6},{6,5},{7,4},{8,11},{9,10},{10,... | collective-permute-start | bytes 24584 | tf_op jit(solution)/shard_map/ppermute | solution.py:325
  11.2 6.9 %collective-permute-start.4 = (f32[16,128]{1,0:T(8,128)S(1)}, f32[16,128]{1,0:T(8,128)S(1)}, u32[]{:S(2)}, u32[]{:S(2)}) collective-permute-start(f32[16,128]{1,0:T(8,128)S(1)} %get-tuple-element.37.own_part), channel_id=1, source_target_pairs={{0,2},{1,3},{2,0},{3,1},{4,6},{5,7},{6,4},{7,5},{8,10},{9,11},{10,... | collective-permute-start | bytes 24584 | tf_op jit(solution)/shard_map/ppermute | solution.py:325
  13.2 5.0 %collective-permute-start.3 = (f32[16,128]{1,0:T(8,128)S(1)}, f32[16,128]{1,0:T(8,128)S(1)}, u32[]{:S(2)}, u32[]{:S(2)}) collective-permute-start(f32[16,128]{1,0:T(8,128)S(1)} %get-tuple-element.37.own_part), channel_id=1, source_target_pairs={{0,1},{1,0},{2,3},{3,2},{4,5},{5,4},{6,7},{7,6},{8,9},{9,8},{10,11... | collective-permute-start | bytes 24584 | tf_op jit(solution)/shard_map/ppermute | solution.py:325
  14.7 11.7 %collective-permute-start.9 = (bf16[1040,128]{1,0:T(8,128)(2,1)S(1)}, bf16[1040,128]{1,0:T(8,128)(2,1)S(1)}, u32[]{:S(2)}, u32[]{:S(2)}) collective-permute-start(bf16[1040,128]{1,0:T(8,128)(2,1)S(1)} %get-tuple-element.38), channel_id=1, source_target_pairs={{16,1},{17,2},{18,3},{19,4},{20,5},{21,6},{22,7},{23,8},{24,9},{25... | collective-permute-start | bytes 798728 | tf_op jit(solution)/shard_map/ppermute | solution.py:321
  15.4 11.0 %collective-permute-start.10 = (bf16[1040,128]{1,0:T(8,128)(2,1)S(1)}, bf16[1040,128]{1,0:T(8,128)(2,1)S(1)}, u32[]{:S(2)}, u32[]{:S(2)}) collective-permute-start(bf16[1040,128]{1,0:T(8,128)(2,1)S(1)} %get-tuple-element.39), channel_id=1, source_target_pairs={{17,0},{18,1},{19,2},{20,3},{21,4},{22,5},{23,6},{24,7},{25,8},{26... | collective-permute-start | bytes 798728 | tf_op jit(solution)/shard_map/ppermute | solution.py:321
  18.2 5.6 %collective-permute-start.8 = (f32[16,128]{1,0:T(8,128)S(1)}, f32[16,128]{1,0:T(8,128)S(1)}, u32[]{:S(2)}, u32[]{:S(2)}) collective-permute-start(f32[16,128]{1,0:T(8,128)S(1)} %pad_maximum_fusion.refs_0_), channel_id=1, source_target_pairs={{0,12},{1,13},{2,14},{3,15},{4,8},{5,9},{6,10},{7,11},{8,4},{9,5},... | collective-permute-start | bytes 24584 | tf_op jit(solution)/shard_map/ppermute | solution.py:325
  21.8 4.5 %collective-permute-start.7 = (f32[16,128]{1,0:T(8,128)S(1)}, f32[16,128]{1,0:T(8,128)S(1)}, u32[]{:S(2)}, u32[]{:S(2)}) collective-permute-start(f32[16,128]{1,0:T(8,128)S(1)} %pad_maximum_fusion.refs_0_), channel_id=1, source_target_pairs={{0,8},{1,9},{2,10},{3,11},{4,12},{5,13},{6,14},{7,15},{8,0},{9,1},... | collective-permute-start | bytes 24584 | tf_op jit(solution)/shard_map/ppermute | solution.py:325
  21.8 4.5 %collective-permute-start.6 = (f32[16,128]{1,0:T(8,128)S(1)}, f32[16,128]{1,0:T(8,128)S(1)}, u32[]{:S(2)}, u32[]{:S(2)}) collective-permute-start(f32[16,128]{1,0:T(8,128)S(1)} %pad_maximum_fusion.refs_0_), channel_id=1, source_target_pairs={{0,4},{1,5},{2,6},{3,7},{4,0},{5,1},{6,2},{7,3},{8,12},{9,13},{10,... | collective-permute-start | bytes 24584 | tf_op jit(solution)/shard_map/ppermute | solution.py:325
  26.4 4.4 %collective-permute-start.12 = (bf16[1040,128]{1,0:T(8,128)(2,1)S(1)}, bf16[1040,128]{1,0:T(8,128)(2,1)S(1)}, u32[]{:S(2)}, u32[]{:S(2)}) collective-permute-start(bf16[1040,128]{1,0:T(8,128)(2,1)S(1)} %get-tuple-element.44.left_ref), channel_id=1, source_target_pairs={{0,16},{1,17},{2,18},{3,19},{4,20},{5,21},{6,22},{7,23},{8,24},{9,... | collective-permute-start | bytes 798728 | tf_op jit(solution)/shard_map/ppermute | solution.py:321
  26.5 4.3 %collective-permute-start.13 = (bf16[1040,128]{1,0:T(8,128)(2,1)S(1)}, bf16[1040,128]{1,0:T(8,128)(2,1)S(1)}, u32[]{:S(2)}, u32[]{:S(2)}) collective-permute-start(bf16[1040,128]{1,0:T(8,128)(2,1)S(1)} %get-tuple-element.45.right_ref), channel_id=1, source_target_pairs={{0,16},{1,17},{2,18},{3,19},{4,20},{5,21},{6,22},{7,23},{8,24},{9,... | collective-permute-start | bytes 798728 | tf_op jit(solution)/shard_map/ppermute | solution.py:321
  27.0 1.8 %collective-permute-start.11 = (bf16[1024,128]{1,0:T(8,128)(2,1)S(1)}, bf16[1024,128]{1,0:T(8,128)(2,1)S(1)}, u32[]{:S(2)}, u32[]{:S(2)}) collective-permute-start(bf16[1024,128]{1,0:T(8,128)(2,1)S(1)} %get-tuple-element.42.mine_ref), channel_id=1, source_target_pairs={{16,0},{17,1},{18,2},{19,3},{20,4},{21,5},{22,6},{23,7},{24,8},{25... | collective-permute-start | bytes 786440 | tf_op jit(solution)/shard_map/ppermute | solution.py:321

commit v4 on v3

--- a/solution.py
+++ b/solution.py
@@ -45,6 +45,11 @@
             pulled = lax.dot_general(wide, pair, (((1,), (1,)), ((), ())), preferred_element_type=jnp.float32)
             total = pulled if total is None else total + pulled
         out[row * side : (row + 1) * side, :] = total
+
+
+def labels_of(sent, start, block, panels):
+    tile = sent[pl.ds(start + block // 2 * LABEL_ROWS, LABEL_ROWS), :].astype(jnp.float32).astype(jnp.int32)
+    return tile[block % 2 * panels : (block % 2 + 1) * panels]
 
 
 def fates_of(pulled):
@@ -122,11 +127,11 @@
         mid_ref[...] = acc[reach : reach + inner, :].astype(jnp.bfloat16)
         right_ref[0:reach, :] = acc[reach + inner :, :].astype(jnp.bfloat16)
         keep_ref[...] = acc[reach : reach + inner, :]
-        for b in range(own):
-            exact = known[:, pl.ds(b * side, side)].astype(jnp.float32).astype(jnp.bfloat16)
-            tall = jnp.concatenate([exact, exact], axis=0)
-            left_ref[pl.ds(reach + b * LABEL_ROWS, LABEL_ROWS), :] = tall
-            right_ref[pl.ds(reach + b * LABEL_ROWS, LABEL_ROWS), :] = tall
+        for b in range(0, own, 2):
+            pair = [known[:, pl.ds((b + i) * side, side)] for i in range(2)]
+            tall = jnp.concatenate(pair, axis=0).astype(jnp.float32).astype(jnp.bfloat16)
+            left_ref[pl.ds(reach + b * LABEL_ROWS // 2, LABEL_ROWS), :] = tall
+            right_ref[pl.ds(reach + b * LABEL_ROWS // 2, LABEL_ROWS), :] = tall
         total = acc[0:side, :]
         for w in range(1, own + 2 * BAND_REACH):
             total += acc[w * side : (w + 1) * side, :]
@@ -221,13 +226,11 @@
         panels = known_ref.shape[0]
         for w in range(own + 2 * BAND_REACH):
             if w < BAND_REACH:
-                rows = pl.ds(reach + w * LABEL_ROWS, LABEL_ROWS)
-                labels = left_ref[rows, :][0:panels].astype(jnp.float32).astype(jnp.int32)
+                labels = labels_of(left_ref, reach, w, panels)
             elif w < BAND_REACH + own:
                 labels = known_ref[:, pl.ds((w - BAND_REACH) * side, side)]
             else:
-                rows = pl.ds(reach + (w - BAND_REACH - own) * LABEL_ROWS, LABEL_ROWS)
-                labels = right_ref[rows, :][0:panels].astype(jnp.float32).astype(jnp.int32)
+                labels = labels_of(right_ref, reach, w - BAND_REACH - own, panels)
             fated[pl.ds(w * side, side), :] = jnp.where(one_hot(labels), 1.0, 0.0).astype(jnp.bfloat16)
         pull_backward(table, fated, blk, pulled, own)
         for b in range(own):
@@ -238,30 +241,6 @@
             to_right[at, :] = fates
 
 
-def third_kernel(own, table_ref, left_ref, mid_ref, right_ref, mine_ref, blk, fate_ref, table, fated, pulled, sem):
-    side = blk.shape[1]
-    reach, inner = BAND_REACH * side, own * side
-
-    @pl.when(lax.axis_index("tm") == 0)
-    def _():
-        table_copy = pltpu.make_async_copy(table_ref, table, sem)
-        table_copy.start()
-        fated[0:reach, :] = left_ref[0:reach, :]
-        fated[reach : reach + inner, :] = mid_ref[0:inner, :]
-        fated[reach + inner :, :] = right_ref[0:reach, :]
-        table_copy.wait()
-        pull_backward(table, fated, blk, pulled, own)
-        for b in range(own):
-            at = pl.ds(b * side, side)
-            fate_ref[0, :, at] = fates_of(pulled[at, :])
-
-    @pl.when(lax.axis_index("tm") != 0)
-    def _():
-        for b in range(own):
-            at = pl.ds(b * side, side)
-            fate_ref[0, :, at] = mine_ref[at, :]
-
-
 def combined(parts):
     top = functools.reduce(jnp.maximum, [part[8:16] for part in parts])
     total = sum(part[0:8] * jnp.exp2(part[8:16] - top) for part in parts)
@@ -269,40 +248,63 @@
 
 
 def combine_kernel(count, *refs):
+    mine, out, to_swap, sem = refs[count], refs[count + 3], refs[count + 4], refs[count + 6]
+    copy = pltpu.make_async_copy(mine, to_swap.at[pl.ds(0, mine.shape[0])], sem)
+
+    @pl.when(lax.axis_index("tm") != 0)
+    def _():
+        copy.start()
+
     total, top = combined([part[...] for part in refs[:count]])
-    out = refs[count + 2]
     out[0:8, :] = total
     out[8:16, :] = top
 
-
-def last_kernel(own, all_cells, whole, own_part, keep_first, halo_first, keep_second, left_ref, right_ref, mass_ref):
-    side = keep_first.shape[1]
+    @pl.when(lax.axis_index("tm") != 0)
+    def _():
+        copy.wait()
+
+
+def last_kernel(own, all_cells, table_ref, whole, own_part, keep_first, keep_second, back_left, back_right, swap_left,
+                swap_right, mine_ref, blk, mass_ref, fate_ref, table, fated, pulled, sem):
+    side = blk.shape[1]
     reach, inner = BAND_REACH * side, own * side
     here = lax.axis_index("cell")
     total, top = whole[0:8, :], whole[8:16, :]
-    scale = all_cells / as_column(total[0:1], side)
 
     @pl.when(lax.axis_index("tm") == 0)
     def _():
-        for b in range(own):
-            at = pl.ds(b * side, side)
-            mass = keep_first[at, :] + halo_first[pl.ds(inner + b * side, side), :].astype(jnp.float32)
+        table_copy = pltpu.make_async_copy(table_ref, table, sem)
+        table_copy.start()
+        fated[0:reach, :] = back_left[0:reach, :]
+        fated[reach : reach + inner, :] = swap_left[0:inner, :]
+        fated[reach + inner :, :] = back_right[0:reach, :]
+        scale = all_cells / as_column(total[0:1], side)
+        for b in range(own):
+            at = pl.ds(b * side, side)
+            mass = keep_first[at, :] + swap_left[pl.ds(inner + b * side, side), :].astype(jnp.float32)
             mass_ref[0, :, at] = (mass * scale).astype(jnp.bfloat16)
+        table_copy.wait()
+        pull_backward(table, fated, blk, pulled, own)
+        for b in range(own):
+            at = pl.ds(b * side, side)
+            fate_ref[0, :, at] = fates_of(pulled[at, :])
 
     @pl.when(lax.axis_index("tm") != 0)
     def _():
         has_left, has_right = here > 0, here < lax.axis_size("cell") - 1
         power = pl.ds(inner + reach, 16)
+        scale = all_cells / as_column(total[0:1], side)
         own_scale = as_column(jnp.exp2(own_part[8:9] - top[0:1]), side)
-        left_scale = as_column(jnp.exp2(left_ref[power, :][0:1].astype(jnp.float32) - top[0:1]), side)
-        right_scale = as_column(jnp.exp2(right_ref[power, :][0:1].astype(jnp.float32) - top[0:1]), side)
+        left_scale = as_column(jnp.exp2(swap_left[power, :][0:1].astype(jnp.float32) - top[0:1]), side)
+        right_scale = as_column(jnp.exp2(swap_right[power, :][0:1].astype(jnp.float32) - top[0:1]), side)
         for b in range(own):
             at = pl.ds(b * side, side)
             aside = pl.ds(inner + b * side, side)
             mass = keep_second[at, :] * own_scale
-            mass += jnp.where(has_left, left_ref[aside, :].astype(jnp.float32) * left_scale, 0.0)
-            mass += jnp.where(has_right, right_ref[aside, :].astype(jnp.float32) * right_scale, 0.0)
+            mass += jnp.where(has_left, swap_left[aside, :].astype(jnp.float32) * left_scale, 0.0)
+            mass += jnp.where(has_right, swap_right[aside, :].astype(jnp.float32) * right_scale, 0.0)
             mass_ref[0, :, at] = (mass * scale).astype(jnp.bfloat16)
+            fate_ref[0, :, at] = mine_ref[at, :]
 
 
 def across(array, distance, sender, mode):
@@ -354,7 +356,7 @@
     left, mid, right, keep_first, part, *loads = pl.pallas_call(
         functools.partial(first_kernel, own),
         out_shape=(
-            bf16(reach + own * LABEL_ROWS, side), bf16(inner, side), bf16(reach + own * LABEL_ROWS, side), f32(inner, side),
+            bf16(reach + own * LABEL_ROWS // 2, side), bf16(inner, side), bf16(reach + own * LABEL_ROWS // 2, side), f32(inner, side),
             f32(16, side), *loaded,
         ),
         in_specs=[hbm] * 6,
@@ -400,7 +402,6 @@
 
     back_left = across(to_right, 1, 1, XB[0])
     back_right = across(to_left, -1, 1, XB[1])
-    back_mid = across(to_mid, 0, 1, XB[2])
 
     whole = part
     bit = 1
@@ -412,36 +413,29 @@
     whole, back_left, back_right = pl.pallas_call(
         functools.partial(combine_kernel, len(parts)),
         out_shape=(f32(16, side), bf16(inner + reach + 16, side), bf16(inner + reach + 16, side)),
-        in_specs=[vmem] * len(parts) + [anywhere] * 2,
+        in_specs=[vmem] * len(parts) + [anywhere] * 3,
         out_specs=[vmem] + [anywhere] * 2,
-        input_output_aliases={len(parts): 1, len(parts) + 1: 2},
+        scratch_shapes=[sem],
+        input_output_aliases={len(parts) + 1: 1, len(parts) + 2: 2},
         compiler_params=params,
         name="combine",
-    )(*parts, back_left, back_right)
+    )(*parts, to_mid, back_left, back_right)
 
     swap_left = across(back_left, 0, 0, XC)
     swap_right = across(back_right, 0, 0, XC)
 
-    fate = pl.pallas_call(
-        functools.partial(third_kernel, own),
-        out_shape=bf16(1, height, cells),
-        in_specs=[vmem] * 6,
-        out_specs=vmem,
+    forward_mass, fate = pl.pallas_call(
+        functools.partial(last_kernel, own, float(cells * cell_count)),
+        out_shape=(bf16(1, height, cells), bf16(1, height, cells)),
+        in_specs=[vmem] * 11,
+        out_specs=[vmem] * 2,
         scratch_shapes=[
-            pltpu.SMEM((2, slots), jnp.int32), pltpu.VMEM((window * side, side), jnp.bfloat16), pltpu.VMEM((inner, side), jnp.float32), sem,
+            pltpu.SMEM((2, slots), jnp.int32), pltpu.VMEM((window * side, side), jnp.bfloat16),
+            pltpu.VMEM((inner, side), jnp.float32), sem,
         ],
         compiler_params=params,
-        name="pull_second",
-    )(table, back_left, back_mid, back_right, to_mid, blocks)
-
-    forward_mass = pl.pallas_call(
-        functools.partial(last_kernel, own, float(cells * cell_count)),
-        out_shape=bf16(1, height, cells),
-        in_specs=[vmem] * 7,
-        out_specs=vmem,
-        compiler_params=params,
-        name="normalise",
-    )(whole, part, keep_first, back_mid, keep_second, swap_left, swap_right)
+        name="pull_second_normalise",
+    )(table, whole, part, keep_first, keep_second, back_left, back_right, swap_left, swap_right, to_mid, blocks)
     return forward_mass, fate
 
 

time: 31.7 us -> 30.4 us (0.959)
  Pallas kernels: 5.38 us -> 4.65 us
  waiting for transfers between devices: 8.08 us -> 7.71 us
    pallas_call x1 -> x0, Pallas kernels: 1.98 us -> none  [on_device(): pl.pallas_call(functools.partial(third_kernel, own), out_shape=bf16(1, he...]
    pallas_call x1, Pallas kernels: 0.79 us -> 2.02 us  [on_device(): pl.pallas_call(functools.partial(last_kernel, own, float(cells * cell_cou...]
    ppermute x8 -> x7, waiting for transfers between devices: 4.31 us -> 3.93 us  [across(): return lax.ppermute(array, ('tm', 'cell'), list(route.items()))]
    ppermute x8 -> x7, starting transfers between devices: 9.36 us -> 9.17 us  [across(): return lax.ppermute(array, ('tm', 'cell'), list(route.items()))]
  transfers between devices with their start and end apart: 14 -> 13, of which waited for: 5 -> 6; matrix products, arithmetic and copies ran while one was open for 0% -> 0% of each run, Pallas kernels for 6% -> 0%
where the time goes in v4:
time: 30.4 us; the launch traced here: 30.3 us
  starting transfers between devices  17.2 us (57%)
  waiting for transfers between devices  7.71 us (25%)
  Pallas kernels  4.65 us (15%)
  between operations  0.72 us (2%)
    ppermute x7, starting transfers between devices, across(): return lax.ppermute(array, ('tm', 'cell'), list(route.items()))  9.17 us
    ppermute x6, starting transfers between devices, flipped(): lax.ppermute(array, 'cell', [(c, c ^ bits) for c in range(lax.axis_size('...  8 us
    ppermute x7, waiting for transfers between devices, across(): return lax.ppermute(array, ('tm', 'cell'), list(route.items()))  3.93 us
    ppermute x6, waiting for transfers between devices, flipped(): lax.ppermute(array, 'cell', [(c, c ^ bits) for c in range(lax.axis_size('...  3.78 us
    pallas_call x1, Pallas kernels, on_device(): pl.pallas_call(functools.partial(first_kernel, own), out_shape=(bf16(reac...  2.51 us
    pallas_call x1, Pallas kernels, on_device(): pl.pallas_call(functools.partial(last_kernel, own, float(cells * cell_cou...  2.02 us
  transfers between devices with their start and end apart: 13, of which 6 were waited for; matrix products, arithmetic and copies ran while one was open for 0% of the time, Pallas kernels for 0%

profile of v4, /device:TPU:0, one launch (start us, length us, event | category | flops | bytes accessed | tf_op | source)
XLA Modules:
  0.0 30.3 jit_solution(280670213552760350)
XLA Ops:
  0.6 2.5 %push_first.1 = (bf16[544,128]{1,0:T(8,128)(2,1)S(1)}, bf16[512,128]{1,0:T(8,128)(2,1)S(1)}, bf16[544,128]{1,0:T(8,128)(2,1)S(1)}, f32[512,128]{1,0:T(8,128)S(1)...) custom-call(s32[1,64]{1,0:T(1,128)} %rows_hbm.3, ...), custom_call_target="tpu_custom_call" | custom-call | tf_op jit(solution)/shard_map/push_first/pallas_call | solution.py:356
  3.1 1.9 %collective-permute-start = (bf16[544,128]{1,0:T(8,128)(2,1)S(1)}, bf16[544,128]{1,0:T(8,128)(2,1)S(1)}, u32[]{:S(2)}, u32[]{:S(2)}) collective-permute-start(bf16[544,128]{1,0:T(8,128)(2,1)S(1)} %get-tuple-element.31), channel_id=1, source_target_pairs={{0,17},{1,18},{2,19},{3,20},{4,21},{5,22},{6,23},{7,24},{8,25},{9,... | collective-permute-start | bytes 417800 | tf_op jit(solution)/shard_map/ppermute | solution.py:323
  5.0 3.4 %collective-permute-start.2 = (bf16[544,128]{1,0:T(8,128)(2,1)S(1)}, bf16[544,128]{1,0:T(8,128)(2,1)S(1)}, u32[]{:S(2)}, u32[]{:S(2)}) collective-permute-start(bf16[544,128]{1,0:T(8,128)(2,1)S(1)} %get-tuple-element.33), channel_id=1, source_target_pairs={{1,16},{2,17},{3,18},{4,19},{5,20},{6,21},{7,22},{8,23},{9,24},{10... | collective-permute-start | bytes 417800 | tf_op jit(solution)/shard_map/ppermute | solution.py:323
  8.5 0.0 collective-permute-start.1
  8.5 0.1 prepare.1
  8.5 1.3 %collective-permute-done.1.mid_ref = bf16[512,128]{1,0:T(8,128)(2,1)S(1)} collective-permute-done((bf16[512,128]{1,0:T(8,128)(2,1)S(1)}, bf16[512,128]{1,0:T(8,128)(2,1)S(1)}, u32[]{:S(2)}, u32[]{:S(2)}) %collective-permute-start.1) | collective-permute-done | bytes 131104 | tf_op jit(solution)/shard_map/ppermute | solution.py:323
  9.8 1.2 %collective-permute-done.2.right_ref = bf16[544,128]{1,0:T(8,128)(2,1)S(1)} collective-permute-done((bf16[544,128]{1,0:T(8,128)(2,1)S(1)}, bf16[544,128]{1,0:T(8,128)(2,1)S(1)}, u32[]{:S(2)}, u32[]{:S(2)}) %collective-permute-start.2) | collective-permute-done | bytes 139296 | tf_op jit(solution)/shard_map/ppermute | solution.py:323
  11.1 0.1 collective-permute-start.5
  11.1 1.8 %collective-permute-start.4 = (f32[16,128]{1,0:T(8,128)S(1)}, f32[16,128]{1,0:T(8,128)S(1)}, u32[]{:S(2)}, u32[]{:S(2)}) collective-permute-start(f32[16,128]{1,0:T(8,128)S(1)} %get-tuple-element.37.own_part), channel_id=1, source_target_pairs={{0,2},{1,3},{2,0},{3,1},{4,6},{5,7},{6,4},{7,5},{8,10},{9,11},{10,... | collective-permute-start | bytes 24584 | tf_op jit(solution)/shard_map/ppermute | solution.py:327
  13.0 1.7 %collective-permute-start.3 = (f32[16,128]{1,0:T(8,128)S(1)}, f32[16,128]{1,0:T(8,128)S(1)}, u32[]{:S(2)}, u32[]{:S(2)}) collective-permute-start(f32[16,128]{1,0:T(8,128)S(1)} %get-tuple-element.37.own_part), channel_id=1, source_target_pairs={{0,1},{1,0},{2,3},{3,2},{4,5},{5,4},{6,7},{7,6},{8,9},{9,8},{10,11... | collective-permute-start | bytes 24584 | tf_op jit(solution)/shard_map/ppermute | solution.py:327
  14.6 0.7 %collective-permute-start.9 = (bf16[1040,128]{1,0:T(8,128)(2,1)S(1)}, bf16[1040,128]{1,0:T(8,128)(2,1)S(1)}, u32[]{:S(2)}, u32[]{:S(2)}) collective-permute-start(bf16[1040,128]{1,0:T(8,128)(2,1)S(1)} %get-tuple-element.39), channel_id=1, source_target_pairs={{16,1},{17,2},{18,3},{19,4},{20,5},{21,6},{22,7},{23,8},{24,9},{25... | collective-permute-start | bytes 798728 | tf_op jit(solution)/shard_map/ppermute | solution.py:323
  15.3 2.6 %collective-permute-start.10 = (bf16[1040,128]{1,0:T(8,128)(2,1)S(1)}, bf16[1040,128]{1,0:T(8,128)(2,1)S(1)}, u32[]{:S(2)}, u32[]{:S(2)}) collective-permute-start(bf16[1040,128]{1,0:T(8,128)(2,1)S(1)} %get-tuple-element.40), channel_id=1, source_target_pairs={{17,0},{18,1},{19,2},{20,3},{21,4},{22,5},{23,6},{24,7},{25,8},{26... | collective-permute-start | bytes 798728 | tf_op jit(solution)/shard_map/ppermute | solution.py:323
  17.9 0.0 collective-permute-done.5
  17.9 0.0 collective-permute-done.4
  18.0 3.7 %collective-permute-start.8 = (f32[16,128]{1,0:T(8,128)S(1)}, f32[16,128]{1,0:T(8,128)S(1)}, u32[]{:S(2)}, u32[]{:S(2)}) collective-permute-start(f32[16,128]{1,0:T(8,128)S(1)} %pad_maximum_fusion.refs_0_), channel_id=1, source_target_pairs={{0,12},{1,13},{2,14},{3,15},{4,8},{5,9},{6,10},{7,11},{8,4},{9,5},... | collective-permute-start | bytes 24584 | tf_op jit(solution)/shard_map/ppermute | solution.py:327
  21.7 0.0 collective-permute-start.7
  21.7 0.8 %collective-permute-start.6 = (f32[16,128]{1,0:T(8,128)S(1)}, f32[16,128]{1,0:T(8,128)S(1)}, u32[]{:S(2)}, u32[]{:S(2)}) collective-permute-start(f32[16,128]{1,0:T(8,128)S(1)} %pad_maximum_fusion.refs_0_), channel_id=1, source_target_pairs={{0,4},{1,5},{2,6},{3,7},{4,0},{5,1},{6,2},{7,3},{8,12},{9,13},{10,... | collective-permute-start | bytes 24584 | tf_op jit(solution)/shard_map/ppermute | solution.py:327
  22.4 1.1 %collective-permute-done.8.refs_3_ = f32[16,128]{1,0:T(8,128)S(1)} collective-permute-done((f32[16,128]{1,0:T(8,128)S(1)}, f32[16,128]{1,0:T(8,128)S(1)}, u32[]{:S(2)}, u32[]{:S(2)}) %collective-permute-start.8) | collective-permute-done | bytes 8224 | tf_op jit(solution)/shard_map/ppermute | solution.py:327
  23.6 2.6 %collective-permute-done.7.refs_2_ = f32[16,128]{1,0:T(8,128)S(1)} collective-permute-done((f32[16,128]{1,0:T(8,128)S(1)}, f32[16,128]{1,0:T(8,128)S(1)}, u32[]{:S(2)}, u32[]{:S(2)}) %collective-permute-start.7) | collective-permute-done | bytes 8224 | tf_op jit(solution)/shard_map/ppermute | solution.py:327
  26.3 0.1 collective-permute-start.11
  26.3 0.5 %collective-permute-start.12 = (bf16[1040,128]{1,0:T(8,128)(2,1)S(1)}, bf16[1040,128]{1,0:T(8,128)(2,1)S(1)}, u32[]{:S(2)}, u32[]{:S(2)}) collective-permute-start(bf16[1040,128]{1,0:T(8,128)(2,1)S(1)} %get-tuple-element.45.back_right), channel_id=1, source_target_pairs={{0,16},{1,17},{2,18},{3,19},{4,20},{5,21},{6,22},{7,23},{8,24},{9,... | collective-permute-start | bytes 798728 | tf_op jit(solution)/shard_map/ppermute | solution.py:323
  26.8 1.0 %collective-permute-done.11.swap_left = bf16[1040,128]{1,0:T(8,128)(2,1)S(1)} collective-permute-done((bf16[1040,128]{1,0:T(8,128)(2,1)S(1)}, bf16[1040,128]{1,0:T(8,128)(2,1)S(1)}, u32[]{:S(2)}, u32[]{:S(2)}) %collective-permute-start.11) | collective-permute-done | bytes 266272 | tf_op jit(solution)/shard_map/ppermute | solution.py:323
  27.9 0.4 %collective-permute-done.12.swap_right = bf16[1040,128]{1,0:T(8,128)(2,1)S(1)} collective-permute-done((bf16[1040,128]{1,0:T(8,128)(2,1)S(1)}, bf16[1040,128]{1,0:T(8,128)(2,1)S(1)}, u32[]{:S(2)}, u32[]{:S(2)}) %collective-permute-start.12) | collective-permute-done | bytes 266272 | tf_op jit(solution)/shard_map/ppermute | solution.py:323
  28.3 2.0 %pull_second_normalise.1 = (bf16[1,128,512]{2,1,0:T(8,128)(2,1)}, bf16[1,128,512]{2,1,0:T(8,128)(2,1)}) custom-call(s32[2,64]{1,0:T(2,128)S(1)} %get-tuple-element.28.table_ref, f32[16,128]{1,0:T(8,128)S(1)} %get-tuple-element.41.whole, f32[16,128]{1,0:T(8,128)S(1)} %get-tuple-element.37.own_part, f32[512,128]{1,0:T(8,128)S(1)} %get-tuple-element.42.keep_first, ...), custom_call_target="tpu_custom_call" | custom-call | tf_op jit(solution)/shard_map/pull_second_normalise/pallas_call | solution.py:427
  (9 shorter events, 0.1 us)
Async XLA Ops:
  3.1 6.7 %collective-permute-start = (bf16[544,128]{1,0:T(8,128)(2,1)S(1)}, bf16[544,128]{1,0:T(8,128)(2,1)S(1)}, u32[]{:S(2)}, u32[]{:S(2)}) collective-permute-start(bf16[544,128]{1,0:T(8,128)(2,1)S(1)} %get-tuple-element.31), channel_id=1, source_target_pairs={{0,17},{1,18},{2,19},{3,20},{4,21},{5,22},{6,23},{7,24},{8,25},{9,... | collective-permute-start | bytes 417800 | tf_op jit(solution)/shard_map/ppermute | solution.py:323
  5.0 6.0 %collective-permute-start.2 = (bf16[544,128]{1,0:T(8,128)(2,1)S(1)}, bf16[544,128]{1,0:T(8,128)(2,1)S(1)}, u32[]{:S(2)}, u32[]{:S(2)}) collective-permute-start(bf16[544,128]{1,0:T(8,128)(2,1)S(1)} %get-tuple-element.33), channel_id=1, source_target_pairs={{1,16},{2,17},{3,18},{4,19},{5,20},{6,21},{7,22},{8,23},{9,24},{10... | collective-permute-start | bytes 417800 | tf_op jit(solution)/shard_map/ppermute | solution.py:323
  8.5 1.3 %collective-permute-start.1 = (bf16[512,128]{1,0:T(8,128)(2,1)S(1)}, bf16[512,128]{1,0:T(8,128)(2,1)S(1)}, u32[]{:S(2)}, u32[]{:S(2)}) collective-permute-start(bf16[512,128]{1,0:T(8,128)(2,1)S(1)} %get-tuple-element.32), channel_id=1, source_target_pairs={{0,16},{1,17},{2,18},{3,19},{4,20},{5,21},{6,22},{7,23},{8,24},{9,... | collective-permute-start | bytes 393224 | tf_op jit(solution)/shard_map/ppermute | solution.py:323
  11.1 6.9 %collective-permute-start.5 = (f32[16,128]{1,0:T(8,128)S(1)}, f32[16,128]{1,0:T(8,128)S(1)}, u32[]{:S(2)}, u32[]{:S(2)}) collective-permute-start(f32[16,128]{1,0:T(8,128)S(1)} %get-tuple-element.37.own_part), channel_id=1, source_target_pairs={{0,3},{1,2},{2,1},{3,0},{4,7},{5,6},{6,5},{7,4},{8,11},{9,10},{10,... | collective-permute-start | bytes 24584 | tf_op jit(solution)/shard_map/ppermute | solution.py:327
  11.1 6.8 %collective-permute-start.4 = (f32[16,128]{1,0:T(8,128)S(1)}, f32[16,128]{1,0:T(8,128)S(1)}, u32[]{:S(2)}, u32[]{:S(2)}) collective-permute-start(f32[16,128]{1,0:T(8,128)S(1)} %get-tuple-element.37.own_part), channel_id=1, source_target_pairs={{0,2},{1,3},{2,0},{3,1},{4,6},{5,7},{6,4},{7,5},{8,10},{9,11},{10,... | collective-permute-start | bytes 24584 | tf_op jit(solution)/shard_map/ppermute | solution.py:327
  13.0 5.0 %collective-permute-start.3 = (f32[16,128]{1,0:T(8,128)S(1)}, f32[16,128]{1,0:T(8,128)S(1)}, u32[]{:S(2)}, u32[]{:S(2)}) collective-permute-start(f32[16,128]{1,0:T(8,128)S(1)} %get-tuple-element.37.own_part), channel_id=1, source_target_pairs={{0,1},{1,0},{2,3},{3,2},{4,5},{5,4},{6,7},{7,6},{8,9},{9,8},{10,11... | collective-permute-start | bytes 24584 | tf_op jit(solution)/shard_map/ppermute | solution.py:327
  14.6 11.6 %collective-permute-start.9 = (bf16[1040,128]{1,0:T(8,128)(2,1)S(1)}, bf16[1040,128]{1,0:T(8,128)(2,1)S(1)}, u32[]{:S(2)}, u32[]{:S(2)}) collective-permute-start(bf16[1040,128]{1,0:T(8,128)(2,1)S(1)} %get-tuple-element.39), channel_id=1, source_target_pairs={{16,1},{17,2},{18,3},{19,4},{20,5},{21,6},{22,7},{23,8},{24,9},{25... | collective-permute-start | bytes 798728 | tf_op jit(solution)/shard_map/ppermute | solution.py:323
  15.3 10.9 %collective-permute-start.10 = (bf16[1040,128]{1,0:T(8,128)(2,1)S(1)}, bf16[1040,128]{1,0:T(8,128)(2,1)S(1)}, u32[]{:S(2)}, u32[]{:S(2)}) collective-permute-start(bf16[1040,128]{1,0:T(8,128)(2,1)S(1)} %get-tuple-element.40), channel_id=1, source_target_pairs={{17,0},{18,1},{19,2},{20,3},{21,4},{22,5},{23,6},{24,7},{25,8},{26... | collective-permute-start | bytes 798728 | tf_op jit(solution)/shard_map/ppermute | solution.py:323
  18.0 5.6 %collective-permute-start.8 = (f32[16,128]{1,0:T(8,128)S(1)}, f32[16,128]{1,0:T(8,128)S(1)}, u32[]{:S(2)}, u32[]{:S(2)}) collective-permute-start(f32[16,128]{1,0:T(8,128)S(1)} %pad_maximum_fusion.refs_0_), channel_id=1, source_target_pairs={{0,12},{1,13},{2,14},{3,15},{4,8},{5,9},{6,10},{7,11},{8,4},{9,5},... | collective-permute-start | bytes 24584 | tf_op jit(solution)/shard_map/ppermute | solution.py:327
  21.7 4.5 %collective-permute-start.7 = (f32[16,128]{1,0:T(8,128)S(1)}, f32[16,128]{1,0:T(8,128)S(1)}, u32[]{:S(2)}, u32[]{:S(2)}) collective-permute-start(f32[16,128]{1,0:T(8,128)S(1)} %pad_maximum_fusion.refs_0_), channel_id=1, source_target_pairs={{0,8},{1,9},{2,10},{3,11},{4,12},{5,13},{6,14},{7,15},{8,0},{9,1},... | collective-permute-start | bytes 24584 | tf_op jit(solution)/shard_map/ppermute | solution.py:327
  21.7 4.5 %collective-permute-start.6 = (f32[16,128]{1,0:T(8,128)S(1)}, f32[16,128]{1,0:T(8,128)S(1)}, u32[]{:S(2)}, u32[]{:S(2)}) collective-permute-start(f32[16,128]{1,0:T(8,128)S(1)} %pad_maximum_fusion.refs_0_), channel_id=1, source_target_pairs={{0,4},{1,5},{2,6},{3,7},{4,0},{5,1},{6,2},{7,3},{8,12},{9,13},{10,... | collective-permute-start | bytes 24584 | tf_op jit(solution)/shard_map/ppermute | solution.py:327
  26.3 1.6 %collective-permute-start.11 = (bf16[1040,128]{1,0:T(8,128)(2,1)S(1)}, bf16[1040,128]{1,0:T(8,128)(2,1)S(1)}, u32[]{:S(2)}, u32[]{:S(2)}) collective-permute-start(bf16[1040,128]{1,0:T(8,128)(2,1)S(1)} %get-tuple-element.44.back_left), channel_id=1, source_target_pairs={{0,16},{1,17},{2,18},{3,19},{4,20},{5,21},{6,22},{7,23},{8,24},{9,... | collective-permute-start | bytes 798728 | tf_op jit(solution)/shard_map/ppermute | solution.py:323
  26.3 1.9 %collective-permute-start.12 = (bf16[1040,128]{1,0:T(8,128)(2,1)S(1)}, bf16[1040,128]{1,0:T(8,128)(2,1)S(1)}, u32[]{:S(2)}, u32[]{:S(2)}) collective-permute-start(bf16[1040,128]{1,0:T(8,128)(2,1)S(1)} %get-tuple-element.45.back_right), channel_id=1, source_target_pairs={{0,16},{1,17},{2,18},{3,19},{4,20},{5,21},{6,22},{7,23},{8,24},{9,... | collective-permute-start | bytes 798728 | tf_op jit(solution)/shard_map/ppermute | solution.py:323

commit v5 on v4

--- a/solution.py
+++ b/solution.py
@@ -10,9 +10,6 @@
 BAND_REACH = 4
 LABEL_ROWS = 16
 CHUNKS = 2
-XA = ("inc", "chain", "full")
-XB = ("inc", "chain", "full")
-XC = "full"
 
 
 def rows_of(block, side):
@@ -248,24 +245,26 @@
 
 
 def combine_kernel(count, *refs):
-    mine, out, to_swap, sem = refs[count], refs[count + 3], refs[count + 4], refs[count + 6]
-    copy = pltpu.make_async_copy(mine, to_swap.at[pl.ds(0, mine.shape[0])], sem)
+    mine, back_left, back_right, out, to_swap = refs[count:]
+    inner = mine.shape[0] // 2
+    rest = back_left.shape[0] - inner
+
+    @pl.when(lax.axis_index("tm") == 0)
+    def _():
+        to_swap[0:rest, :] = back_left[inner:, :]
+        to_swap[rest : 2 * rest, :] = back_right[inner:, :]
 
     @pl.when(lax.axis_index("tm") != 0)
     def _():
-        copy.start()
+        to_swap[0 : 2 * inner, :] = mine[...]
 
     total, top = combined([part[...] for part in refs[:count]])
     out[0:8, :] = total
     out[8:16, :] = top
 
-    @pl.when(lax.axis_index("tm") != 0)
-    def _():
-        copy.wait()
-
-
-def last_kernel(own, all_cells, table_ref, whole, own_part, keep_first, keep_second, back_left, back_right, swap_left,
-                swap_right, mine_ref, blk, mass_ref, fate_ref, table, fated, pulled, sem):
+
+def last_kernel(own, all_cells, table_ref, whole, own_part, keep_first, keep_second, back_left, back_right, swap,
+                mine_ref, blk, mass_ref, fate_ref, table, fated, pulled, sem):
     side = blk.shape[1]
     reach, inner = BAND_REACH * side, own * side
     here = lax.axis_index("cell")
@@ -276,12 +275,12 @@
         table_copy = pltpu.make_async_copy(table_ref, table, sem)
         table_copy.start()
         fated[0:reach, :] = back_left[0:reach, :]
-        fated[reach : reach + inner, :] = swap_left[0:inner, :]
+        fated[reach : reach + inner, :] = swap[0:inner, :]
         fated[reach + inner :, :] = back_right[0:reach, :]
         scale = all_cells / as_column(total[0:1], side)
         for b in range(own):
             at = pl.ds(b * side, side)
-            mass = keep_first[at, :] + swap_left[pl.ds(inner + b * side, side), :].astype(jnp.float32)
+            mass = keep_first[at, :] + swap[pl.ds(inner + b * side, side), :].astype(jnp.float32)
             mass_ref[0, :, at] = (mass * scale).astype(jnp.bfloat16)
         table_copy.wait()
         pull_backward(table, fated, blk, pulled, own)
@@ -292,35 +291,28 @@
     @pl.when(lax.axis_index("tm") != 0)
     def _():
         has_left, has_right = here > 0, here < lax.axis_size("cell") - 1
-        power = pl.ds(inner + reach, 16)
         scale = all_cells / as_column(total[0:1], side)
         own_scale = as_column(jnp.exp2(own_part[8:9] - top[0:1]), side)
-        left_scale = as_column(jnp.exp2(swap_left[power, :][0:1].astype(jnp.float32) - top[0:1]), side)
-        right_scale = as_column(jnp.exp2(swap_right[power, :][0:1].astype(jnp.float32) - top[0:1]), side)
-        for b in range(own):
-            at = pl.ds(b * side, side)
-            aside = pl.ds(inner + b * side, side)
+        left_scale = as_column(jnp.exp2(swap[pl.ds(reach, 16), :][0:1].astype(jnp.float32) - top[0:1]), side)
+        right_scale = as_column(jnp.exp2(swap[pl.ds(2 * reach + 16, 16), :][0:1].astype(jnp.float32) - top[0:1]), side)
+        for b in range(own):
+            at = pl.ds(b * side, side)
+            on_right = pl.ds(reach + 16 + b * side, side)
             mass = keep_second[at, :] * own_scale
-            mass += jnp.where(has_left, swap_left[aside, :].astype(jnp.float32) * left_scale, 0.0)
-            mass += jnp.where(has_right, swap_right[aside, :].astype(jnp.float32) * right_scale, 0.0)
+            mass += jnp.where(has_left, swap[at, :].astype(jnp.float32) * left_scale, 0.0)
+            mass += jnp.where(has_right, swap[on_right, :].astype(jnp.float32) * right_scale, 0.0)
             mass_ref[0, :, at] = (mass * scale).astype(jnp.bfloat16)
             fate_ref[0, :, at] = mine_ref[at, :]
 
 
-def across(array, distance, sender, mode):
+def across(array, distance, sender, both=False):
     count = lax.axis_size("cell")
     at = lambda core, c: core * count + c
     other = 1 - sender
-    route = {at(sender, c): at(other, c + distance) for c in range(count) if 0 <= c + distance < count}
-    if mode == "full":
-        for c in range(count):
-            route[at(other, c)] = at(sender, c - distance) if 0 <= c - distance < count else at(other, c)
-            route.setdefault(at(sender, c), at(sender, c))
-    if mode == "chain":
-        for c in range(count):
-            route[at(other, c)] = at(sender, c)
-            route.setdefault(at(sender, c), at(other, (c + distance) % count))
-    return lax.ppermute(array, ("tm", "cell"), list(route.items()))
+    route = [(at(sender, c), at(other, c + distance)) for c in range(count) if 0 <= c + distance < count]
+    if both:
+        route += [(there, here) for here, there in route]
+    return lax.ppermute(array, ("tm", "cell"), route)
 
 
 def flipped(array, bits):
@@ -369,9 +361,9 @@
         name="push_first",
     )(*inputs)
 
-    from_left = across(right, 1, 0, XA[0])
-    from_right = across(left, -1, 0, XA[1])
-    from_mid = across(mid, 0, 0, XA[2])
+    from_left = across(right, 1, 0)
+    from_right = across(left, -1, 0)
+    from_mid = across(mid, 0, 0, both=True)
 
     table, rates, known, blocks, half = pl.pallas_call(
         functools.partial(prepare_kernel, own),
@@ -400,8 +392,8 @@
         name="push_second_pull_first",
     )(table, rates, known, from_left, from_mid, from_right, part, half, blocks)
 
-    back_left = across(to_right, 1, 1, XB[0])
-    back_right = across(to_left, -1, 1, XB[1])
+    back_left = across(to_right, 1, 1)
+    back_right = across(to_left, -1, 1)
 
     whole = part
     bit = 1
@@ -410,24 +402,21 @@
             whole = jnp.concatenate(combined(parts), axis=0)
         parts = [whole] + [flipped(whole, k * bit) for k in range(1, 4) if k * bit < cell_count]
         bit *= 4
-    whole, back_left, back_right = pl.pallas_call(
+    whole, to_swap = pl.pallas_call(
         functools.partial(combine_kernel, len(parts)),
-        out_shape=(f32(16, side), bf16(inner + reach + 16, side), bf16(inner + reach + 16, side)),
-        in_specs=[vmem] * len(parts) + [anywhere] * 3,
-        out_specs=[vmem] + [anywhere] * 2,
-        scratch_shapes=[sem],
-        input_output_aliases={len(parts) + 1: 1, len(parts) + 2: 2},
+        out_shape=(f32(16, side), bf16(2 * max(inner, reach + 16), side)),
+        in_specs=[vmem] * (len(parts) + 3),
+        out_specs=[vmem] * 2,
         compiler_params=params,
         name="combine",
     )(*parts, to_mid, back_left, back_right)
 
-    swap_left = across(back_left, 0, 0, XC)
-    swap_right = across(back_right, 0, 0, XC)
+    swap = across(to_swap, 0, 0, both=True)
 
     forward_mass, fate = pl.pallas_call(
         functools.partial(last_kernel, own, float(cells * cell_count)),
         out_shape=(bf16(1, height, cells), bf16(1, height, cells)),
-        in_specs=[vmem] * 11,
+        in_specs=[vmem] * 10,
         out_specs=[vmem] * 2,
         scratch_shapes=[
             pltpu.SMEM((2, slots), jnp.int32), pltpu.VMEM((window * side, side), jnp.bfloat16),
@@ -435,7 +424,7 @@
         ],
         compiler_params=params,
         name="pull_second_normalise",
-    )(table, whole, part, keep_first, keep_second, back_left, back_right, swap_left, swap_right, to_mid, blocks)
+    )(table, whole, part, keep_first, keep_second, back_left, back_right, swap, to_mid, blocks)
     return forward_mass, fate
 
 

time: 30.4 us -> 30.1 us (level)
  starting transfers between devices: 17.2 us -> 15.2 us
  waiting for transfers between devices: 7.71 us -> 9.31 us
    ppermute x7 -> x6, starting transfers between devices: 9.17 us -> 5.34 us  [across(): return lax.ppermute(array, ('tm', 'cell'), route)]
    ppermute x6, starting transfers between devices: 8 us -> 9.84 us  [flipped(): lax.ppermute(array, 'cell', [(c, c ^ bits) for c in range(lax.axis_size('...]
    ppermute x6, waiting for transfers between devices: 3.78 us -> 5.55 us  [flipped(): lax.ppermute(array, 'cell', [(c, c ^ bits) for c in range(lax.axis_size('...]
    ppermute x7 -> x6, waiting for transfers between devices: 3.93 us -> 3.76 us  [across(): return lax.ppermute(array, ('tm', 'cell'), route)]
  transfers between devices with their start and end apart: 13 -> 12, of which waited for: 6 -> 8; matrix products, arithmetic and copies ran while one was open for 0% -> 0% of each run, Pallas kernels for 0% -> 0%
where the time goes in v5:
time: 30.1 us; the launch traced here: 29.9 us
  starting transfers between devices  15.2 us (50%)
  waiting for transfers between devices  9.31 us (31%)
  Pallas kernels  4.66 us (15%)
  between operations  0.72 us (2%)
    ppermute x6, starting transfers between devices, flipped(): lax.ppermute(array, 'cell', [(c, c ^ bits) for c in range(lax.axis_size('...  9.84 us
    ppermute x6, waiting for transfers between devices, flipped(): lax.ppermute(array, 'cell', [(c, c ^ bits) for c in range(lax.axis_size('...  5.55 us
    ppermute x6, starting transfers between devices, across(): return lax.ppermute(array, ('tm', 'cell'), route)  5.34 us
    ppermute x6, waiting for transfers between devices, across(): return lax.ppermute(array, ('tm', 'cell'), route)  3.76 us
    pallas_call x1, Pallas kernels, on_device(): pl.pallas_call(functools.partial(first_kernel, own), out_shape=(bf16(reac...  2.51 us
    pallas_call x1, Pallas kernels, on_device(): pl.pallas_call(functools.partial(last_kernel, own, float(cells * cell_cou...  2.01 us
  transfers between devices with their start and end apart: 12, of which 8 were waited for; matrix products, arithmetic and copies ran while one was open for 0% of the time, Pallas kernels for 0%

profile of v5, /device:TPU:0, one launch (start us, length us, event | category | flops | bytes accessed | tf_op | source)
XLA Modules:
  0.0 29.9 jit_solution(8778363110044587396)
XLA Ops:
  0.6 2.5 %push_first.1 = (bf16[544,128]{1,0:T(8,128)(2,1)S(1)}, bf16[512,128]{1,0:T(8,128)(2,1)S(1)}, bf16[544,128]{1,0:T(8,128)(2,1)S(1)}, f32[512,128]{1,0:T(8,128)S(1)...) custom-call(s32[1,64]{1,0:T(1,128)} %rows_hbm.3, ...), custom_call_target="tpu_custom_call" | custom-call | tf_op jit(solution)/shard_map/push_first/pallas_call | solution.py:348
  3.1 1.9 %collective-permute-start = (bf16[544,128]{1,0:T(8,128)(2,1)S(1)}, bf16[544,128]{1,0:T(8,128)(2,1)S(1)}, u32[]{:S(2)}, u32[]{:S(2)}) collective-permute-start(bf16[544,128]{1,0:T(8,128)(2,1)S(1)} %get-tuple-element.30), channel_id=1, source_target_pairs={{0,17},{1,18},{2,19},{3,20},{4,21},{5,22},{6,23},{7,24},{8,25},{9,... | collective-permute-start | bytes 417800 | tf_op jit(solution)/shard_map/ppermute | solution.py:315
  5.0 0.7 %collective-permute-start.2 = (bf16[544,128]{1,0:T(8,128)(2,1)S(1)}, bf16[544,128]{1,0:T(8,128)(2,1)S(1)}, u32[]{:S(2)}, u32[]{:S(2)}) collective-permute-start(bf16[544,128]{1,0:T(8,128)(2,1)S(1)} %get-tuple-element.32), channel_id=1, source_target_pairs={{1,16},{2,17},{3,18},{4,19},{5,20},{6,21},{7,22},{8,23},{9,24},{10... | collective-permute-start | bytes 417800 | tf_op jit(solution)/shard_map/ppermute | solution.py:315
  5.7 0.1 collective-permute-start.1
  5.8 0.1 prepare.1
  5.9 1.2 %collective-permute-done.1.mid_ref = bf16[512,128]{1,0:T(8,128)(2,1)S(1)} collective-permute-done((bf16[512,128]{1,0:T(8,128)(2,1)S(1)}, bf16[512,128]{1,0:T(8,128)(2,1)S(1)}, u32[]{:S(2)}, u32[]{:S(2)}) %collective-permute-start.1) | collective-permute-done | bytes 131104 | tf_op jit(solution)/shard_map/ppermute | solution.py:315
  7.1 0.5 %collective-permute-done.left_ref = bf16[544,128]{1,0:T(8,128)(2,1)S(1)} collective-permute-done((bf16[544,128]{1,0:T(8,128)(2,1)S(1)}, bf16[544,128]{1,0:T(8,128)(2,1)S(1)}, u32[]{:S(2)}, u32[]{:S(2)}) %collective-permute-start) | collective-permute-done | bytes 139296 | tf_op jit(solution)/shard_map/ppermute | solution.py:315
  7.6 0.0 collective-permute-done.2.right_ref
  7.6 4.7 %collective-permute-start.5 = (f32[16,128]{1,0:T(8,128)S(1)}, f32[16,128]{1,0:T(8,128)S(1)}, u32[]{:S(2)}, u32[]{:S(2)}) collective-permute-start(f32[16,128]{1,0:T(8,128)S(1)} %get-tuple-element.36.own_part), channel_id=1, source_target_pairs={{0,3},{1,2},{2,1},{3,0},{4,7},{5,6},{6,5},{7,4},{8,11},{9,10},{10,... | collective-permute-start | bytes 24584 | tf_op jit(solution)/shard_map/ppermute | solution.py:319
  12.3 0.7 %collective-permute-start.4 = (f32[16,128]{1,0:T(8,128)S(1)}, f32[16,128]{1,0:T(8,128)S(1)}, u32[]{:S(2)}, u32[]{:S(2)}) collective-permute-start(f32[16,128]{1,0:T(8,128)S(1)} %get-tuple-element.36.own_part), channel_id=1, source_target_pairs={{0,2},{1,3},{2,0},{3,1},{4,6},{5,7},{6,4},{7,5},{8,10},{9,11},{10,... | collective-permute-start | bytes 24584 | tf_op jit(solution)/shard_map/ppermute | solution.py:319
  13.0 0.0 collective-permute-start.3
  13.0 0.7 %collective-permute-start.9 = (bf16[1040,128]{1,0:T(8,128)(2,1)S(1)}, bf16[1040,128]{1,0:T(8,128)(2,1)S(1)}, u32[]{:S(2)}, u32[]{:S(2)}) collective-permute-start(bf16[1040,128]{1,0:T(8,128)(2,1)S(1)} %get-tuple-element.38), channel_id=1, source_target_pairs={{16,1},{17,2},{18,3},{19,4},{20,5},{21,6},{22,7},{23,8},{24,9},{25... | collective-permute-start | bytes 798728 | tf_op jit(solution)/shard_map/ppermute | solution.py:315
  13.7 1.3 %collective-permute-start.10 = (bf16[1040,128]{1,0:T(8,128)(2,1)S(1)}, bf16[1040,128]{1,0:T(8,128)(2,1)S(1)}, u32[]{:S(2)}, u32[]{:S(2)}) collective-permute-start(bf16[1040,128]{1,0:T(8,128)(2,1)S(1)} %get-tuple-element.39), channel_id=1, source_target_pairs={{17,0},{18,1},{19,2},{20,3},{21,4},{22,5},{23,6},{24,7},{25,8},{26... | collective-permute-start | bytes 798728 | tf_op jit(solution)/shard_map/ppermute | solution.py:315
  15.0 1.0 %collective-permute-done.4 = f32[16,128]{1,0:T(8,128)S(1)} collective-permute-done((f32[16,128]{1,0:T(8,128)S(1)}, f32[16,128]{1,0:T(8,128)S(1)}, u32[]{:S(2)}, u32[]{:S(2)}) %collective-permute-start.4) | collective-permute-done | bytes 8224 | tf_op jit(solution)/shard_map/ppermute | solution.py:319
  16.0 0.7 %collective-permute-done.3 = f32[16,128]{1,0:T(8,128)S(1)} collective-permute-done((f32[16,128]{1,0:T(8,128)S(1)}, f32[16,128]{1,0:T(8,128)S(1)}, u32[]{:S(2)}, u32[]{:S(2)}) %collective-permute-start.3) | collective-permute-done | bytes 8224 | tf_op jit(solution)/shard_map/ppermute | solution.py:319
  16.7 3.7 %collective-permute-start.8 = (f32[16,128]{1,0:T(8,128)S(1)}, f32[16,128]{1,0:T(8,128)S(1)}, u32[]{:S(2)}, u32[]{:S(2)}) collective-permute-start(f32[16,128]{1,0:T(8,128)S(1)} %pad_maximum_fusion.refs_0_), channel_id=1, source_target_pairs={{0,12},{1,13},{2,14},{3,15},{4,8},{5,9},{6,10},{7,11},{8,4},{9,5},... | collective-permute-start | bytes 24584 | tf_op jit(solution)/shard_map/ppermute | solution.py:319
  20.3 0.8 %collective-permute-start.6 = (f32[16,128]{1,0:T(8,128)S(1)}, f32[16,128]{1,0:T(8,128)S(1)}, u32[]{:S(2)}, u32[]{:S(2)}) collective-permute-start(f32[16,128]{1,0:T(8,128)S(1)} %pad_maximum_fusion.refs_0_), channel_id=1, source_target_pairs={{0,4},{1,5},{2,6},{3,7},{4,0},{5,1},{6,2},{7,3},{8,12},{9,13},{10,... | collective-permute-start | bytes 24584 | tf_op jit(solution)/shard_map/ppermute | solution.py:319
  21.1 1.2 %collective-permute-done.8.refs_3_ = f32[16,128]{1,0:T(8,128)S(1)} collective-permute-done((f32[16,128]{1,0:T(8,128)S(1)}, f32[16,128]{1,0:T(8,128)S(1)}, u32[]{:S(2)}, u32[]{:S(2)}) %collective-permute-start.8) | collective-permute-done | bytes 8224 | tf_op jit(solution)/shard_map/ppermute | solution.py:319
  22.3 2.7 %collective-permute-done.7.refs_2_ = f32[16,128]{1,0:T(8,128)S(1)} collective-permute-done((f32[16,128]{1,0:T(8,128)S(1)}, f32[16,128]{1,0:T(8,128)S(1)}, u32[]{:S(2)}, u32[]{:S(2)}) %collective-permute-start.7) | collective-permute-done | bytes 8224 | tf_op jit(solution)/shard_map/ppermute | solution.py:319
  25.0 0.0 collective-permute-done.6.refs_1_
  25.0 0.9 %collective-permute-done.10.refs_6_.back_right = bf16[1040,128]{1,0:T(8,128)(2,1)S(1)} collective-permute-done((bf16[1040,128]{1,0:T(8,128)(2,1)S(1)}, bf16[1040,128]{1,0:T(8,128)(2,1)S(1)}, u32[]{:S(2)}, u32[]{:S(2)}) %collective-permute-start.10) | collective-permute-done | bytes 266272 | tf_op jit(solution)/shard_map/ppermute | solution.py:315
  25.9 0.8 %collective-permute-start.11 = (bf16[1056,128]{1,0:T(8,128)(2,1)S(1)}, bf16[1056,128]{1,0:T(8,128)(2,1)S(1)}, u32[]{:S(2)}, u32[]{:S(2)}) collective-permute-start(bf16[1056,128]{1,0:T(8,128)(2,1)S(1)} %get-tuple-element.43), channel_id=1, source_target_pairs={{0,16},{1,17},{2,18},{3,19},{4,20},{5,21},{6,22},{7,23},{8,24},{9,... | collective-permute-start | bytes 811016 | tf_op jit(solution)/shard_map/ppermute | solution.py:315
  26.7 1.2 %collective-permute-done.11.swap = bf16[1056,128]{1,0:T(8,128)(2,1)S(1)} collective-permute-done((bf16[1056,128]{1,0:T(8,128)(2,1)S(1)}, bf16[1056,128]{1,0:T(8,128)(2,1)S(1)}, u32[]{:S(2)}, u32[]{:S(2)}) %collective-permute-start.11) | collective-permute-done | bytes 270368 | tf_op jit(solution)/shard_map/ppermute | solution.py:315
  27.9 2.0 %pull_second_normalise.1 = (bf16[1,128,512]{2,1,0:T(8,128)(2,1)}, bf16[1,128,512]{2,1,0:T(8,128)(2,1)}) custom-call(s32[2,64]{1,0:T(2,128)S(1)} %get-tuple-element.27.table_ref, f32[16,128]{1,0:T(8,128)S(1)} %get-tuple-element.40.whole, f32[16,128]{1,0:T(8,128)S(1)} %get-tuple-element.36.own_part, f32[512,128]{1,0:T(8,128)S(1)} %get-tuple-element.41.keep_first, ...), custom_call_target="tpu_custom_call" | custom-call | tf_op jit(solution)/shard_map/pull_second_normalise/pallas_call | solution.py:416
  (7 shorter events, 0.1 us)
Async XLA Ops:
  3.1 4.5 %collective-permute-start = (bf16[544,128]{1,0:T(8,128)(2,1)S(1)}, bf16[544,128]{1,0:T(8,128)(2,1)S(1)}, u32[]{:S(2)}, u32[]{:S(2)}) collective-permute-start(bf16[544,128]{1,0:T(8,128)(2,1)S(1)} %get-tuple-element.30), channel_id=1, source_target_pairs={{0,17},{1,18},{2,19},{3,20},{4,21},{5,22},{6,23},{7,24},{8,25},{9,... | collective-permute-start | bytes 417800 | tf_op jit(solution)/shard_map/ppermute | solution.py:315
  5.0 2.6 %collective-permute-start.2 = (bf16[544,128]{1,0:T(8,128)(2,1)S(1)}, bf16[544,128]{1,0:T(8,128)(2,1)S(1)}, u32[]{:S(2)}, u32[]{:S(2)}) collective-permute-start(bf16[544,128]{1,0:T(8,128)(2,1)S(1)} %get-tuple-element.32), channel_id=1, source_target_pairs={{1,16},{2,17},{3,18},{4,19},{5,20},{6,21},{7,22},{8,23},{9,24},{10... | collective-permute-start | bytes 417800 | tf_op jit(solution)/shard_map/ppermute | solution.py:315
  5.7 1.4 %collective-permute-start.1 = (bf16[512,128]{1,0:T(8,128)(2,1)S(1)}, bf16[512,128]{1,0:T(8,128)(2,1)S(1)}, u32[]{:S(2)}, u32[]{:S(2)}) collective-permute-start(bf16[512,128]{1,0:T(8,128)(2,1)S(1)} %get-tuple-element.31), channel_id=1, source_target_pairs={{0,16},{1,17},{2,18},{3,19},{4,20},{5,21},{6,22},{7,23},{8,24},{9,... | collective-permute-start | bytes 393224 | tf_op jit(solution)/shard_map/ppermute | solution.py:315
  7.6 7.4 %collective-permute-start.5 = (f32[16,128]{1,0:T(8,128)S(1)}, f32[16,128]{1,0:T(8,128)S(1)}, u32[]{:S(2)}, u32[]{:S(2)}) collective-permute-start(f32[16,128]{1,0:T(8,128)S(1)} %get-tuple-element.36.own_part), channel_id=1, source_target_pairs={{0,3},{1,2},{2,1},{3,0},{4,7},{5,6},{6,5},{7,4},{8,11},{9,10},{10,... | collective-permute-start | bytes 24584 | tf_op jit(solution)/shard_map/ppermute | solution.py:319
  12.3 3.7 %collective-permute-start.4 = (f32[16,128]{1,0:T(8,128)S(1)}, f32[16,128]{1,0:T(8,128)S(1)}, u32[]{:S(2)}, u32[]{:S(2)}) collective-permute-start(f32[16,128]{1,0:T(8,128)S(1)} %get-tuple-element.36.own_part), channel_id=1, source_target_pairs={{0,2},{1,3},{2,0},{3,1},{4,6},{5,7},{6,4},{7,5},{8,10},{9,11},{10,... | collective-permute-start | bytes 24584 | tf_op jit(solution)/shard_map/ppermute | solution.py:319
  13.0 3.7 %collective-permute-start.3 = (f32[16,128]{1,0:T(8,128)S(1)}, f32[16,128]{1,0:T(8,128)S(1)}, u32[]{:S(2)}, u32[]{:S(2)}) collective-permute-start(f32[16,128]{1,0:T(8,128)S(1)} %get-tuple-element.36.own_part), channel_id=1, source_target_pairs={{0,1},{1,0},{2,3},{3,2},{4,5},{5,4},{6,7},{7,6},{8,9},{9,8},{10,11... | collective-permute-start | bytes 24584 | tf_op jit(solution)/shard_map/ppermute | solution.py:319
  13.0 12.0 %collective-permute-start.9 = (bf16[1040,128]{1,0:T(8,128)(2,1)S(1)}, bf16[1040,128]{1,0:T(8,128)(2,1)S(1)}, u32[]{:S(2)}, u32[]{:S(2)}) collective-permute-start(bf16[1040,128]{1,0:T(8,128)(2,1)S(1)} %get-tuple-element.38), channel_id=1, source_target_pairs={{16,1},{17,2},{18,3},{19,4},{20,5},{21,6},{22,7},{23,8},{24,9},{25... | collective-permute-start | bytes 798728 | tf_op jit(solution)/shard_map/ppermute | solution.py:315
  13.7 12.2 %collective-permute-start.10 = (bf16[1040,128]{1,0:T(8,128)(2,1)S(1)}, bf16[1040,128]{1,0:T(8,128)(2,1)S(1)}, u32[]{:S(2)}, u32[]{:S(2)}) collective-permute-start(bf16[1040,128]{1,0:T(8,128)(2,1)S(1)} %get-tuple-element.39), channel_id=1, source_target_pairs={{17,0},{18,1},{19,2},{20,3},{21,4},{22,5},{23,6},{24,7},{25,8},{26... | collective-permute-start | bytes 798728 | tf_op jit(solution)/shard_map/ppermute | solution.py:315
  16.7 5.6 %collective-permute-start.8 = (f32[16,128]{1,0:T(8,128)S(1)}, f32[16,128]{1,0:T(8,128)S(1)}, u32[]{:S(2)}, u32[]{:S(2)}) collective-permute-start(f32[16,128]{1,0:T(8,128)S(1)} %pad_maximum_fusion.refs_0_), channel_id=1, source_target_pairs={{0,12},{1,13},{2,14},{3,15},{4,8},{5,9},{6,10},{7,11},{8,4},{9,5},... | collective-permute-start | bytes 24584 | tf_op jit(solution)/shard_map/ppermute | solution.py:319
  20.3 4.7 %collective-permute-start.7 = (f32[16,128]{1,0:T(8,128)S(1)}, f32[16,128]{1,0:T(8,128)S(1)}, u32[]{:S(2)}, u32[]{:S(2)}) collective-permute-start(f32[16,128]{1,0:T(8,128)S(1)} %pad_maximum_fusion.refs_0_), channel_id=1, source_target_pairs={{0,8},{1,9},{2,10},{3,11},{4,12},{5,13},{6,14},{7,15},{8,0},{9,1},... | collective-permute-start | bytes 24584 | tf_op jit(solution)/shard_map/ppermute | solution.py:319
  20.3 4.7 %collective-permute-start.6 = (f32[16,128]{1,0:T(8,128)S(1)}, f32[16,128]{1,0:T(8,128)S(1)}, u32[]{:S(2)}, u32[]{:S(2)}) collective-permute-start(f32[16,128]{1,0:T(8,128)S(1)} %pad_maximum_fusion.refs_0_), channel_id=1, source_target_pairs={{0,4},{1,5},{2,6},{3,7},{4,0},{5,1},{6,2},{7,3},{8,12},{9,13},{10,... | collective-permute-start | bytes 24584 | tf_op jit(solution)/shard_map/ppermute | solution.py:319
  25.9 1.9 %collective-permute-start.11 = (bf16[1056,128]{1,0:T(8,128)(2,1)S(1)}, bf16[1056,128]{1,0:T(8,128)(2,1)S(1)}, u32[]{:S(2)}, u32[]{:S(2)}) collective-permute-start(bf16[1056,128]{1,0:T(8,128)(2,1)S(1)} %get-tuple-element.43), channel_id=1, source_target_pairs={{0,16},{1,17},{2,18},{3,19},{4,20},{5,21},{6,22},{7,23},{8,24},{9,... | collective-permute-start | bytes 811016 | tf_op jit(solution)/shard_map/ppermute | solution.py:315

commit v6 on v5

--- a/solution.py
+++ b/solution.py
@@ -183,6 +183,17 @@
     def _():
         table_copy = pltpu.make_async_copy(table_ref, table, sem)
         table_copy.start()
+        panels = known_ref.shape[0]
+        for w in range(own + 2 * BAND_REACH):
+            if w < BAND_REACH:
+                labels = labels_of(left_ref, reach, w, panels)
+            elif w < BAND_REACH + own:
+                labels = known_ref[:, pl.ds((w - BAND_REACH) * side, side)]
+            else:
+                labels = labels_of(right_ref, reach, w - BAND_REACH - own, panels)
+            fated[pl.ds(w * side, side), :] = jnp.where(one_hot(labels), 1.0, 0.0).astype(jnp.bfloat16)
+        table_copy.wait()
+        pull_backward(table, fated, blk, pulled, own)
         has_left, has_right = here > 0, here < lax.axis_size("cell") - 1
         mass = []
         for b in range(own):
@@ -201,11 +212,16 @@
             grown = scaled.astype(jnp.float32) / growth_ref[0:1, at]
             src[at, :] = grown.astype(jnp.bfloat16)
         acc[...] = jnp.zeros_like(acc)
-        table_copy.wait()
         for n in range(slots):
             row = n // (slots // own) * side
             col = rows_of(table[1, n], side)
             acc[col, :] += jnp.dot(src[row : row + side, :], blk[table[0, n]], preferred_element_type=jnp.float32)
+        for b in range(own):
+            at = pl.ds(b * side, side)
+            fates = fates_of(pulled[at, :])
+            to_left[at, :] = fates
+            to_mid[at, :] = fates
+            to_right[at, :] = fates
         power_row = as_row(power + half, side)
         to_left[pl.ds(inner, reach), :] = acc[0:reach, :].astype(jnp.bfloat16)
         to_right[pl.ds(inner, reach), :] = acc[reach + inner :, :].astype(jnp.bfloat16)
@@ -219,23 +235,6 @@
         sums = jnp.sum(jnp.transpose(total), axis=0, keepdims=True)
         part_ref[0:8, :] = jnp.broadcast_to(sums, (8, side))
         part_ref[8:16, :] = power_row
-
-        panels = known_ref.shape[0]
-        for w in range(own + 2 * BAND_REACH):
-            if w < BAND_REACH:
-                labels = labels_of(left_ref, reach, w, panels)
-            elif w < BAND_REACH + own:
-                labels = known_ref[:, pl.ds((w - BAND_REACH) * side, side)]
-            else:
-                labels = labels_of(right_ref, reach, w - BAND_REACH - own, panels)
-            fated[pl.ds(w * side, side), :] = jnp.where(one_hot(labels), 1.0, 0.0).astype(jnp.bfloat16)
-        pull_backward(table, fated, blk, pulled, own)
-        for b in range(own):
-            at = pl.ds(b * side, side)
-            fates = fates_of(pulled[at, :])
-            to_left[at, :] = fates
-            to_mid[at, :] = fates
-            to_right[at, :] = fates
 
 
 def combined(parts):

time: 30.1 us -> 30.1 us (level)
  no operation moved by 1% of the time
where the time goes in v6:
time: 30.1 us; the launch traced here: 29.9 us
  starting transfers between devices  15.2 us (50%)
  waiting for transfers between devices  9.33 us (31%)
  Pallas kernels  4.66 us (15%)
  between operations  0.72 us (2%)
    ppermute x6, starting transfers between devices, flipped(): lax.ppermute(array, 'cell', [(c, c ^ bits) for c in range(lax.axis_size('...  9.84 us
    ppermute x6, waiting for transfers between devices, flipped(): lax.ppermute(array, 'cell', [(c, c ^ bits) for c in range(lax.axis_size('...  5.55 us
    ppermute x6, starting transfers between devices, across(): return lax.ppermute(array, ('tm', 'cell'), route)  5.34 us
    ppermute x6, waiting for transfers between devices, across(): return lax.ppermute(array, ('tm', 'cell'), route)  3.78 us
    pallas_call x1, Pallas kernels, on_device(): pl.pallas_call(functools.partial(first_kernel, own), out_shape=(bf16(reac...  2.51 us
    pallas_call x1, Pallas kernels, on_device(): pl.pallas_call(functools.partial(last_kernel, own, float(cells * cell_cou...  2.02 us
  transfers between devices with their start and end apart: 12, of which 8 were waited for; matrix products, arithmetic and copies ran while one was open for 0% of the time, Pallas kernels for 0%

profile of v6, /device:TPU:0, one launch (start us, length us, event | category | flops | bytes accessed | tf_op | source)
XLA Modules:
  0.0 29.9 jit_solution(15130261384374949570)
XLA Ops:
  0.6 2.5 %push_first.1 = (bf16[544,128]{1,0:T(8,128)(2,1)S(1)}, bf16[512,128]{1,0:T(8,128)(2,1)S(1)}, bf16[544,128]{1,0:T(8,128)(2,1)S(1)}, f32[512,128]{1,0:T(8,128)S(1)...) custom-call(s32[1,64]{1,0:T(1,128)} %rows_hbm.3, ...), custom_call_target="tpu_custom_call" | custom-call | tf_op jit(solution)/shard_map/push_first/pallas_call | solution.py:347
  3.1 1.9 %collective-permute-start = (bf16[544,128]{1,0:T(8,128)(2,1)S(1)}, bf16[544,128]{1,0:T(8,128)(2,1)S(1)}, u32[]{:S(2)}, u32[]{:S(2)}) collective-permute-start(bf16[544,128]{1,0:T(8,128)(2,1)S(1)} %get-tuple-element.30), channel_id=1, source_target_pairs={{0,17},{1,18},{2,19},{3,20},{4,21},{5,22},{6,23},{7,24},{8,25},{9,... | collective-permute-start | bytes 417800 | tf_op jit(solution)/shard_map/ppermute | solution.py:314
  5.0 0.7 %collective-permute-start.2 = (bf16[544,128]{1,0:T(8,128)(2,1)S(1)}, bf16[544,128]{1,0:T(8,128)(2,1)S(1)}, u32[]{:S(2)}, u32[]{:S(2)}) collective-permute-start(bf16[544,128]{1,0:T(8,128)(2,1)S(1)} %get-tuple-element.32), channel_id=1, source_target_pairs={{1,16},{2,17},{3,18},{4,19},{5,20},{6,21},{7,22},{8,23},{9,24},{10... | collective-permute-start | bytes 417800 | tf_op jit(solution)/shard_map/ppermute | solution.py:314
  5.7 0.1 collective-permute-start.1
  5.8 0.1 prepare.1
  5.9 1.2 %collective-permute-done.1.mid_ref = bf16[512,128]{1,0:T(8,128)(2,1)S(1)} collective-permute-done((bf16[512,128]{1,0:T(8,128)(2,1)S(1)}, bf16[512,128]{1,0:T(8,128)(2,1)S(1)}, u32[]{:S(2)}, u32[]{:S(2)}) %collective-permute-start.1) | collective-permute-done | bytes 131104 | tf_op jit(solution)/shard_map/ppermute | solution.py:314
  7.1 0.5 %collective-permute-done.left_ref = bf16[544,128]{1,0:T(8,128)(2,1)S(1)} collective-permute-done((bf16[544,128]{1,0:T(8,128)(2,1)S(1)}, bf16[544,128]{1,0:T(8,128)(2,1)S(1)}, u32[]{:S(2)}, u32[]{:S(2)}) %collective-permute-start) | collective-permute-done | bytes 139296 | tf_op jit(solution)/shard_map/ppermute | solution.py:314
  7.6 4.7 %collective-permute-start.5 = (f32[16,128]{1,0:T(8,128)S(1)}, f32[16,128]{1,0:T(8,128)S(1)}, u32[]{:S(2)}, u32[]{:S(2)}) collective-permute-start(f32[16,128]{1,0:T(8,128)S(1)} %get-tuple-element.36.own_part), channel_id=1, source_target_pairs={{0,3},{1,2},{2,1},{3,0},{4,7},{5,6},{6,5},{7,4},{8,11},{9,10},{10,... | collective-permute-start | bytes 24584 | tf_op jit(solution)/shard_map/ppermute | solution.py:318
  12.3 0.7 %collective-permute-start.4 = (f32[16,128]{1,0:T(8,128)S(1)}, f32[16,128]{1,0:T(8,128)S(1)}, u32[]{:S(2)}, u32[]{:S(2)}) collective-permute-start(f32[16,128]{1,0:T(8,128)S(1)} %get-tuple-element.36.own_part), channel_id=1, source_target_pairs={{0,2},{1,3},{2,0},{3,1},{4,6},{5,7},{6,4},{7,5},{8,10},{9,11},{10,... | collective-permute-start | bytes 24584 | tf_op jit(solution)/shard_map/ppermute | solution.py:318
  13.0 0.0 collective-permute-start.3
  13.0 0.7 %collective-permute-start.9 = (bf16[1040,128]{1,0:T(8,128)(2,1)S(1)}, bf16[1040,128]{1,0:T(8,128)(2,1)S(1)}, u32[]{:S(2)}, u32[]{:S(2)}) collective-permute-start(bf16[1040,128]{1,0:T(8,128)(2,1)S(1)} %get-tuple-element.38), channel_id=1, source_target_pairs={{16,1},{17,2},{18,3},{19,4},{20,5},{21,6},{22,7},{23,8},{24,9},{25... | collective-permute-start | bytes 798728 | tf_op jit(solution)/shard_map/ppermute | solution.py:314
  13.7 1.3 %collective-permute-start.10 = (bf16[1040,128]{1,0:T(8,128)(2,1)S(1)}, bf16[1040,128]{1,0:T(8,128)(2,1)S(1)}, u32[]{:S(2)}, u32[]{:S(2)}) collective-permute-start(bf16[1040,128]{1,0:T(8,128)(2,1)S(1)} %get-tuple-element.39), channel_id=1, source_target_pairs={{17,0},{18,1},{19,2},{20,3},{21,4},{22,5},{23,6},{24,7},{25,8},{26... | collective-permute-start | bytes 798728 | tf_op jit(solution)/shard_map/ppermute | solution.py:314
  15.0 1.0 %collective-permute-done.4 = f32[16,128]{1,0:T(8,128)S(1)} collective-permute-done((f32[16,128]{1,0:T(8,128)S(1)}, f32[16,128]{1,0:T(8,128)S(1)}, u32[]{:S(2)}, u32[]{:S(2)}) %collective-permute-start.4) | collective-permute-done | bytes 8224 | tf_op jit(solution)/shard_map/ppermute | solution.py:318
  16.0 0.7 %collective-permute-done.3 = f32[16,128]{1,0:T(8,128)S(1)} collective-permute-done((f32[16,128]{1,0:T(8,128)S(1)}, f32[16,128]{1,0:T(8,128)S(1)}, u32[]{:S(2)}, u32[]{:S(2)}) %collective-permute-start.3) | collective-permute-done | bytes 8224 | tf_op jit(solution)/shard_map/ppermute | solution.py:318
  16.7 3.7 %collective-permute-start.8 = (f32[16,128]{1,0:T(8,128)S(1)}, f32[16,128]{1,0:T(8,128)S(1)}, u32[]{:S(2)}, u32[]{:S(2)}) collective-permute-start(f32[16,128]{1,0:T(8,128)S(1)} %pad_maximum_fusion.refs_0_), channel_id=1, source_target_pairs={{0,12},{1,13},{2,14},{3,15},{4,8},{5,9},{6,10},{7,11},{8,4},{9,5},... | collective-permute-start | bytes 24584 | tf_op jit(solution)/shard_map/ppermute | solution.py:318
  20.3 0.8 %collective-permute-start.6 = (f32[16,128]{1,0:T(8,128)S(1)}, f32[16,128]{1,0:T(8,128)S(1)}, u32[]{:S(2)}, u32[]{:S(2)}) collective-permute-start(f32[16,128]{1,0:T(8,128)S(1)} %pad_maximum_fusion.refs_0_), channel_id=1, source_target_pairs={{0,4},{1,5},{2,6},{3,7},{4,0},{5,1},{6,2},{7,3},{8,12},{9,13},{10,... | collective-permute-start | bytes 24584 | tf_op jit(solution)/shard_map/ppermute | solution.py:318
  21.1 1.2 %collective-permute-done.8.refs_3_ = f32[16,128]{1,0:T(8,128)S(1)} collective-permute-done((f32[16,128]{1,0:T(8,128)S(1)}, f32[16,128]{1,0:T(8,128)S(1)}, u32[]{:S(2)}, u32[]{:S(2)}) %collective-permute-start.8) | collective-permute-done | bytes 8224 | tf_op jit(solution)/shard_map/ppermute | solution.py:318
  22.3 2.8 %collective-permute-done.7.refs_2_ = f32[16,128]{1,0:T(8,128)S(1)} collective-permute-done((f32[16,128]{1,0:T(8,128)S(1)}, f32[16,128]{1,0:T(8,128)S(1)}, u32[]{:S(2)}, u32[]{:S(2)}) %collective-permute-start.7) | collective-permute-done | bytes 8224 | tf_op jit(solution)/shard_map/ppermute | solution.py:318
  25.0 0.0 collective-permute-done.6.refs_1_
  25.0 0.0 collective-permute-done.9.refs_5_.back_left
  25.0 0.9 %collective-permute-done.10.refs_6_.back_right = bf16[1040,128]{1,0:T(8,128)(2,1)S(1)} collective-permute-done((bf16[1040,128]{1,0:T(8,128)(2,1)S(1)}, bf16[1040,128]{1,0:T(8,128)(2,1)S(1)}, u32[]{:S(2)}, u32[]{:S(2)}) %collective-permute-start.10) | collective-permute-done | bytes 266272 | tf_op jit(solution)/shard_map/ppermute | solution.py:314
  26.0 0.8 %collective-permute-start.11 = (bf16[1056,128]{1,0:T(8,128)(2,1)S(1)}, bf16[1056,128]{1,0:T(8,128)(2,1)S(1)}, u32[]{:S(2)}, u32[]{:S(2)}) collective-permute-start(bf16[1056,128]{1,0:T(8,128)(2,1)S(1)} %get-tuple-element.43), channel_id=1, source_target_pairs={{0,16},{1,17},{2,18},{3,19},{4,20},{5,21},{6,22},{7,23},{8,24},{9,... | collective-permute-start | bytes 811016 | tf_op jit(solution)/shard_map/ppermute | solution.py:314
  26.7 1.2 %collective-permute-done.11.swap = bf16[1056,128]{1,0:T(8,128)(2,1)S(1)} collective-permute-done((bf16[1056,128]{1,0:T(8,128)(2,1)S(1)}, bf16[1056,128]{1,0:T(8,128)(2,1)S(1)}, u32[]{:S(2)}, u32[]{:S(2)}) %collective-permute-start.11) | collective-permute-done | bytes 270368 | tf_op jit(solution)/shard_map/ppermute | solution.py:314
  27.9 2.0 %pull_second_normalise.1 = (bf16[1,128,512]{2,1,0:T(8,128)(2,1)}, bf16[1,128,512]{2,1,0:T(8,128)(2,1)}) custom-call(s32[2,64]{1,0:T(2,128)S(1)} %get-tuple-element.27.table_ref, f32[16,128]{1,0:T(8,128)S(1)} %get-tuple-element.40.whole, f32[16,128]{1,0:T(8,128)S(1)} %get-tuple-element.36.own_part, f32[512,128]{1,0:T(8,128)S(1)} %get-tuple-element.41.keep_first, ...), custom_call_target="tpu_custom_call" | custom-call | tf_op jit(solution)/shard_map/pull_second_normalise/pallas_call | solution.py:415
  (7 shorter events, 0.1 us)
Async XLA Ops:
  3.1 4.5 %collective-permute-start = (bf16[544,128]{1,0:T(8,128)(2,1)S(1)}, bf16[544,128]{1,0:T(8,128)(2,1)S(1)}, u32[]{:S(2)}, u32[]{:S(2)}) collective-permute-start(bf16[544,128]{1,0:T(8,128)(2,1)S(1)} %get-tuple-element.30), channel_id=1, source_target_pairs={{0,17},{1,18},{2,19},{3,20},{4,21},{5,22},{6,23},{7,24},{8,25},{9,... | collective-permute-start | bytes 417800 | tf_op jit(solution)/shard_map/ppermute | solution.py:314
  5.0 2.6 %collective-permute-start.2 = (bf16[544,128]{1,0:T(8,128)(2,1)S(1)}, bf16[544,128]{1,0:T(8,128)(2,1)S(1)}, u32[]{:S(2)}, u32[]{:S(2)}) collective-permute-start(bf16[544,128]{1,0:T(8,128)(2,1)S(1)} %get-tuple-element.32), channel_id=1, source_target_pairs={{1,16},{2,17},{3,18},{4,19},{5,20},{6,21},{7,22},{8,23},{9,24},{10... | collective-permute-start | bytes 417800 | tf_op jit(solution)/shard_map/ppermute | solution.py:314
  5.7 1.4 %collective-permute-start.1 = (bf16[512,128]{1,0:T(8,128)(2,1)S(1)}, bf16[512,128]{1,0:T(8,128)(2,1)S(1)}, u32[]{:S(2)}, u32[]{:S(2)}) collective-permute-start(bf16[512,128]{1,0:T(8,128)(2,1)S(1)} %get-tuple-element.31), channel_id=1, source_target_pairs={{0,16},{1,17},{2,18},{3,19},{4,20},{5,21},{6,22},{7,23},{8,24},{9,... | collective-permute-start | bytes 393224 | tf_op jit(solution)/shard_map/ppermute | solution.py:314
  7.6 7.4 %collective-permute-start.5 = (f32[16,128]{1,0:T(8,128)S(1)}, f32[16,128]{1,0:T(8,128)S(1)}, u32[]{:S(2)}, u32[]{:S(2)}) collective-permute-start(f32[16,128]{1,0:T(8,128)S(1)} %get-tuple-element.36.own_part), channel_id=1, source_target_pairs={{0,3},{1,2},{2,1},{3,0},{4,7},{5,6},{6,5},{7,4},{8,11},{9,10},{10,... | collective-permute-start | bytes 24584 | tf_op jit(solution)/shard_map/ppermute | solution.py:318
  12.3 3.7 %collective-permute-start.4 = (f32[16,128]{1,0:T(8,128)S(1)}, f32[16,128]{1,0:T(8,128)S(1)}, u32[]{:S(2)}, u32[]{:S(2)}) collective-permute-start(f32[16,128]{1,0:T(8,128)S(1)} %get-tuple-element.36.own_part), channel_id=1, source_target_pairs={{0,2},{1,3},{2,0},{3,1},{4,6},{5,7},{6,4},{7,5},{8,10},{9,11},{10,... | collective-permute-start | bytes 24584 | tf_op jit(solution)/shard_map/ppermute | solution.py:318
  13.0 3.7 %collective-permute-start.3 = (f32[16,128]{1,0:T(8,128)S(1)}, f32[16,128]{1,0:T(8,128)S(1)}, u32[]{:S(2)}, u32[]{:S(2)}) collective-permute-start(f32[16,128]{1,0:T(8,128)S(1)} %get-tuple-element.36.own_part), channel_id=1, source_target_pairs={{0,1},{1,0},{2,3},{3,2},{4,5},{5,4},{6,7},{7,6},{8,9},{9,8},{10,11... | collective-permute-start | bytes 24584 | tf_op jit(solution)/shard_map/ppermute | solution.py:318
  13.0 12.0 %collective-permute-start.9 = (bf16[1040,128]{1,0:T(8,128)(2,1)S(1)}, bf16[1040,128]{1,0:T(8,128)(2,1)S(1)}, u32[]{:S(2)}, u32[]{:S(2)}) collective-permute-start(bf16[1040,128]{1,0:T(8,128)(2,1)S(1)} %get-tuple-element.38), channel_id=1, source_target_pairs={{16,1},{17,2},{18,3},{19,4},{20,5},{21,6},{22,7},{23,8},{24,9},{25... | collective-permute-start | bytes 798728 | tf_op jit(solution)/shard_map/ppermute | solution.py:314
  13.7 12.2 %collective-permute-start.10 = (bf16[1040,128]{1,0:T(8,128)(2,1)S(1)}, bf16[1040,128]{1,0:T(8,128)(2,1)S(1)}, u32[]{:S(2)}, u32[]{:S(2)}) collective-permute-start(bf16[1040,128]{1,0:T(8,128)(2,1)S(1)} %get-tuple-element.39), channel_id=1, source_target_pairs={{17,0},{18,1},{19,2},{20,3},{21,4},{22,5},{23,6},{24,7},{25,8},{26... | collective-permute-start | bytes 798728 | tf_op jit(solution)/shard_map/ppermute | solution.py:314
  16.7 5.6 %collective-permute-start.8 = (f32[16,128]{1,0:T(8,128)S(1)}, f32[16,128]{1,0:T(8,128)S(1)}, u32[]{:S(2)}, u32[]{:S(2)}) collective-permute-start(f32[16,128]{1,0:T(8,128)S(1)} %pad_maximum_fusion.refs_0_), channel_id=1, source_target_pairs={{0,12},{1,13},{2,14},{3,15},{4,8},{5,9},{6,10},{7,11},{8,4},{9,5},... | collective-permute-start | bytes 24584 | tf_op jit(solution)/shard_map/ppermute | solution.py:318
  20.3 4.7 %collective-permute-start.7 = (f32[16,128]{1,0:T(8,128)S(1)}, f32[16,128]{1,0:T(8,128)S(1)}, u32[]{:S(2)}, u32[]{:S(2)}) collective-permute-start(f32[16,128]{1,0:T(8,128)S(1)} %pad_maximum_fusion.refs_0_), channel_id=1, source_target_pairs={{0,8},{1,9},{2,10},{3,11},{4,12},{5,13},{6,14},{7,15},{8,0},{9,1},... | collective-permute-start | bytes 24584 | tf_op jit(solution)/shard_map/ppermute | solution.py:318
  20.3 4.7 %collective-permute-start.6 = (f32[16,128]{1,0:T(8,128)S(1)}, f32[16,128]{1,0:T(8,128)S(1)}, u32[]{:S(2)}, u32[]{:S(2)}) collective-permute-start(f32[16,128]{1,0:T(8,128)S(1)} %pad_maximum_fusion.refs_0_), channel_id=1, source_target_pairs={{0,4},{1,5},{2,6},{3,7},{4,0},{5,1},{6,2},{7,3},{8,12},{9,13},{10,... | collective-permute-start | bytes 24584 | tf_op jit(solution)/shard_map/ppermute | solution.py:318
  26.0 1.9 %collective-permute-start.11 = (bf16[1056,128]{1,0:T(8,128)(2,1)S(1)}, bf16[1056,128]{1,0:T(8,128)(2,1)S(1)}, u32[]{:S(2)}, u32[]{:S(2)}) collective-permute-start(bf16[1056,128]{1,0:T(8,128)(2,1)S(1)} %get-tuple-element.43), channel_id=1, source_target_pairs={{0,16},{1,17},{2,18},{3,19},{4,20},{5,21},{6,22},{7,23},{8,24},{9,... | collective-permute-start | bytes 811016 | tf_op jit(solution)/shard_map/ppermute | solution.py:314

commit v7 on v5

--- a/solution.py
+++ b/solution.py
@@ -10,6 +10,9 @@
 BAND_REACH = 4
 LABEL_ROWS = 16
 CHUNKS = 2
+XA = ("inc", "chain", "full")
+XB = ("inc", "inc", "full")
+XC = "full"
 
 
 def rows_of(block, side):
@@ -305,14 +308,20 @@
             fate_ref[0, :, at] = mine_ref[at, :]
 
 
-def across(array, distance, sender, both=False):
+def across(array, distance, sender, mode):
     count = lax.axis_size("cell")
     at = lambda core, c: core * count + c
     other = 1 - sender
-    route = [(at(sender, c), at(other, c + distance)) for c in range(count) if 0 <= c + distance < count]
-    if both:
-        route += [(there, here) for here, there in route]
-    return lax.ppermute(array, ("tm", "cell"), route)
+    route = {at(sender, c): at(other, c + distance) for c in range(count) if 0 <= c + distance < count}
+    if mode == "full":
+        for c in range(count):
+            route[at(other, c)] = at(sender, c - distance) if 0 <= c - distance < count else at(other, c)
+            route.setdefault(at(sender, c), at(sender, c))
+    if mode == "chain":
+        for c in range(count):
+            route[at(other, c)] = at(sender, c)
+            route.setdefault(at(sender, c), at(other, (c + distance) % count))
+    return lax.ppermute(array, ("tm", "cell"), list(route.items()))
 
 
 def flipped(array, bits):
@@ -361,9 +370,9 @@
         name="push_first",
     )(*inputs)
 
-    from_left = across(right, 1, 0)
-    from_right = across(left, -1, 0)
-    from_mid = across(mid, 0, 0, both=True)
+    from_left = across(right, 1, 0, XA[0])
+    from_right = across(left, -1, 0, XA[1])
+    from_mid = across(mid, 0, 0, XA[2])
 
     table, rates, known, blocks, half = pl.pallas_call(
         functools.partial(prepare_kernel, own),
@@ -392,8 +401,8 @@
         name="push_second_pull_first",
     )(table, rates, known, from_left, from_mid, from_right, part, half, blocks)
 
-    back_left = across(to_right, 1, 1)
-    back_right = across(to_left, -1, 1)
+    back_left = across(to_right, 1, 1, XB[0])
+    back_right = across(to_left, -1, 1, XB[1])
 
     whole = part
     bit = 1
@@ -411,7 +420,7 @@
         name="combine",
     )(*parts, to_mid, back_left, back_right)
 
-    swap = across(to_swap, 0, 0, both=True)
+    swap = across(to_swap, 0, 0, XC)
 
     forward_mass, fate = pl.pallas_call(
         functools.partial(last_kernel, own, float(cells * cell_count)),

time: 30.1 us -> 30.1 us (level)
  waiting for transfers between devices: 9.31 us -> 8.47 us
  starting transfers between devices: 15.2 us -> 16 us
    ppermute x6, starting transfers between devices: 5.34 us -> 8.02 us  [across(): return lax.ppermute(array, ('tm', 'cell'), list(route.items()))]
    ppermute x6, starting transfers between devices: 9.84 us -> 8 us  [flipped(): lax.ppermute(array, 'cell', [(c, c ^ bits) for c in range(lax.axis_size('...]
    ppermute x6, waiting for transfers between devices: 5.55 us -> 3.91 us  [flipped(): lax.ppermute(array, 'cell', [(c, c ^ bits) for c in range(lax.axis_size('...]
    ppermute x6, waiting for transfers between devices: 3.76 us -> 4.55 us  [across(): return lax.ppermute(array, ('tm', 'cell'), list(route.items()))]
  transfers between devices with their start and end apart: 12 -> 12, of which waited for: 8 -> 6; matrix products, arithmetic and copies ran while one was open for 0% -> 0% of each run, Pallas kernels for 0% -> 0%
where the time goes in v7:
time: 30.1 us; the launch traced here: 29.9 us
  starting transfers between devices  16 us (53%)
  waiting for transfers between devices  8.47 us (28%)
  Pallas kernels  4.64 us (15%)
  between operations  0.73 us (2%)
    ppermute x6, starting transfers between devices, across(): return lax.ppermute(array, ('tm', 'cell'), list(route.items()))  8.02 us
    ppermute x6, starting transfers between devices, flipped(): lax.ppermute(array, 'cell', [(c, c ^ bits) for c in range(lax.axis_size('...  8 us
    ppermute x6, waiting for transfers between devices, across(): return lax.ppermute(array, ('tm', 'cell'), list(route.items()))  4.55 us
    ppermute x6, waiting for transfers between devices, flipped(): lax.ppermute(array, 'cell', [(c, c ^ bits) for c in range(lax.axis_size('...  3.91 us
    pallas_call x1, Pallas kernels, on_device(): pl.pallas_call(functools.partial(first_kernel, own), out_shape=(bf16(reac...  2.51 us
    pallas_call x1, Pallas kernels, on_device(): pl.pallas_call(functools.partial(last_kernel, own, float(cells * cell_cou...  2.02 us
  transfers between devices with their start and end apart: 12, of which 6 were waited for; matrix products, arithmetic and copies ran while one was open for 0% of the time, Pallas kernels for 0%

profile of v7, /device:TPU:0, one launch (start us, length us, event | category | flops | bytes accessed | tf_op | source)
XLA Modules:
  0.0 29.9 jit_solution(6084725939018546569)
XLA Ops:
  0.6 2.5 %push_first.1 = (bf16[544,128]{1,0:T(8,128)(2,1)S(1)}, bf16[512,128]{1,0:T(8,128)(2,1)S(1)}, bf16[544,128]{1,0:T(8,128)(2,1)S(1)}, f32[512,128]{1,0:T(8,128)S(1)...) custom-call(s32[1,64]{1,0:T(1,128)} %rows_hbm.3, ...), custom_call_target="tpu_custom_call" | custom-call | tf_op jit(solution)/shard_map/push_first/pallas_call | solution.py:357
  3.1 1.9 %collective-permute-start = (bf16[544,128]{1,0:T(8,128)(2,1)S(1)}, bf16[544,128]{1,0:T(8,128)(2,1)S(1)}, u32[]{:S(2)}, u32[]{:S(2)}) collective-permute-start(bf16[544,128]{1,0:T(8,128)(2,1)S(1)} %get-tuple-element.30), channel_id=1, source_target_pairs={{0,17},{1,18},{2,19},{3,20},{4,21},{5,22},{6,23},{7,24},{8,25},{9,... | collective-permute-start | bytes 417800 | tf_op jit(solution)/shard_map/ppermute | solution.py:324
  5.0 3.4 %collective-permute-start.2 = (bf16[544,128]{1,0:T(8,128)(2,1)S(1)}, bf16[544,128]{1,0:T(8,128)(2,1)S(1)}, u32[]{:S(2)}, u32[]{:S(2)}) collective-permute-start(bf16[544,128]{1,0:T(8,128)(2,1)S(1)} %get-tuple-element.32), channel_id=1, source_target_pairs={{1,16},{2,17},{3,18},{4,19},{5,20},{6,21},{7,22},{8,23},{9,24},{10... | collective-permute-start | bytes 417800 | tf_op jit(solution)/shard_map/ppermute | solution.py:324
  8.5 0.0 collective-permute-start.1
  8.5 0.1 prepare.1
  8.5 1.3 %collective-permute-done.1.mid_ref = bf16[512,128]{1,0:T(8,128)(2,1)S(1)} collective-permute-done((bf16[512,128]{1,0:T(8,128)(2,1)S(1)}, bf16[512,128]{1,0:T(8,128)(2,1)S(1)}, u32[]{:S(2)}, u32[]{:S(2)}) %collective-permute-start.1) | collective-permute-done | bytes 131104 | tf_op jit(solution)/shard_map/ppermute | solution.py:324
  9.8 0.0 collective-permute-done.left_ref
  9.8 1.2 %collective-permute-done.2.right_ref = bf16[544,128]{1,0:T(8,128)(2,1)S(1)} collective-permute-done((bf16[544,128]{1,0:T(8,128)(2,1)S(1)}, bf16[544,128]{1,0:T(8,128)(2,1)S(1)}, u32[]{:S(2)}, u32[]{:S(2)}) %collective-permute-start.2) | collective-permute-done | bytes 139296 | tf_op jit(solution)/shard_map/ppermute | solution.py:324
  11.1 0.1 collective-permute-start.5
  11.1 1.8 %collective-permute-start.4 = (f32[16,128]{1,0:T(8,128)S(1)}, f32[16,128]{1,0:T(8,128)S(1)}, u32[]{:S(2)}, u32[]{:S(2)}) collective-permute-start(f32[16,128]{1,0:T(8,128)S(1)} %get-tuple-element.36.own_part), channel_id=1, source_target_pairs={{0,2},{1,3},{2,0},{3,1},{4,6},{5,7},{6,4},{7,5},{8,10},{9,11},{10,... | collective-permute-start | bytes 24584 | tf_op jit(solution)/shard_map/ppermute | solution.py:328
  13.0 1.7 %collective-permute-start.3 = (f32[16,128]{1,0:T(8,128)S(1)}, f32[16,128]{1,0:T(8,128)S(1)}, u32[]{:S(2)}, u32[]{:S(2)}) collective-permute-start(f32[16,128]{1,0:T(8,128)S(1)} %get-tuple-element.36.own_part), channel_id=1, source_target_pairs={{0,1},{1,0},{2,3},{3,2},{4,5},{5,4},{6,7},{7,6},{8,9},{9,8},{10,11... | collective-permute-start | bytes 24584 | tf_op jit(solution)/shard_map/ppermute | solution.py:328
  14.6 0.7 %collective-permute-start.9 = (bf16[1040,128]{1,0:T(8,128)(2,1)S(1)}, bf16[1040,128]{1,0:T(8,128)(2,1)S(1)}, u32[]{:S(2)}, u32[]{:S(2)}) collective-permute-start(bf16[1040,128]{1,0:T(8,128)(2,1)S(1)} %get-tuple-element.38), channel_id=1, source_target_pairs={{16,1},{17,2},{18,3},{19,4},{20,5},{21,6},{22,7},{23,8},{24,9},{25... | collective-permute-start | bytes 798728 | tf_op jit(solution)/shard_map/ppermute | solution.py:324
  15.3 1.3 %collective-permute-start.10 = (bf16[1040,128]{1,0:T(8,128)(2,1)S(1)}, bf16[1040,128]{1,0:T(8,128)(2,1)S(1)}, u32[]{:S(2)}, u32[]{:S(2)}) collective-permute-start(bf16[1040,128]{1,0:T(8,128)(2,1)S(1)} %get-tuple-element.39), channel_id=1, source_target_pairs={{17,0},{18,1},{19,2},{20,3},{21,4},{22,5},{23,6},{24,7},{25,8},{26... | collective-permute-start | bytes 798728 | tf_op jit(solution)/shard_map/ppermute | solution.py:324
  16.6 0.0 collective-permute-done.5
  16.6 0.0 collective-permute-done.4
  16.6 0.0 collective-permute-done.3
  16.7 3.7 %collective-permute-start.8 = (f32[16,128]{1,0:T(8,128)S(1)}, f32[16,128]{1,0:T(8,128)S(1)}, u32[]{:S(2)}, u32[]{:S(2)}) collective-permute-start(f32[16,128]{1,0:T(8,128)S(1)} %pad_maximum_fusion.refs_0_), channel_id=1, source_target_pairs={{0,12},{1,13},{2,14},{3,15},{4,8},{5,9},{6,10},{7,11},{8,4},{9,5},... | collective-permute-start | bytes 24584 | tf_op jit(solution)/shard_map/ppermute | solution.py:328
  20.3 0.8 %collective-permute-start.6 = (f32[16,128]{1,0:T(8,128)S(1)}, f32[16,128]{1,0:T(8,128)S(1)}, u32[]{:S(2)}, u32[]{:S(2)}) collective-permute-start(f32[16,128]{1,0:T(8,128)S(1)} %pad_maximum_fusion.refs_0_), channel_id=1, source_target_pairs={{0,4},{1,5},{2,6},{3,7},{4,0},{5,1},{6,2},{7,3},{8,12},{9,13},{10,... | collective-permute-start | bytes 24584 | tf_op jit(solution)/shard_map/ppermute | solution.py:328
  21.1 1.2 %collective-permute-done.8.refs_3_ = f32[16,128]{1,0:T(8,128)S(1)} collective-permute-done((f32[16,128]{1,0:T(8,128)S(1)}, f32[16,128]{1,0:T(8,128)S(1)}, u32[]{:S(2)}, u32[]{:S(2)}) %collective-permute-start.8) | collective-permute-done | bytes 8224 | tf_op jit(solution)/shard_map/ppermute | solution.py:328
  22.3 2.7 %collective-permute-done.7.refs_2_ = f32[16,128]{1,0:T(8,128)S(1)} collective-permute-done((f32[16,128]{1,0:T(8,128)S(1)}, f32[16,128]{1,0:T(8,128)S(1)}, u32[]{:S(2)}, u32[]{:S(2)}) %collective-permute-start.7) | collective-permute-done | bytes 8224 | tf_op jit(solution)/shard_map/ppermute | solution.py:328
  25.0 0.9 %collective-permute-done.10.refs_6_.back_right = bf16[1040,128]{1,0:T(8,128)(2,1)S(1)} collective-permute-done((bf16[1040,128]{1,0:T(8,128)(2,1)S(1)}, bf16[1040,128]{1,0:T(8,128)(2,1)S(1)}, u32[]{:S(2)}, u32[]{:S(2)}) %collective-permute-start.10) | collective-permute-done | bytes 266272 | tf_op jit(solution)/shard_map/ppermute | solution.py:324
  25.9 0.8 %collective-permute-start.11 = (bf16[1056,128]{1,0:T(8,128)(2,1)S(1)}, bf16[1056,128]{1,0:T(8,128)(2,1)S(1)}, u32[]{:S(2)}, u32[]{:S(2)}) collective-permute-start(bf16[1056,128]{1,0:T(8,128)(2,1)S(1)} %get-tuple-element.43), channel_id=1, source_target_pairs={{0,16},{1,17},{2,18},{3,19},{4,20},{5,21},{6,22},{7,23},{8,24},{9,... | collective-permute-start | bytes 811016 | tf_op jit(solution)/shard_map/ppermute | solution.py:324
  26.7 1.2 %collective-permute-done.11.swap = bf16[1056,128]{1,0:T(8,128)(2,1)S(1)} collective-permute-done((bf16[1056,128]{1,0:T(8,128)(2,1)S(1)}, bf16[1056,128]{1,0:T(8,128)(2,1)S(1)}, u32[]{:S(2)}, u32[]{:S(2)}) %collective-permute-start.11) | collective-permute-done | bytes 270368 | tf_op jit(solution)/shard_map/ppermute | solution.py:324
  27.9 2.0 %pull_second_normalise.1 = (bf16[1,128,512]{2,1,0:T(8,128)(2,1)}, bf16[1,128,512]{2,1,0:T(8,128)(2,1)}) custom-call(s32[2,64]{1,0:T(2,128)S(1)} %get-tuple-element.27.table_ref, f32[16,128]{1,0:T(8,128)S(1)} %get-tuple-element.40.whole, f32[16,128]{1,0:T(8,128)S(1)} %get-tuple-element.36.own_part, f32[512,128]{1,0:T(8,128)S(1)} %get-tuple-element.41.keep_first, ...), custom_call_target="tpu_custom_call" | custom-call | tf_op jit(solution)/shard_map/pull_second_normalise/pallas_call | solution.py:425
  (7 shorter events, 0.1 us)
Async XLA Ops:
  3.1 6.7 %collective-permute-start = (bf16[544,128]{1,0:T(8,128)(2,1)S(1)}, bf16[544,128]{1,0:T(8,128)(2,1)S(1)}, u32[]{:S(2)}, u32[]{:S(2)}) collective-permute-start(bf16[544,128]{1,0:T(8,128)(2,1)S(1)} %get-tuple-element.30), channel_id=1, source_target_pairs={{0,17},{1,18},{2,19},{3,20},{4,21},{5,22},{6,23},{7,24},{8,25},{9,... | collective-permute-start | bytes 417800 | tf_op jit(solution)/shard_map/ppermute | solution.py:324
  5.0 6.0 %collective-permute-start.2 = (bf16[544,128]{1,0:T(8,128)(2,1)S(1)}, bf16[544,128]{1,0:T(8,128)(2,1)S(1)}, u32[]{:S(2)}, u32[]{:S(2)}) collective-permute-start(bf16[544,128]{1,0:T(8,128)(2,1)S(1)} %get-tuple-element.32), channel_id=1, source_target_pairs={{1,16},{2,17},{3,18},{4,19},{5,20},{6,21},{7,22},{8,23},{9,24},{10... | collective-permute-start | bytes 417800 | tf_op jit(solution)/shard_map/ppermute | solution.py:324
  8.5 1.3 %collective-permute-start.1 = (bf16[512,128]{1,0:T(8,128)(2,1)S(1)}, bf16[512,128]{1,0:T(8,128)(2,1)S(1)}, u32[]{:S(2)}, u32[]{:S(2)}) collective-permute-start(bf16[512,128]{1,0:T(8,128)(2,1)S(1)} %get-tuple-element.31), channel_id=1, source_target_pairs={{0,16},{1,17},{2,18},{3,19},{4,20},{5,21},{6,22},{7,23},{8,24},{9,... | collective-permute-start | bytes 393224 | tf_op jit(solution)/shard_map/ppermute | solution.py:324
  11.1 5.5 %collective-permute-start.5 = (f32[16,128]{1,0:T(8,128)S(1)}, f32[16,128]{1,0:T(8,128)S(1)}, u32[]{:S(2)}, u32[]{:S(2)}) collective-permute-start(f32[16,128]{1,0:T(8,128)S(1)} %get-tuple-element.36.own_part), channel_id=1, source_target_pairs={{0,3},{1,2},{2,1},{3,0},{4,7},{5,6},{6,5},{7,4},{8,11},{9,10},{10,... | collective-permute-start | bytes 24584 | tf_op jit(solution)/shard_map/ppermute | solution.py:328
  11.1 5.5 %collective-permute-start.4 = (f32[16,128]{1,0:T(8,128)S(1)}, f32[16,128]{1,0:T(8,128)S(1)}, u32[]{:S(2)}, u32[]{:S(2)}) collective-permute-start(f32[16,128]{1,0:T(8,128)S(1)} %get-tuple-element.36.own_part), channel_id=1, source_target_pairs={{0,2},{1,3},{2,0},{3,1},{4,6},{5,7},{6,4},{7,5},{8,10},{9,11},{10,... | collective-permute-start | bytes 24584 | tf_op jit(solution)/shard_map/ppermute | solution.py:328
  13.0 3.7 %collective-permute-start.3 = (f32[16,128]{1,0:T(8,128)S(1)}, f32[16,128]{1,0:T(8,128)S(1)}, u32[]{:S(2)}, u32[]{:S(2)}) collective-permute-start(f32[16,128]{1,0:T(8,128)S(1)} %get-tuple-element.36.own_part), channel_id=1, source_target_pairs={{0,1},{1,0},{2,3},{3,2},{4,5},{5,4},{6,7},{7,6},{8,9},{9,8},{10,11... | collective-permute-start | bytes 24584 | tf_op jit(solution)/shard_map/ppermute | solution.py:328
  14.6 10.4 %collective-permute-start.9 = (bf16[1040,128]{1,0:T(8,128)(2,1)S(1)}, bf16[1040,128]{1,0:T(8,128)(2,1)S(1)}, u32[]{:S(2)}, u32[]{:S(2)}) collective-permute-start(bf16[1040,128]{1,0:T(8,128)(2,1)S(1)} %get-tuple-element.38), channel_id=1, source_target_pairs={{16,1},{17,2},{18,3},{19,4},{20,5},{21,6},{22,7},{23,8},{24,9},{25... | collective-permute-start | bytes 798728 | tf_op jit(solution)/shard_map/ppermute | solution.py:324
  15.3 10.6 %collective-permute-start.10 = (bf16[1040,128]{1,0:T(8,128)(2,1)S(1)}, bf16[1040,128]{1,0:T(8,128)(2,1)S(1)}, u32[]{:S(2)}, u32[]{:S(2)}) collective-permute-start(bf16[1040,128]{1,0:T(8,128)(2,1)S(1)} %get-tuple-element.39), channel_id=1, source_target_pairs={{17,0},{18,1},{19,2},{20,3},{21,4},{22,5},{23,6},{24,7},{25,8},{26... | collective-permute-start | bytes 798728 | tf_op jit(solution)/shard_map/ppermute | solution.py:324
  16.7 5.6 %collective-permute-start.8 = (f32[16,128]{1,0:T(8,128)S(1)}, f32[16,128]{1,0:T(8,128)S(1)}, u32[]{:S(2)}, u32[]{:S(2)}) collective-permute-start(f32[16,128]{1,0:T(8,128)S(1)} %pad_maximum_fusion.refs_0_), channel_id=1, source_target_pairs={{0,12},{1,13},{2,14},{3,15},{4,8},{5,9},{6,10},{7,11},{8,4},{9,5},... | collective-permute-start | bytes 24584 | tf_op jit(solution)/shard_map/ppermute | solution.py:328
  20.3 4.7 %collective-permute-start.7 = (f32[16,128]{1,0:T(8,128)S(1)}, f32[16,128]{1,0:T(8,128)S(1)}, u32[]{:S(2)}, u32[]{:S(2)}) collective-permute-start(f32[16,128]{1,0:T(8,128)S(1)} %pad_maximum_fusion.refs_0_), channel_id=1, source_target_pairs={{0,8},{1,9},{2,10},{3,11},{4,12},{5,13},{6,14},{7,15},{8,0},{9,1},... | collective-permute-start | bytes 24584 | tf_op jit(solution)/shard_map/ppermute | solution.py:328
  20.3 4.7 %collective-permute-start.6 = (f32[16,128]{1,0:T(8,128)S(1)}, f32[16,128]{1,0:T(8,128)S(1)}, u32[]{:S(2)}, u32[]{:S(2)}) collective-permute-start(f32[16,128]{1,0:T(8,128)S(1)} %pad_maximum_fusion.refs_0_), channel_id=1, source_target_pairs={{0,4},{1,5},{2,6},{3,7},{4,0},{5,1},{6,2},{7,3},{8,12},{9,13},{10,... | collective-permute-start | bytes 24584 | tf_op jit(solution)/shard_map/ppermute | solution.py:328
  25.9 1.9 %collective-permute-start.11 = (bf16[1056,128]{1,0:T(8,128)(2,1)S(1)}, bf16[1056,128]{1,0:T(8,128)(2,1)S(1)}, u32[]{:S(2)}, u32[]{:S(2)}) collective-permute-start(bf16[1056,128]{1,0:T(8,128)(2,1)S(1)} %get-tuple-element.43), channel_id=1, source_target_pairs={{0,16},{1,17},{2,18},{3,19},{4,20},{5,21},{6,22},{7,23},{8,24},{9,... | collective-permute-start | bytes 811016 | tf_op jit(solution)/shard_map/ppermute | solution.py:324
